TPU v7x, 32 devices: a whole 2x2x4 slice. The times are simulated.
32 devices in a mesh: proj: 8 (over y, x, core), row: 4 (over z).
Axes of the slice: x: 2, y: 2, z: 4, core: 2. Of those that a mesh axis runs over, the one named last changes fastest.
Arguments:
- projections: float32 [4096, 4, 1536], P('proj', 'row'), may hold values from -40000 to 40000
Outputs:
- gram: float32 [4096, 4096], P('proj', 'row')
All inputs are finite; a program needn't handle non-finite values.
Results may differ from a plain program's by a relative error of at most 0.0017.
Values may be sent and summed in bfloat16 or wider, within the bound.
No kernel may reach another device: no remote copies, remote signals or barrier semaphores. Data moves between devices by JAX's collectives and lax.ppermute only.
A program may use at most 128 MiB of HBM per device.

v0:
```python
import math

import jax
import jax.numpy as jnp
from jax import lax
from jax.sharding import PartitionSpec as P


def per_device(projections):
    tile_rows, det_rows, columns = projections.shape
    entries = det_rows * lax.axis_size("row") * columns
    filtered = projections - jnp.mean(projections, axis=2, keepdims=True)
    energy = lax.psum(jnp.sum(filtered * filtered, axis=(1, 2)), "row")
    band_power = energy / entries
    normed = (
        filtered * lax.rsqrt(band_power + 1e-05)[:, None, None] * (1.0 / math.sqrt(entries))
    ).astype(jnp.bfloat16)
    flattened = normed.reshape(tile_rows, det_rows * columns)
    contract = (((1,), (1,)), ((), ()))
    product = lax.dot_general(
        flattened,
        lax.all_gather(flattened, "proj", axis=0, tiled=True),
        contract,
        preferred_element_type=jnp.float32,
    )
    return lax.psum_scatter(product, "row", scatter_dimension=1, tiled=True)


def solution(mesh):
    in_specs = (P("proj", "row", None),)
    out_specs = P("proj", "row")
    return jax.shard_map(
        per_device, mesh=mesh, in_specs=in_specs, out_specs=out_specs, check_vma=False
    )
```

profile of v0, /device:TPU:13, one launch (start us, length us, event | category | flops | bytes accessed | tf_op | source)
XLA Modules:
  0.0 258.6 jit_solution(6861131534138078150)
XLA Ops:
  6.5 0.0 copy-start
  6.5 0.0 all-gather.3.cloned.1.call-start
  6.5 4.2 %reduce_sum.18 = f32[512]{0:T(512)S(1)} reduce(f32[512,1,1536]{2,1,0:T(1,128)} %param.1, f32[]{:T(128)} %constant.2.clone.1), dimensions={1,2}, to_apply=%region_0.0 | reduce | flops 785920 | bytes 3147780 | tf_op jit(solution)/shard_map/reduce_sum | solution.py:12
  10.8 0.0 copy-done
  10.8 0.4 multiply_reduce_fusion
  11.3 7.3 %psum.7 = f32[512]{0:T(512)S(1)} all-reduce(f32[512]{0:T(512)S(1)} %multiply_reduce_fusion), channel_id=1, replica_groups=mesh['proj'=8,'row'=4] {'row'}, use_global_device_ids=true, to_apply=%region_2.0 | all-reduce | flops 512 | bytes 4096 | tf_op jit(solution)/shard_map/psum | solution.py:13
  18.5 1.6 multiply_convert_fusion
  20.1 0.0 all-gather.3.cloned.1.call-update
  20.2 0.0 reduce-scatter.2.cloned.1.call-start
  20.2 74.9 %all-gather.3.cloned.1.call-done = bf16[4096,1,1536]{2,0,1:T(8,128)(2,1)} async-done(((bf16[512,1,1536]{2,0,1:T(8,128)(2,1)}), bf16[4096,1,1536]{2,0,1:T(8,128)(2,1)}) %all-gather.3.cloned.1.call-update) | async-done | bytes 12582928 | tf_op jit(solution)/shard_map/all_gather | solution.py:22
  95.1 12.1 %fusion = f32[512,4096]{1,0:T(8,128)} fusion(bf16[4096,1,1536]{2,0,1:T(8,128)(2,1)} %all-gather.3.cloned.1.call-done, bf16[512,1,1536]{2,0,1:T(8,128)(2,1)} %multiply_convert_fusion), kind=kOutput, calls=%fused_computation | convolution fusion | flops 6442450944 | bytes 22544384 | tf_op jit(solution)/shard_map/dot_general | solution.py:20
  107.3 0.0 reduce-scatter.2.cloned.1.call-update
  107.3 144.5 %reduce-scatter.2.cloned.1.call-done = f32[512,1024]{1,0:T(8,128)} async-done(((f32[512,4096]{1,0:T(8,128)}), f32[512,1024]{1,0:T(8,128)}) %reduce-scatter.2.cloned.1.call-update) | async-done | bytes 2097168 | tf_op jit(solution)/shard_map/reduce_scatter | solution.py:26
  (2 shorter events, 0.0 us)
Async XLA Ops:
  6.5 4.3 %copy-start = (f32[512,1,1536]{2,1,0:T(1,128)S(1)}, f32[512,1,1536]{2,1,0:T(1,128)}, u32[]{:S(2)}) copy-start(f32[512,1,1536]{2,1,0:T(1,128)} %param.1) | copy-start | bytes 9437188
  6.5 88.6 %all-gather.3.cloned.1.call-start = ((), (), s32[]{:S(2)}) async-start(), calls=%async_computation.2 | async-start | bytes 14155776 | tf_op jit(solution)/shard_map/all_gather | solution.py:22
  20.2 231.6 %reduce-scatter.2.cloned.1.call-start = ((), (), s32[]{:S(2)}) async-start(), calls=%async_computation.1 | async-start | bytes 10485760 | tf_op jit(solution)/shard_map/reduce_scatter | solution.py:26
Sparse Core Ops, SparseCore 0:
  20.3 74.8 all-gather.2
  107.4 144.3 reduce-scatter.1
where the time goes:
time: 261 us; the launch traced here: 259 us
  waiting for transfers between devices  219 us (84%)
  between operations  13.4 us (5%)
  matrix products  12.1 us (5%)
  blocking collectives  7.26 us (3%)
  other arithmetic  6.33 us (2%)
    reduce_scatter x1, waiting for transfers between devices, per_device(): return lax.psum_scatter(product, 'row', scatter_dimension=1, tiled=True)  144 us
    all_gather x1, waiting for transfers between devices, per_device(): lax.all_gather(flattened, 'proj', axis=0, tiled=True)  74.9 us
    dot_general x1, matrix products, per_device(): lax.dot_general(flattened, lax.all_gather(flattened, 'proj', axis=0, tile...  12.1 us
    psum x1, blocking collectives, per_device(): energy = lax.psum(jnp.sum(filtered * filtered, axis=(1, 2)), 'row')  7.26 us
  transfers between devices with their start and end apart: 2, of which 2 were waited for; matrix products, arithmetic and copies ran while one was open for 0% of the time, Pallas kernels for 0%

commit v1 on v0

v1 whole, which is shorter than its diff:
```python
import math

import jax
import jax.numpy as jnp
from jax import lax
from jax.sharding import PartitionSpec as P

CHUNKS = 2
AXES = ("proj", "row")


def hop(x, axis, size, mask):
    return lax.ppermute(x, axis, [(i, i ^ mask) for i in range(size)])


def scale_up(share):
    t = jnp.ones_like(share)
    for e in (32, 16, 8, 4, 2, 1):
        small = share < 2.0 ** (-2 * e)
        t = jnp.where(small, t * 2.0**e, t)
        share = jnp.where(small, share * 2.0 ** (2 * e), share)
    return t


def per_device(projections):
    tile, det_rows, columns = projections.shape
    np_, nr = lax.axis_size("proj"), lax.axis_size("row")
    group = np_ // nr
    entries = det_rows * nr * columns
    p, z = lax.axis_index("proj"), lax.axis_index("row")

    filtered = projections - jnp.mean(projections, axis=2, keepdims=True)
    energy = jnp.sum(filtered * filtered, axis=(1, 2))
    parts = [energy] + [hop(energy, "row", nr, d) for d in range(1, nr)]
    while len(parts) > 1:
        parts = [a + b for a, b in zip(parts[::2], parts[1::2])]
    band_power = parts[0] / entries
    t = scale_up(band_power / (band_power + 1e-05))
    factor = lax.rsqrt(band_power + 1e-05)
    normed = (filtered * factor[:, None, None] * (1.0 / math.sqrt(entries)) * t[:, None, None]).astype(jnp.bfloat16)
    own = normed.reshape(tile, det_rows * columns)
    every_t = lax.all_gather(t, "proj", axis=0, tiled=True)
    piece = tile // CHUNKS
    held = {(0, q): own[q * piece : (q + 1) * piece] for q in range(CHUNKS)}

    def gather(k):
        if k == 0:
            return
        bits = [b for b in (1 << i for i in range(nr.bit_length())) if k & b]
        for q in range(CHUNKS):
            b = bits[q % len(bits)]
            held[k, q] = hop(held[k ^ b, q], "proj", np_, b * group)

    def chain(k, block):
        part = lax.dot_general(own, block, (((1,), (1,)), ((), ())), preferred_element_type=jnp.float32)
        total = part
        carry = part
        for stage in range(1, nr):
            pairs = []
            for src in range(np_):
                d = (src // group) ^ k
                if stage - 1 < d:
                    pairs.append((src * nr + stage - 1, src * nr + stage))
                if nr - stage > d:
                    pairs.append((src * nr + nr - stage, src * nr + nr - stage - 1))
            got = lax.ppermute(carry.astype(jnp.float16), AXES, pairs).astype(jnp.float32)
            carry = part + got
            total = total + got
        return total

    for k in sorted(range(nr), key=lambda k: bin(k).count("1")):
        gather(k)
    result = [[None] * CHUNKS for _ in range(group)]
    for k in range(nr):
        mine = (p // group) ^ k == z
        for q in range(CHUNKS):
            for j in range(group):
                block = held[k, q] if j == 0 else hop(held[k, q], "proj", np_, j)
                total = chain(k, block)
                before = result[j][q]
                result[j][q] = total if before is None else jnp.where(mine, total, before)
    blocks = [jnp.concatenate(r, axis=1) for r in result]
    member = p % group
    ordered = []
    for j in range(group):
        b = blocks[j]
        for i in range(1, group):
            b = jnp.where(member == i, blocks[j ^ i], b)
        ordered.append(b)
    out = jnp.concatenate(ordered, axis=1)
    back = 1.0 / t
    width = tile * group
    across = 1.0 / lax.dynamic_slice_in_dim(every_t, z * width, width)
    return out * back[:, None] * across[None, :]


def solution(mesh):
    return jax.shard_map(
        per_device, mesh=mesh, in_specs=(P("proj", "row", None),), out_specs=P("proj", "row"), check_vma=False
    )
```

time: 261 us -> 255 us (0.977)
  the two profiles are of different devices: /device:TPU:13 before, /device:TPU:6 now
where the time goes in v1:
time: 255 us; the launch traced here: 254 us
  starting transfers between devices  111 us (44%)
  waiting for transfers between devices  80.9 us (32%)
  other arithmetic  22.2 us (9%)
  blocking collectives  21.5 us (8%)
  matrix products  11.1 us (4%)
  local copies, waits for them, and re-layouts  5.66 us (2%)
    ppermute x48, starting transfers between devices, chain(): lax.ppermute(carry.astype(jnp.float16), AXES, pairs).astype(jnp.float32)  103 us
    ppermute x48, waiting for transfers between devices, chain(): lax.ppermute(carry.astype(jnp.float16), AXES, pairs).astype(jnp.float32)  73.7 us
    all_gather x1, blocking collectives, per_device(): every_t = lax.all_gather(t, 'proj', axis=0, tiled=True)  21.5 us
    dot_general x16, matrix products, chain(): lax.dot_general(own, block, (((1,), (1,)), ((), ())), preferred_element_t...  11.1 us
    ppermute x17, starting transfers between devices, hop(): return lax.ppermute(x, axis, [(i, i ^ mask) for i in range(size)])  8.83 us
    ppermute x17, waiting for transfers between devices, hop(): return lax.ppermute(x, axis, [(i, i ^ mask) for i in range(size)])  7.13 us
  transfers between devices with their start and end apart: 65, of which 15 were waited for; matrix products, arithmetic and copies ran while one was open for 7% of the time, Pallas kernels for 0%

profile of v1, /device:TPU:6, one launch (start us, length us, event | category | flops | bytes accessed | tf_op | source)
XLA Modules:
  0.0 253.9 jit_solution(15553048502706803834)
XLA Ops:
  0.0 4.2 %reduce_sum.18 = f32[512]{0:T(512)S(1)} reduce(f32[512,1,1536]{2,1,0:T(1,128)} %param.1, f32[]{:T(128)} %constant.28.clone.1), dimensions={1,2}, to_apply=%region_0.0 | reduce | flops 785920 | bytes 3147780 | tf_op jit(solution)/shard_map/reduce_sum | solution.py:32
  4.3 3.9 %multiply_reduce_fusion = f32[512]{0:T(512)S(1)} fusion(f32[512,1,1536]{2,1,0:T(1,128)S(1)} %copy-done, f32[512]{0:T(512)S(1)} %broadcast_multiply_fusion.1), kind=kLoop, calls=%fused_computation.1 | loop fusion | flops 2358784 | bytes 3149824 | tf_op jit(solution)/shard_map/reduce_sum | solution.py:33
  8.2 1.6 collective-permute-start
  9.9 2.6 %collective-permute-start.1 = (f32[512]{0:T(512)S(1)}, f32[512]{0:T(512)S(1)}, u32[]{:S(2)}, u32[]{:S(2)}) collective-permute-start(f32[512]{0:T(512)S(1)} %multiply_reduce_fusion), channel_id=1, source_target_pairs={{0,2},{1,3},{2,0},{3,1},{4,6},{5,7},{6,4},{7,5},{8,10},{9,11},{10,... | collective-permute-start | bytes 6152 | tf_op jit(solution)/shard_map/ppermute | solution.py:13
  12.7 1.7 collective-permute-done.1
  14.3 3.5 %collective-permute-done.2 = f32[512]{0:T(512)S(1)} collective-permute-done((f32[512]{0:T(512)S(1)}, f32[512]{0:T(512)S(1)}, u32[]{:S(2)}, u32[]{:S(2)}) %collective-permute-start.2) | collective-permute-done | bytes 2080 | tf_op jit(solution)/shard_map/ppermute | solution.py:13
  17.9 4.7 %multiply_convert_fusion = bf16[512,1,1536]{2,1,0:T(2,128)(2,1)S(1)} fusion(f32[512,1,1536]{2,1,0:T(1,128)S(1)} %copy-done, f32[512]{0:T(512)S(1)} %get-tuple-element.45, f32[512]{0:T(512)S(1)} %get-tuple-element.44, f32[512]{0:T(512)S(1)} %broadcast_multiply_fusion.1), kind=kLoop, calls=%fused_computation | loop fusion | flops 3145728 | bytes 4724736 | tf_op jit(solution)/shard_map/convert_element_type | solution.py:40
  22.9 3.3 %fusion.96 = (bf16[256,1,1536]{2,1,0:T(2,128)(2,1)S(1)}, bf16[256,1,1536]{2,1,0:T(2,128)(2,1)S(1)}) fusion(bf16[512,1,1536]{2,1,0:T(2,128)(2,1)S(1)} %multiply_convert_fusion), kind=kLoop, calls=%fused_computation.169 | loop fusion | bytes 3145728 | tf_op jit(solution)/shard_map/slice | solution.py:44
  26.4 1.3 fusion.104
  27.7 2.0 collective-permute-start.50
  29.7 1.3 fusion.100
  31.1 2.0 collective-permute-start.62
  33.6 21.5 %all-gather = f32[8,1,512]{2,1,0:T(1,128)S(1)} all-gather(f32[1,1,512]{2,1,0:T(1,128)S(1)} %bitcast.98), channel_id=1, replica_groups=mesh['proj'=8,'row'=4] {'proj'}, dimensions={0}, use_global_device_ids=true | all-gather | bytes 18432 | tf_op jit(solution)/shard_map/all_gather | solution.py:42
  55.1 1.0 fusion.90
  56.2 0.7 collective-permute-start.51
  56.8 1.0 fusion.94
  57.9 0.7 collective-permute-start.63
  59.8 1.6 collective-permute-start.28
  62.0 0.9 collective-permute-start.52
  63.5 12.6 %collective-permute-start.19 = (f16[512,256]{0,1:T(8,128)(2,1)S(1)}, f16[512,256]{0,1:T(8,128)(2,1)S(1)}, u32[]{:S(2)}, u32[]{:S(2)}) collective-permute-start(f16[512,256]{0,1:T(8,128)(2,1)S(1)} %get-tuple-element.42), channel_id=1, source_target_pairs={{3,2},{7,6},{8,9},{11,10},{12,13},{15,14},{16,17},{19,18},{20,21},... | collective-permute-start | bytes 786440 | tf_op jit(solution)/shard_map/ppermute | solution.py:66
  76.7 1.3 collective-permute-start.38
  79.2 11.7 %collective-permute-start.44 = (f16[512,256]{0,1:T(8,128)(2,1)S(1)}, f16[512,256]{0,1:T(8,128)(2,1)S(1)}, u32[]{:S(2)}, u32[]{:S(2)}) collective-permute-start(f16[512,256]{0,1:T(8,128)(2,1)S(1)} %get-tuple-element.22), channel_id=1, source_target_pairs={{0,1},{3,2},{4,5},{7,6},{8,9},{12,13},{19,18},{23,22},{24,25},{27,... | collective-permute-start | bytes 786440 | tf_op jit(solution)/shard_map/ppermute | solution.py:66
  91.5 1.3 collective-permute-start.47
  93.5 1.3 collective-permute-start.56
  94.9 1.3 collective-permute-start.59
  96.3 1.4 collective-permute-done.44
  97.7 5.5 %collective-permute-done.47 = f16[512,256]{0,1:T(8,128)(2,1)S(1)} collective-permute-done((f16[512,256]{0,1:T(8,128)(2,1)S(1)}, f16[512,256]{0,1:T(8,128)(2,1)S(1)}, u32[]{:S(2)}, u32[]{:S(2)}) %collective-permute-start.47) | collective-permute-done | bytes 262176 | tf_op jit(solution)/shard_map/ppermute | solution.py:66
  103.3 5.5 %collective-permute-done.56 = f16[512,256]{0,1:T(8,128)(2,1)S(1)} collective-permute-done((f16[512,256]{0,1:T(8,128)(2,1)S(1)}, f16[512,256]{0,1:T(8,128)(2,1)S(1)}, u32[]{:S(2)}, u32[]{:S(2)}) %collective-permute-start.56) | collective-permute-done | bytes 262176 | tf_op jit(solution)/shard_map/ppermute | solution.py:66
  109.6 2.4 collective-permute-done.59
  112.8 0.7 collective-permute-start.45
  117.5 0.8 collective-permute-done.14
  120.7 24.6 %collective-permute-start.10 = (f16[512,256]{0,1:T(8,128)(2,1)S(1)}, f16[512,256]{0,1:T(8,128)(2,1)S(1)}, u32[]{:S(2)}, u32[]{:S(2)}) collective-permute-start(f16[512,256]{0,1:T(8,128)(2,1)S(1)} %get-tuple-element.38), channel_id=1, source_target_pairs={{0,1},{3,2},{4,5},{7,6},{8,9},{12,13},{19,18},{23,22},{24,25},{27,... | collective-permute-start | bytes 786440 | tf_op jit(solution)/shard_map/ppermute | solution.py:66
  145.9 1.3 collective-permute-start.15
  147.9 14.7 %collective-permute-start.30 = (f16[512,256]{0,1:T(8,128)(2,1)S(1)}, f16[512,256]{0,1:T(8,128)(2,1)S(1)}, u32[]{:S(2)}, u32[]{:S(2)}) collective-permute-start(f16[512,256]{0,1:T(8,128)(2,1)S(1)} %get-tuple-element.30), channel_id=1, source_target_pairs={{0,1},{3,2},{4,5},{7,6},{8,9},{12,13},{19,18},{23,22},{24,25},{27,... | collective-permute-start | bytes 786440 | tf_op jit(solution)/shard_map/ppermute | solution.py:66
  163.2 1.3 collective-permute-start.34
  165.3 3.9 %collective-permute-done.30 = f16[512,256]{0,1:T(8,128)(2,1)S(1)} collective-permute-done((f16[512,256]{0,1:T(8,128)(2,1)S(1)}, f16[512,256]{0,1:T(8,128)(2,1)S(1)}, u32[]{:S(2)}, u32[]{:S(2)}) %collective-permute-start.30) | collective-permute-done | bytes 262176 | tf_op jit(solution)/shard_map/ppermute | solution.py:66
  170.0 3.0 %collective-permute-done.34 = f16[512,256]{0,1:T(8,128)(2,1)S(1)} collective-permute-done((f16[512,256]{0,1:T(8,128)(2,1)S(1)}, f16[512,256]{0,1:T(8,128)(2,1)S(1)}, u32[]{:S(2)}, u32[]{:S(2)}) %collective-permute-start.34) | collective-permute-done | bytes 262176 | tf_op jit(solution)/shard_map/ppermute | solution.py:66
  179.3 1.3 collective-permute-start.43
  185.4 33.8 %collective-permute-done.43 = f16[512,256]{0,1:T(8,128)(2,1)S(1)} collective-permute-done((f16[512,256]{0,1:T(8,128)(2,1)S(1)}, f16[512,256]{0,1:T(8,128)(2,1)S(1)}, u32[]{:S(2)}, u32[]{:S(2)}) %collective-permute-start.43) | collective-permute-done | bytes 262176 | tf_op jit(solution)/shard_map/ppermute | solution.py:66
  219.8 1.6 fusion.58
  221.4 1.3 collective-permute-start.55
  225.7 4.0 %collective-permute-done.55 = f16[512,256]{0,1:T(8,128)(2,1)S(1)} collective-permute-done((f16[512,256]{0,1:T(8,128)(2,1)S(1)}, f16[512,256]{0,1:T(8,128)(2,1)S(1)}, u32[]{:S(2)}, u32[]{:S(2)}) %collective-permute-start.55) | collective-permute-done | bytes 262176 | tf_op jit(solution)/shard_map/ppermute | solution.py:66
  229.7 1.5 collective-permute-start.8
  231.2 1.6 fusion.69
  235.0 1.3 collective-permute-start.27
  236.3 5.3 %collective-permute-done.8 = f16[512,256]{0,1:T(8,128)(2,1)S(1)} collective-permute-done((f16[512,256]{0,1:T(8,128)(2,1)S(1)}, f16[512,256]{0,1:T(8,128)(2,1)S(1)}, u32[]{:S(2)}, u32[]{:S(2)}) %collective-permute-start.8) | collective-permute-done | bytes 262176 | tf_op jit(solution)/shard_map/ppermute | solution.py:66
  242.2 8.8 %collective-permute-done.27 = f16[512,256]{0,1:T(8,128)(2,1)S(1)} collective-permute-done((f16[512,256]{0,1:T(8,128)(2,1)S(1)}, f16[512,256]{0,1:T(8,128)(2,1)S(1)}, u32[]{:S(2)}, u32[]{:S(2)}) %collective-permute-start.27) | collective-permute-done | bytes 262176 | tf_op jit(solution)/shard_map/ppermute | solution.py:66
  252.1 1.8 copy.3
  (153 shorter events, 36.3 us)
Async XLA Ops:
  8.2 4.5 %collective-permute-start = (f32[512]{0:T(512)S(1)}, f32[512]{0:T(512)S(1)}, u32[]{:S(2)}, u32[]{:S(2)}) collective-permute-start(f32[512]{0:T(512)S(1)} %multiply_reduce_fusion), channel_id=1, source_target_pairs={{0,1},{1,0},{2,3},{3,2},{4,5},{5,4},{6,7},{7,6},{8,9},{9,8},{10,11... | collective-permute-start | bytes 6152 | tf_op jit(solution)/shard_map/ppermute | solution.py:13
  9.9 4.5 %collective-permute-start.1 = (f32[512]{0:T(512)S(1)}, f32[512]{0:T(512)S(1)}, u32[]{:S(2)}, u32[]{:S(2)}) collective-permute-start(f32[512]{0:T(512)S(1)} %multiply_reduce_fusion), channel_id=1, source_target_pairs={{0,2},{1,3},{2,0},{3,1},{4,6},{5,7},{6,4},{7,5},{8,10},{9,11},{10,... | collective-permute-start | bytes 6152 | tf_op jit(solution)/shard_map/ppermute | solution.py:13
  12.4 5.4 %collective-permute-start.2 = (f32[512]{0:T(512)S(1)}, f32[512]{0:T(512)S(1)}, u32[]{:S(2)}, u32[]{:S(2)}) collective-permute-start(f32[512]{0:T(512)S(1)} %multiply_reduce_fusion), channel_id=1, source_target_pairs={{0,3},{1,2},{2,1},{3,0},{4,7},{5,6},{6,5},{7,4},{8,11},{9,10},{10,... | collective-permute-start | bytes 6152 | tf_op jit(solution)/shard_map/ppermute | solution.py:13
  27.7 27.4 %collective-permute-start.50 = (f16[512,256]{0,1:T(8,128)(2,1)}, f16[512,256]{0,1:T(8,128)(2,1)}, u32[]{:S(2)}, u32[]{:S(2)}) collective-permute-start(f16[512,256]{0,1:T(8,128)(2,1)} %get-tuple-element.26), channel_id=1, source_target_pairs={{3,2},{7,6},{8,9},{11,10},{12,13},{15,14},{16,17},{19,18},{20,21},... | collective-permute-start | bytes 786440 | tf_op jit(solution)/shard_map/ppermute | solution.py:66
  31.1 25.8 %collective-permute-start.62 = (f16[512,256]{0,1:T(8,128)(2,1)}, f16[512,256]{0,1:T(8,128)(2,1)}, u32[]{:S(2)}, u32[]{:S(2)}) collective-permute-start(f16[512,256]{0,1:T(8,128)(2,1)} %get-tuple-element.18), channel_id=1, source_target_pairs={{3,2},{7,6},{8,9},{11,10},{12,13},{15,14},{16,17},{19,18},{20,21},... | collective-permute-start | bytes 786440 | tf_op jit(solution)/shard_map/ppermute | solution.py:66
  33.1 30.4 %collective-permute-start.3 = (bf16[256,1536]{1,0:T(8,128)(2,1)}, bf16[256,1536]{1,0:T(8,128)(2,1)S(1)}, u32[]{:S(2)}, u32[]{:S(2)}) collective-permute-start(bf16[256,1536]{1,0:T(8,128)(2,1)} %bitcast.94), channel_id=1, source_target_pairs={{0,16},{4,20},{8,24},{12,28},{16,0},{20,4},{24,8},{28,12},{1,17},{... | collective-permute-start | bytes 2359304 | tf_op jit(solution)/shard_map/ppermute | solution.py:13
  33.6 43.1 %collective-permute-start.13 = (bf16[256,1536]{1,0:T(8,128)(2,1)}, bf16[256,1536]{1,0:T(8,128)(2,1)S(1)}, u32[]{:S(2)}, u32[]{:S(2)}) collective-permute-start(bf16[256,1536]{1,0:T(8,128)(2,1)} %bitcast.95), channel_id=1, source_target_pairs={{0,8},{4,12},{8,0},{12,4},{16,24},{20,28},{24,16},{28,20},{1,9},{5... | collective-permute-start | bytes 2359304 | tf_op jit(solution)/shard_map/ppermute | solution.py:13
  33.6 26.2 %collective-permute-start.18 = (bf16[256,1536]{1,0:T(8,128)(2,1)}, bf16[256,1536]{1,0:T(8,128)(2,1)S(1)}, u32[]{:S(2)}, u32[]{:S(2)}) collective-permute-start(bf16[256,1536]{1,0:T(8,128)(2,1)} %bitcast.96), channel_id=1, source_target_pairs={{0,4},{4,0},{8,12},{12,8},{16,20},{20,16},{24,28},{28,24},{1,5},{5... | collective-permute-start | bytes 2359304 | tf_op jit(solution)/shard_map/ppermute | solution.py:13
  58.6 3.4 %collective-permute-start.37 = (bf16[256,1536]{1,0:T(8,128)(2,1)S(1)}, bf16[256,1536]{1,0:T(8,128)(2,1)S(1)}, u32[]{:S(2)}, u32[]{:S(2)}) collective-permute-start(bf16[256,1536]{1,0:T(8,128)(2,1)S(1)} %bitcast.90), channel_id=1, source_target_pairs={{0,4},{4,0},{8,12},{12,8},{16,20},{20,16},{24,28},{28,24},{1,5},{5... | collective-permute-start | bytes 2359304 | tf_op jit(solution)/shard_map/ppermute | solution.py:13
  59.1 32.4 %collective-permute-start.22 = (bf16[256,1536]{1,0:T(8,128)(2,1)S(1)}, bf16[256,1536]{1,0:T(8,128)(2,1)S(1)}, u32[]{:S(2)}, u32[]{:S(2)}) collective-permute-start(bf16[256,1536]{1,0:T(8,128)(2,1)S(1)} %bitcast.91), channel_id=1, source_target_pairs={{0,8},{4,12},{8,0},{12,4},{16,24},{20,28},{24,16},{28,20},{1,9},{5... | collective-permute-start | bytes 2359304 | tf_op jit(solution)/shard_map/ppermute | solution.py:13
  59.8 19.4 %collective-permute-start.28 = (bf16[256,1536]{1,0:T(8,128)(2,1)S(1)}, bf16[256,1536]{1,0:T(8,128)(2,1)S(1)}, u32[]{:S(2)}, u32[]{:S(2)}) collective-permute-start(bf16[256,1536]{1,0:T(8,128)(2,1)S(1)} %bitcast.92), channel_id=1, source_target_pairs={{0,16},{4,20},{8,24},{12,28},{16,0},{20,4},{24,8},{28,12},{1,17},{... | collective-permute-start | bytes 2359304 | tf_op jit(solution)/shard_map/ppermute | solution.py:13
  62.0 121.3 %collective-permute-start.52 = (f16[512,256]{0,1:T(8,128)(2,1)S(1)}, f16[512,256]{0,1:T(8,128)(2,1)S(1)}, u32[]{:S(2)}, u32[]{:S(2)}) collective-permute-start(f16[512,256]{0,1:T(8,128)(2,1)S(1)} %fusion.67), channel_id=1, source_target_pairs={{1,0},{5,4},{26,27},{30,31}} | collective-permute-start | bytes 786440 | tf_op jit(solution)/shard_map/ppermute | solution.py:66
  63.5 30.0 %collective-permute-start.19 = (f16[512,256]{0,1:T(8,128)(2,1)S(1)}, f16[512,256]{0,1:T(8,128)(2,1)S(1)}, u32[]{:S(2)}, u32[]{:S(2)}) collective-permute-start(f16[512,256]{0,1:T(8,128)(2,1)S(1)} %get-tuple-element.42), channel_id=1, source_target_pairs={{3,2},{7,6},{8,9},{11,10},{12,13},{15,14},{16,17},{19,18},{20,21},... | collective-permute-start | bytes 786440 | tf_op jit(solution)/shard_map/ppermute | solution.py:66
  76.7 18.2 %collective-permute-start.38 = (f16[512,256]{0,1:T(8,128)(2,1)S(1)}, f16[512,256]{0,1:T(8,128)(2,1)S(1)}, u32[]{:S(2)}, u32[]{:S(2)}) collective-permute-start(f16[512,256]{0,1:T(8,128)(2,1)S(1)} %get-tuple-element.34), channel_id=1, source_target_pairs={{3,2},{7,6},{8,9},{11,10},{12,13},{15,14},{16,17},{19,18},{20,21},... | collective-permute-start | bytes 786440 | tf_op jit(solution)/shard_map/ppermute | solution.py:66
  79.2 18.4 %collective-permute-start.44 = (f16[512,256]{0,1:T(8,128)(2,1)S(1)}, f16[512,256]{0,1:T(8,128)(2,1)S(1)}, u32[]{:S(2)}, u32[]{:S(2)}) collective-permute-start(f16[512,256]{0,1:T(8,128)(2,1)S(1)} %get-tuple-element.22), channel_id=1, source_target_pairs={{0,1},{3,2},{4,5},{7,6},{8,9},{12,13},{19,18},{23,22},{24,25},{27,... | collective-permute-start | bytes 786440 | tf_op jit(solution)/shard_map/ppermute | solution.py:66
  91.5 11.7 %collective-permute-start.47 = (f16[512,256]{0,1:T(8,128)(2,1)S(1)}, f16[512,256]{0,1:T(8,128)(2,1)S(1)}, u32[]{:S(2)}, u32[]{:S(2)}) collective-permute-start(f16[512,256]{0,1:T(8,128)(2,1)S(1)} %get-tuple-element.24), channel_id=1, source_target_pairs={{0,1},{3,2},{4,5},{7,6},{11,10},{15,14},{16,17},{20,21},{24,25},{2... | collective-permute-start | bytes 786440 | tf_op jit(solution)/shard_map/ppermute | solution.py:66
  93.5 15.4 %collective-permute-start.56 = (f16[512,256]{0,1:T(8,128)(2,1)S(1)}, f16[512,256]{0,1:T(8,128)(2,1)S(1)}, u32[]{:S(2)}, u32[]{:S(2)}) collective-permute-start(f16[512,256]{0,1:T(8,128)(2,1)S(1)} %get-tuple-element.14), channel_id=1, source_target_pairs={{0,1},{3,2},{4,5},{7,6},{8,9},{12,13},{19,18},{23,22},{24,25},{27,... | collective-permute-start | bytes 786440 | tf_op jit(solution)/shard_map/ppermute | solution.py:66
  94.9 17.2 %collective-permute-start.59 = (f16[512,256]{0,1:T(8,128)(2,1)S(1)}, f16[512,256]{0,1:T(8,128)(2,1)S(1)}, u32[]{:S(2)}, u32[]{:S(2)}) collective-permute-start(f16[512,256]{0,1:T(8,128)(2,1)S(1)} %get-tuple-element.16), channel_id=1, source_target_pairs={{0,1},{3,2},{4,5},{7,6},{11,10},{15,14},{16,17},{20,21},{24,25},{2... | collective-permute-start | bytes 786440 | tf_op jit(solution)/shard_map/ppermute | solution.py:66
  97.6 48.3 %collective-permute-start.4 = (bf16[256,1536]{1,0:T(8,128)(2,1)S(1)}, bf16[256,1536]{1,0:T(8,128)(2,1)S(1)}, u32[]{:S(2)}, u32[]{:S(2)}) collective-permute-start(bf16[256,1536]{1,0:T(8,128)(2,1)S(1)} %collective-permute-done.3), channel_id=1, source_target_pairs={{0,8},{4,12},{8,0},{12,4},{16,24},{20,28},{24,16},{28,20},{1,9},{5... | collective-permute-start | bytes 2359304 | tf_op jit(solution)/shard_map/ppermute | solution.py:13
  103.2 13.5 %collective-permute-start.9 = (bf16[256,1536]{1,0:T(8,128)(2,1)S(1)}, bf16[256,1536]{1,0:T(8,128)(2,1)S(1)}, u32[]{:S(2)}, u32[]{:S(2)}) collective-permute-start(bf16[256,1536]{1,0:T(8,128)(2,1)S(1)} %collective-permute-done.3), channel_id=1, source_target_pairs={{0,4},{4,0},{8,12},{12,8},{16,20},{20,16},{24,28},{28,24},{1,5},{5... | collective-permute-start | bytes 2359304 | tf_op jit(solution)/shard_map/ppermute | solution.py:13
  108.9 4.0 %collective-permute-start.20 = (f16[512,256]{0,1:T(8,128)(2,1)S(1)}, f16[512,256]{0,1:T(8,128)(2,1)S(1)}, u32[]{:S(2)}, u32[]{:S(2)}) collective-permute-start(f16[512,256]{0,1:T(8,128)(2,1)S(1)} %fusion.82), channel_id=1, source_target_pairs={{2,1},{6,5},{10,9},{14,13},{17,18},{21,22},{25,26},{29,30}} | collective-permute-start | bytes 786440 | tf_op jit(solution)/shard_map/ppermute | solution.py:66
  116.8 3.9 %collective-permute-start.33 = (bf16[256,1536]{1,0:T(8,128)(2,1)S(1)}, bf16[256,1536]{1,0:T(8,128)(2,1)S(1)}, u32[]{:S(2)}, u32[]{:S(2)}) collective-permute-start(bf16[256,1536]{1,0:T(8,128)(2,1)S(1)} %collective-permute-done.22), channel_id=1, source_target_pairs={{0,4},{4,0},{8,12},{12,8},{16,20},{20,16},{24,28},{28,24},{1,5},{5... | collective-permute-start | bytes 2359304 | tf_op jit(solution)/shard_map/ppermute | solution.py:13
  118.3 29.6 %collective-permute-start.23 = (bf16[256,1536]{1,0:T(8,128)(2,1)S(1)}, bf16[256,1536]{1,0:T(8,128)(2,1)S(1)}, u32[]{:S(2)}, u32[]{:S(2)}) collective-permute-start(bf16[256,1536]{1,0:T(8,128)(2,1)S(1)} %collective-permute-done.22), channel_id=1, source_target_pairs={{0,16},{4,20},{8,24},{12,28},{16,0},{20,4},{24,8},{28,12},{1,17},{... | collective-permute-start | bytes 2359304 | tf_op jit(solution)/shard_map/ppermute | solution.py:13
  119.4 64.5 %collective-permute-start.46 = (f16[512,256]{0,1:T(8,128)(2,1)S(1)}, f16[512,256]{0,1:T(8,128)(2,1)S(1)}, u32[]{:S(2)}, u32[]{:S(2)}) collective-permute-start(f16[512,256]{0,1:T(8,128)(2,1)S(1)} %fusion.62), channel_id=1, source_target_pairs={{10,11},{14,15},{17,16},{21,20}} | collective-permute-start | bytes 786440 | tf_op jit(solution)/shard_map/ppermute | solution.py:66
  120.7 42.4 %collective-permute-start.10 = (f16[512,256]{0,1:T(8,128)(2,1)S(1)}, f16[512,256]{0,1:T(8,128)(2,1)S(1)}, u32[]{:S(2)}, u32[]{:S(2)}) collective-permute-start(f16[512,256]{0,1:T(8,128)(2,1)S(1)} %get-tuple-element.38), channel_id=1, source_target_pairs={{0,1},{3,2},{4,5},{7,6},{8,9},{12,13},{19,18},{23,22},{24,25},{27,... | collective-permute-start | bytes 786440 | tf_op jit(solution)/shard_map/ppermute | solution.py:66
  145.9 18.6 %collective-permute-start.15 = (f16[512,256]{0,1:T(8,128)(2,1)S(1)}, f16[512,256]{0,1:T(8,128)(2,1)S(1)}, u32[]{:S(2)}, u32[]{:S(2)}) collective-permute-start(f16[512,256]{0,1:T(8,128)(2,1)S(1)} %get-tuple-element.40), channel_id=1, source_target_pairs={{0,1},{3,2},{4,5},{7,6},{11,10},{15,14},{16,17},{20,21},{24,25},{2... | collective-permute-start | bytes 786440 | tf_op jit(solution)/shard_map/ppermute | solution.py:66
  147.9 21.4 %collective-permute-start.30 = (f16[512,256]{0,1:T(8,128)(2,1)S(1)}, f16[512,256]{0,1:T(8,128)(2,1)S(1)}, u32[]{:S(2)}, u32[]{:S(2)}) collective-permute-start(f16[512,256]{0,1:T(8,128)(2,1)S(1)} %get-tuple-element.30), channel_id=1, source_target_pairs={{0,1},{3,2},{4,5},{7,6},{8,9},{12,13},{19,18},{23,22},{24,25},{27,... | collective-permute-start | bytes 786440 | tf_op jit(solution)/shard_map/ppermute | solution.py:66
  163.2 9.9 %collective-permute-start.34 = (f16[512,256]{0,1:T(8,128)(2,1)S(1)}, f16[512,256]{0,1:T(8,128)(2,1)S(1)}, u32[]{:S(2)}, u32[]{:S(2)}) collective-permute-start(f16[512,256]{0,1:T(8,128)(2,1)S(1)} %get-tuple-element.32), channel_id=1, source_target_pairs={{0,1},{3,2},{4,5},{7,6},{11,10},{15,14},{16,17},{20,21},{24,25},{2... | collective-permute-start | bytes 786440 | tf_op jit(solution)/shard_map/ppermute | solution.py:66
  164.6 8.5 %collective-permute-start.41 = (f16[512,256]{0,1:T(8,128)(2,1)S(1)}, f16[512,256]{0,1:T(8,128)(2,1)S(1)}, u32[]{:S(2)}, u32[]{:S(2)}) collective-permute-start(f16[512,256]{0,1:T(8,128)(2,1)S(1)} %get-tuple-element.20), channel_id=1, source_target_pairs={{0,1},{4,5},{8,9},{11,10},{12,13},{15,14},{16,17},{19,18},{20,21},... | collective-permute-start | bytes 786440 | tf_op jit(solution)/shard_map/ppermute | solution.py:66
  169.3 4.6 %collective-permute-start.53 = (f16[512,256]{0,1:T(8,128)(2,1)S(1)}, f16[512,256]{0,1:T(8,128)(2,1)S(1)}, u32[]{:S(2)}, u32[]{:S(2)}) collective-permute-start(f16[512,256]{0,1:T(8,128)(2,1)S(1)} %get-tuple-element.12), channel_id=1, source_target_pairs={{0,1},{4,5},{8,9},{11,10},{12,13},{15,14},{16,17},{19,18},{20,21},... | collective-permute-start | bytes 786440 | tf_op jit(solution)/shard_map/ppermute | solution.py:66
  173.0 6.2 %collective-permute-start.5 = (bf16[256,1536]{1,0:T(8,128)(2,1)S(1)}, bf16[256,1536]{1,0:T(8,128)(2,1)S(1)}, u32[]{:S(2)}, u32[]{:S(2)}) collective-permute-start(bf16[256,1536]{1,0:T(8,128)(2,1)S(1)} %collective-permute-done.4), channel_id=1, source_target_pairs={{0,4},{4,0},{8,12},{12,8},{16,20},{20,16},{24,28},{28,24},{1,5},{5... | collective-permute-start | bytes 2359304 | tf_op jit(solution)/shard_map/ppermute | solution.py:13
  178.5 6.2 %collective-permute-start.49 = (f16[512,256]{0,1:T(8,128)(2,1)S(1)}, f16[512,256]{0,1:T(8,128)(2,1)S(1)}, u32[]{:S(2)}, u32[]{:S(2)}) collective-permute-start(f16[512,256]{0,1:T(8,128)(2,1)S(1)} %fusion.65), channel_id=1, source_target_pairs={{9,8},{13,12},{18,19},{22,23}} | collective-permute-start | bytes 786440 | tf_op jit(solution)/shard_map/ppermute | solution.py:66
  179.3 39.8 %collective-permute-start.43 = (f16[512,256]{0,1:T(8,128)(2,1)S(1)}, f16[512,256]{0,1:T(8,128)(2,1)S(1)}, u32[]{:S(2)}, u32[]{:S(2)}) collective-permute-start(f16[512,256]{0,1:T(8,128)(2,1)S(1)} %fusion.59), channel_id=1, source_target_pairs={{2,3},{6,7},{25,24},{29,28}} | collective-permute-start | bytes 786440 | tf_op jit(solution)/shard_map/ppermute | solution.py:66
  182.5 41.1 %collective-permute-start.64 = (f16[512,256]{0,1:T(8,128)(2,1)S(1)}, f16[512,256]{0,1:T(8,128)(2,1)S(1)}, u32[]{:S(2)}, u32[]{:S(2)}) collective-permute-start(f16[512,256]{0,1:T(8,128)(2,1)S(1)} %fusion.78), channel_id=1, source_target_pairs={{1,0},{5,4},{26,27},{30,31}} | collective-permute-start | bytes 786440 | tf_op jit(solution)/shard_map/ppermute | solution.py:66
  183.3 41.0 %collective-permute-start.58 = (f16[512,256]{0,1:T(8,128)(2,1)S(1)}, f16[512,256]{0,1:T(8,128)(2,1)S(1)}, u32[]{:S(2)}, u32[]{:S(2)}) collective-permute-start(f16[512,256]{0,1:T(8,128)(2,1)S(1)} %fusion.73), channel_id=1, source_target_pairs={{10,11},{14,15},{17,16},{21,20}} | collective-permute-start | bytes 786440 | tf_op jit(solution)/shard_map/ppermute | solution.py:66
  184.0 41.0 %collective-permute-start.61 = (f16[512,256]{0,1:T(8,128)(2,1)S(1)}, f16[512,256]{0,1:T(8,128)(2,1)S(1)}, u32[]{:S(2)}, u32[]{:S(2)}) collective-permute-start(f16[512,256]{0,1:T(8,128)(2,1)S(1)} %fusion.76), channel_id=1, source_target_pairs={{9,8},{13,12},{18,19},{22,23}} | collective-permute-start | bytes 786440 | tf_op jit(solution)/shard_map/ppermute | solution.py:66
  184.7 36.7 %collective-permute-start.25 = (f16[512,256]{0,1:T(8,128)(2,1)S(1)}, f16[512,256]{0,1:T(8,128)(2,1)S(1)}, u32[]{:S(2)}, u32[]{:S(2)}) collective-permute-start(f16[512,256]{0,1:T(8,128)(2,1)S(1)} %get-tuple-element.28), channel_id=1, source_target_pairs={{0,1},{4,5},{8,9},{11,10},{12,13},{15,14},{16,17},{19,18},{20,21},... | collective-permute-start | bytes 786440 | tf_op jit(solution)/shard_map/ppermute | solution.py:66
  219.1 3.7 %collective-permute-start.7 = (f16[512,256]{0,1:T(8,128)(2,1)S(1)}, f16[512,256]{0,1:T(8,128)(2,1)S(1)}, u32[]{:S(2)}, u32[]{:S(2)}) collective-permute-start(f16[512,256]{0,1:T(8,128)(2,1)S(1)} %fusion.79), channel_id=1, source_target_pairs={{1,2},{5,6},{9,10},{13,14},{18,17},{22,21},{26,25},{30,29}} | collective-permute-start | bytes 786440 | tf_op jit(solution)/shard_map/ppermute | solution.py:66
  221.4 8.3 %collective-permute-start.55 = (f16[512,256]{0,1:T(8,128)(2,1)S(1)}, f16[512,256]{0,1:T(8,128)(2,1)S(1)}, u32[]{:S(2)}, u32[]{:S(2)}) collective-permute-start(f16[512,256]{0,1:T(8,128)(2,1)S(1)} %fusion.70), channel_id=1, source_target_pairs={{2,3},{6,7},{25,24},{29,28}} | collective-permute-start | bytes 786440 | tf_op jit(solution)/shard_map/ppermute | solution.py:66
  222.8 10.8 %collective-permute-start.21 = (f16[512,256]{0,1:T(8,128)(2,1)S(1)}, f16[512,256]{0,1:T(8,128)(2,1)S(1)}, u32[]{:S(2)}, u32[]{:S(2)}) collective-permute-start(f16[512,256]{0,1:T(8,128)(2,1)S(1)} %fusion.45), channel_id=1, source_target_pairs={{1,0},{5,4},{26,27},{30,31}} | collective-permute-start | bytes 786440 | tf_op jit(solution)/shard_map/ppermute | solution.py:66
  223.6 10.7 %collective-permute-start.12 = (f16[512,256]{0,1:T(8,128)(2,1)S(1)}, f16[512,256]{0,1:T(8,128)(2,1)S(1)}, u32[]{:S(2)}, u32[]{:S(2)}) collective-permute-start(f16[512,256]{0,1:T(8,128)(2,1)S(1)} %fusion.40), channel_id=1, source_target_pairs={{10,11},{14,15},{17,16},{21,20}} | collective-permute-start | bytes 786440 | tf_op jit(solution)/shard_map/ppermute | solution.py:66
  224.3 10.7 %collective-permute-start.17 = (f16[512,256]{0,1:T(8,128)(2,1)S(1)}, f16[512,256]{0,1:T(8,128)(2,1)S(1)}, u32[]{:S(2)}, u32[]{:S(2)}) collective-permute-start(f16[512,256]{0,1:T(8,128)(2,1)S(1)} %fusion.43), channel_id=1, source_target_pairs={{9,8},{13,12},{18,19},{22,23}} | collective-permute-start | bytes 786440 | tf_op jit(solution)/shard_map/ppermute | solution.py:66
  225.0 7.8 %collective-permute-start.26 = (f16[512,256]{0,1:T(8,128)(2,1)S(1)}, f16[512,256]{0,1:T(8,128)(2,1)S(1)}, u32[]{:S(2)}, u32[]{:S(2)}) collective-permute-start(f16[512,256]{0,1:T(8,128)(2,1)S(1)} %fusion.83), channel_id=1, source_target_pairs={{1,2},{5,6},{9,10},{13,14},{18,17},{22,21},{26,25},{30,29}} | collective-permute-start | bytes 786440 | tf_op jit(solution)/shard_map/ppermute | solution.py:66
  229.7 11.9 %collective-permute-start.8 = (f16[512,256]{0,1:T(8,128)(2,1)S(1)}, f16[512,256]{0,1:T(8,128)(2,1)S(1)}, u32[]{:S(2)}, u32[]{:S(2)}) collective-permute-start(f16[512,256]{0,1:T(8,128)(2,1)S(1)} %fusion.37), channel_id=1, source_target_pairs={{2,3},{6,7},{25,24},{29,28}} | collective-permute-start | bytes 786440 | tf_op jit(solution)/shard_map/ppermute | solution.py:66
  232.8 9.4 %collective-permute-start.40 = (f16[512,256]{0,1:T(8,128)(2,1)S(1)}, f16[512,256]{0,1:T(8,128)(2,1)S(1)}, u32[]{:S(2)}, u32[]{:S(2)}) collective-permute-start(f16[512,256]{0,1:T(8,128)(2,1)S(1)} %fusion.56), channel_id=1, source_target_pairs={{1,0},{5,4},{26,27},{30,31}} | collective-permute-start | bytes 786440 | tf_op jit(solution)/shard_map/ppermute | solution.py:66
  233.6 8.6 %collective-permute-start.32 = (f16[512,256]{0,1:T(8,128)(2,1)S(1)}, f16[512,256]{0,1:T(8,128)(2,1)S(1)}, u32[]{:S(2)}, u32[]{:S(2)}) collective-permute-start(f16[512,256]{0,1:T(8,128)(2,1)S(1)} %fusion.51), channel_id=1, source_target_pairs={{10,11},{14,15},{17,16},{21,20}} | collective-permute-start | bytes 786440 | tf_op jit(solution)/shard_map/ppermute | solution.py:66
  234.3 7.9 %collective-permute-start.36 = (f16[512,256]{0,1:T(8,128)(2,1)S(1)}, f16[512,256]{0,1:T(8,128)(2,1)S(1)}, u32[]{:S(2)}, u32[]{:S(2)}) collective-permute-start(f16[512,256]{0,1:T(8,128)(2,1)S(1)} %fusion.54), channel_id=1, source_target_pairs={{9,8},{13,12},{18,19},{22,23}} | collective-permute-start | bytes 786440 | tf_op jit(solution)/shard_map/ppermute | solution.py:66
  235.0 16.0 %collective-permute-start.27 = (f16[512,256]{0,1:T(8,128)(2,1)S(1)}, f16[512,256]{0,1:T(8,128)(2,1)S(1)}, u32[]{:S(2)}, u32[]{:S(2)}) collective-permute-start(f16[512,256]{0,1:T(8,128)(2,1)S(1)} %fusion.48), channel_id=1, source_target_pairs={{2,3},{6,7},{25,24},{29,28}} | collective-permute-start | bytes 786440 | tf_op jit(solution)/shard_map/ppermute | solution.py:66
  (19 other events, 38.0 us)

commit v2 on v0

v2 whole, which is shorter than its diff:
```python
import math

import jax
import jax.numpy as jnp
from jax import lax
from jax.experimental import pallas as pl
from jax.experimental.pallas import tpu as pltpu
from jax.sharding import PartitionSpec as P

CHUNKS = 2
EXTRA = 16
STEPS = 2
AXES = ("proj", "row")


def hop(x, axis, size, mask):
    return lax.ppermute(x, axis, [(i, i ^ mask) for i in range(size)])


def scale_up(share):
    t = jnp.ones_like(share)
    for e in (32, 16, 8, 4, 2, 1):
        small = share < 2.0 ** (-2 * e)
        t = jnp.where(small, t * 2.0**e, t)
        share = jnp.where(small, share * 2.0 ** (2 * e), share)
    return t


def filtered_rows(x_ref):
    columns = x_ref.shape[2]
    parts = []
    for d in range(x_ref.shape[1]):
        x = x_ref[:, d, :]
        parts.append(x - jnp.sum(x, axis=1, keepdims=True) * (1.0 / columns))
    return parts


def energy_kernel(x_ref, energy_ref):
    total = 0.0
    for f in filtered_rows(x_ref):
        total = total + jnp.sum(f * f, axis=1, keepdims=True)
    energy_ref[...] = jnp.transpose(jnp.broadcast_to(total, (total.shape[0], 128)))[:1, :]


def norm_kernel(entries, x_ref, *refs):
    energies, out_ref = refs[:-1], refs[-1]
    step, _, columns = x_ref.shape
    i = pl.program_id(0)
    tile = step * pl.num_programs(0)
    parts = [e[...] for e in energies]
    while len(parts) > 1:
        parts = [a + b for a, b in zip(parts[::2], parts[1::2])]
    power = parts[0] / entries
    t = scale_up(power / (power + 1e-05))
    factor = jnp.transpose(jnp.broadcast_to(lax.rsqrt(power + 1e-05), (128, step)))[:, :1]
    up = jnp.transpose(jnp.broadcast_to(t, (128, step)))[:, :1]
    here = pl.ds(pl.multiple_of(i * step, 128), step)
    for d, f in enumerate(filtered_rows(x_ref)):
        normed = f * factor * (1.0 / math.sqrt(entries)) * up
        out_ref[here, d * columns : (d + 1) * columns] = normed.astype(jnp.bfloat16)
    last = slice(out_ref.shape[0] - EXTRA, out_ref.shape[0])

    @pl.when(i == 0)
    def _():
        out_ref[last, :] = jnp.zeros((EXTRA, out_ref.shape[1]), jnp.bfloat16)

    out_ref[last, here] = jnp.broadcast_to(t, (EXTRA, step)).astype(jnp.bfloat16)


def normalize(x, nr):
    tile, det_rows, columns = x.shape
    step = tile // STEPS
    width = det_rows * columns
    rows = pl.BlockSpec((step, det_rows, columns), lambda i: (i, 0, 0))
    line = pl.BlockSpec((1, step), lambda i: (0, i))
    vec = jax.ShapeDtypeStruct((1, tile), jnp.float32)
    energy = pl.pallas_call(energy_kernel, grid=(STEPS,), in_specs=[rows], out_specs=line, out_shape=vec)(x)
    parts = [energy] + [hop(energy, "row", nr, d) for d in range(1, nr)]
    return pl.pallas_call(
        lambda *refs: norm_kernel(width * nr, *refs),
        grid=(STEPS,),
        in_specs=[rows] + [line] * nr,
        out_specs=pl.BlockSpec((tile + EXTRA, width), lambda i: (0, 0)),
        out_shape=jax.ShapeDtypeStruct((tile + EXTRA, width), jnp.bfloat16),
    )(x, *parts)


def gate(x, *others):
    return pl.pallas_call(
        lambda *refs: None,
        in_specs=[pl.BlockSpec(memory_space=pl.ANY)] * (1 + len(others)),
        out_specs=pl.BlockSpec(memory_space=pl.ANY),
        out_shape=jax.ShapeDtypeStruct(x.shape, x.dtype),
        input_output_aliases={0: 0},
        compiler_params=pltpu.CompilerParams(vmem_limit_bytes=1 << 16),
        cost_estimate=pl.CostEstimate(flops=0, bytes_accessed=0, transcendentals=0),
    )(x, *others)


def tree(np_, nr, group, k):
    stages = []
    size = 1
    while size < nr:
        pairs = []
        for s in range(np_):
            d = (s // group) ^ k

            def head(g):
                return min(range(g * size, (g + 1) * size), key=lambda i: abs(i - d))

            for g in range(0, nr // size, 2):
                a, b = head(g), head(g + 1)
                if abs(a - d) < abs(b - d):
                    a, b = b, a
                pairs.append((s * nr + a, s * nr + b))
        stages.append(pairs)
        size *= 2
    return stages


def schedule(nr, group):
    piece_time, sum_time, gap = 1.5, 1.0, 0.35
    free, there, sends = {}, {(0, q): 0.0 for q in range(CHUNKS)}, []
    for w in range(1, nr.bit_length()):
        for q in range(CHUNKS):
            for k in range(1, nr):
                bits = [b for b in (1 << i for i in range(nr.bit_length())) if k & b]
                if len(bits) == w:
                    b = bits[q % w]
                    begin = max(free.get(b, 0.0), there[k ^ b, q] + (gap if w > 1 else 0.0))
                    free[b] = begin + piece_time
                    there[k, q] = free[b] + gap
                    sends.append((k, q, b))
    ready = [(0.2 + 0.5 * j, (0, j)) for j in range(group)] + [(there[k, q], (k, q)) for k, q, _ in sends]
    events = [(time, 1, "unit", unit) for time, unit in ready]
    line = 0.0
    for time, unit in sorted(ready):
        line = max(line, time) + sum_time
        for stage in range(nr.bit_length() - 1):
            events.append((line + gap + stage * (sum_time + gap), 2, stage, unit))
    return sends, [e[2:] for e in sorted(events, key=lambda e: e[:2])]


def per_device(projections):
    tile = projections.shape[0]
    np_, nr = lax.axis_size("proj"), lax.axis_size("row")
    group = np_ // nr
    p, z = lax.axis_index("proj"), lax.axis_index("row")
    member = p % group
    piece = tile // CHUNKS
    stages = {k: tree(np_, nr, group, k) for k in range(nr)}
    mine = {k: (p // group) ^ k == z for k in range(nr)}
    sends, events = schedule(nr, group)

    block = normalize(projections, nr)
    own = block[:tile]
    held = {(0, q): block[q * piece : (q + 1) * piece + (EXTRA if q == CHUNKS - 1 else 0)] for q in range(CHUNKS)}

    def forward(src):
        for k, q, b in sends:
            if (k ^ b, q) == src:
                held[k, q] = hop(held[src], "proj", np_, b * group)

    for q in range(CHUNKS):
        forward((0, q))
    siblings = [block] + [hop(block, "proj", np_, j) for j in range(1, group)]

    def product(rows, columns):
        return lax.dot_general(rows, columns, (((1,), (1,)), ((), ())), preferred_element_type=jnp.float32)

    token, everyone = [], None
    carry, moving, result, scale = {}, {}, {}, None
    for kind, unit in events:
        k, q = unit
        if kind == "unit":
            if k == 0:
                if q:
                    siblings[q] = gate(siblings[q], *token)
                carry[unit] = product(siblings[q][:tile], own)
            else:
                if everyone is None:
                    everyone = jnp.concatenate([s[:tile] for s in siblings], axis=0)
                    scale = block[tile : tile + 1, :tile]
                held[unit] = gate(held[unit], *token)
                forward(unit)
                carry[unit] = product(everyone, held[unit][:piece])
                if q == CHUNKS - 1:
                    scale = jnp.where(mine[k], held[unit][piece : piece + 1, :tile], scale)
            message = carry[unit].astype(jnp.float16)
            moving[unit] = lax.ppermute(message, AXES, stages[k][0])
        else:
            carry[unit] = gate(carry[unit], *token) + moving[unit].astype(jnp.float32)
            if kind + 1 < len(stages[k]):
                message = carry[unit].astype(jnp.float16)
                moving[unit] = lax.ppermute(message, AXES, stages[k][kind + 1])
            else:
                if k == 0:
                    now = {(q, i): carry[unit][:, i * piece : (i + 1) * piece] for i in range(CHUNKS)}
                else:
                    now = {(j, q): carry[unit][j * tile : (j + 1) * tile] for j in range(group)}
                for at, r in now.items():
                    result[at] = r if at not in result else jnp.where(mine[k], r, result[at])
        token = [carry[unit]]

    across = 1.0 / scale.astype(jnp.float32)
    parts = []
    for j in range(group):
        r = jnp.concatenate([result[j, i] for i in range(CHUNKS)], axis=1) * across
        parts.append(hop(r, "proj", np_, j) if j else r)
    columns = []
    for j in range(group):
        b = parts[j]
        for i in range(1, group):
            b = jnp.where(member == i, parts[j ^ i], b)
        columns.append(b)
    down = 1.0 / block[tile : tile + 1, :tile].astype(jnp.float32)
    return jnp.concatenate(columns, axis=1) * down.reshape(tile, 1)


def solution(mesh):
    return jax.shard_map(
        per_device, mesh=mesh, in_specs=(P("proj", "row", None),), out_specs=P("proj", "row"), check_vma=False
    )
```

time: 261 us -> 153 us (0.59)
  waiting for transfers between devices: 219 us -> 63.6 us
  starting transfers between devices: 0.04 us -> 59.6 us
  between operations: 13.4 us -> 0.75 us
  blocking collectives: 7.26 us -> 0 us
  Pallas kernels: 0 us -> 7.11 us
  other arithmetic: 6.33 us -> 9.41 us
    reduce_scatter x1 -> x0, waiting for transfers between devices: 144 us -> none  [per_device(): return lax.psum_scatter(product, 'row', scatter_dimension=1, tiled=True)]
    all_gather x1 -> x0, waiting for transfers between devices: 74.9 us -> none  [per_device(): lax.all_gather(flattened, 'proj', axis=0, tiled=True)]
    ppermute x0 -> x27, waiting for transfers between devices: none -> 63.6 us  [the longest x8 41.8 us: per_device(): moving[unit] = lax.ppermute(message, AXES, stages[k][kind + 1])]
    ppermute x0 -> x27, starting transfers between devices: none -> 59.6 us  [the longest x8 24.9 us: per_device(): moving[unit] = lax.ppermute(message, AXES, stages[k][kind + 1])]
    psum x1 -> x0, blocking collectives: 7.26 us -> none  [per_device(): energy = lax.psum(jnp.sum(filtered * filtered, axis=(1, 2)), 'row')]
    pallas_call x0 -> x25, Pallas kernels: none -> 7.11 us  [the longest x1 3.94 us: normalize(): pl.pallas_call(lambda *refs: norm_kernel(width * nr, *refs), grid=(STEPS,...]
    reduce_sum x2 -> x0, other arithmetic: 4.7 us -> none  [the longest x1 4.25 us: per_device(): filtered = projections - jnp.mean(projections, axis=2, keepdims=True)]
    add x0 -> x8, other arithmetic: none -> 3.02 us  [per_device(): carry[unit] = gate(carry[unit], *token) + moving[unit].astype(jnp.float32)]
  transfers between devices with their start and end apart: 2 -> 27, of which waited for: 2 -> 14; matrix products, arithmetic and copies ran while one was open for 0% -> 11% of each run, Pallas kernels for 0% -> 0%
where the time goes in v2:
time: 153 us
  waiting for transfers between devices  63.6 us (42%)
  starting transfers between devices  59.6 us (39%)
  matrix products  10 us (7%)
  other arithmetic  9.41 us (6%)
  Pallas kernels  7.11 us (5%)
  local copies, waits for them, and re-layouts  2.24 us (1%)
    ppermute x8, waiting for transfers between devices, per_device(): moving[unit] = lax.ppermute(message, AXES, stages[k][kind + 1])  41.8 us
    ppermute x8, starting transfers between devices, per_device(): moving[unit] = lax.ppermute(message, AXES, stages[k][kind + 1])  24.9 us
    ppermute x11, starting transfers between devices, hop(): return lax.ppermute(x, axis, [(i, i ^ mask) for i in range(size)])  21.1 us
    ppermute x8, starting transfers between devices, per_device(): moving[unit] = lax.ppermute(message, AXES, stages[k][0])  13.7 us
    ppermute x8, waiting for transfers between devices, per_device(): moving[unit] = lax.ppermute(message, AXES, stages[k][0])  13 us
    dot_general x8, matrix products, product(): lax.dot_general(rows, columns, (((1,), (1,)), ((), ())), preferred_elemen...  10 us
    ppermute x11, waiting for transfers between devices, hop(): return lax.ppermute(x, axis, [(i, i ^ mask) for i in range(size)])  8.84 us
    pallas_call x1, Pallas kernels, normalize(): pl.pallas_call(lambda *refs: norm_kernel(width * nr, *refs), grid=(STEPS,...  3.94 us
  transfers between devices with their start and end apart: 27, of which 14 were waited for; matrix products, arithmetic and copies ran while one was open for 11% of the time, Pallas kernels for 0%

profile of v2, /device:TPU:13, one launch (start us, length us, event | category | flops | bytes accessed | tf_op | source)
XLA Modules:
  0.0 152.8 jit_solution(17064887009604969175)
XLA Ops:
  0.0 3.1 %shard_map.17.refs_1_ = f32[1,512]{1,0:T(1,128)} custom-call(f32[512,1,1536]{2,1,0:T(1,128)} %refs_0_.1), custom_call_target="tpu_custom_call" | custom-call | tf_op jit(solution)/shard_map/pallas_call | solution.py:77
  3.3 2.3 %collective-permute-start.1 = (f32[1,512]{1,0:T(1,128)}, f32[1,512]{1,0:T(1,128)S(1)}, u32[]{:S(2)}, u32[]{:S(2)}) collective-permute-start(f32[1,512]{1,0:T(1,128)} %shard_map.17.refs_1_), channel_id=1, source_target_pairs={{0,2},{1,3},{2,0},{3,1},{4,6},{5,7},{6,4},{7,5},{8,10},{9,11},{10,... | collective-permute-start | bytes 6152 | tf_op jit(solution)/shard_map/ppermute | solution.py:17
  5.8 1.1 collective-permute-done.1.refs_3_
  6.9 1.7 %collective-permute-done.2.refs_4_ = f32[1,512]{1,0:T(1,128)S(1)} collective-permute-done((f32[1,512]{1,0:T(1,128)}, f32[1,512]{1,0:T(1,128)S(1)}, u32[]{:S(2)}, u32[]{:S(2)}) %collective-permute-start.2) | collective-permute-done | bytes 2080 | tf_op jit(solution)/shard_map/ppermute | solution.py:17
  9.1 3.9 %shard_map.18 = bf16[528,1536]{1,0:T(8,128)(2,1)} custom-call(f32[512,1,1536]{2,1,0:T(1,128)} %refs_0_.1, f32[1,512]{1,0:T(1,128)} %shard_map.17.refs_1_, f32[1,512]{1,0:T(1,128)} %copy-done.14, f32[1,512]{1,0:T(1,128)} %copy-done.15, f32[1,512]{1,0:T(1,128)} %copy-done.16), custom_call_target="tpu_custom_call" | custom-call | tf_op jit(solution)/shard_map/pallas_call | solution.py:79
  13.1 2.1 %collective-permute-start.3 = (bf16[528,1536]{1,0:T(8,128)(2,1)}, bf16[528,1536]{1,0:T(8,128)(2,1)S(1)}, u32[]{:S(2)}, u32[]{:S(2)}) collective-permute-start(bf16[528,1536]{1,0:T(8,128)(2,1)} %shard_map.18), channel_id=1, source_target_pairs={{0,4},{4,0},{8,12},{12,8},{16,20},{20,16},{24,28},{28,24},{1,5},{5... | collective-permute-start | bytes 4866056 | tf_op jit(solution)/shard_map/ppermute | solution.py:17
  15.2 3.0 %fusion.34 = (f16[512,512]{1,0:T(8,128)(2,1)S(1)}, f32[512,512]{1,0:T(8,128)S(1)}) fusion(bf16[528,1536]{1,0:T(8,128)(2,1)} %shard_map.18), kind=kOutput, calls=%fused_computation.62 | convolution fusion | flops 805568512 | bytes 3145728 | tf_op jit(solution)/shard_map/dot_general | solution.py:169
  18.1 1.3 collective-permute-start.6
  19.5 1.3 collective-permute-start.5
  20.9 2.8 %collective-permute-start.4 = (bf16[256,1536]{1,0:T(8,128)(2,1)S(1)}, bf16[256,1536]{1,0:T(8,128)(2,1)S(1)}, u32[]{:S(2)}, u32[]{:S(2)}) collective-permute-start(bf16[256,1536]{1,0:T(8,128)(2,1)S(1)} %slice.114), channel_id=1, source_target_pairs={{0,16},{4,20},{8,24},{12,28},{16,0},{20,4},{24,8},{28,12},{1,17},{... | collective-permute-start | bytes 2359304 | tf_op jit(solution)/shard_map/ppermute | solution.py:17
  23.8 1.5 collective-permute-start.10
  25.3 1.0 fusion.35
  26.5 8.3 %collective-permute-done.6 = f16[512,512]{1,0:T(8,128)(2,1)S(1)} collective-permute-done((f16[512,512]{1,0:T(8,128)(2,1)S(1)}, f16[512,512]{1,0:T(8,128)(2,1)S(1)}, u32[]{:S(2)}, u32[]{:S(2)}) %collective-permute-start.6) | collective-permute-done | bytes 524320 | tf_op jit(solution)/shard_map/ppermute | solution.py:190
  34.8 1.3 collective-permute-start.8
  36.3 2.4 %collective-permute-done.5.refs_0_ = bf16[256,1536]{1,0:T(8,128)(2,1)S(1)} collective-permute-done((bf16[256,1536]{1,0:T(8,128)(2,1)S(1)}, bf16[256,1536]{1,0:T(8,128)(2,1)S(1)}, u32[]{:S(2)}, u32[]{:S(2)}) %collective-permute-start.5) | collective-permute-done | bytes 786464 | tf_op jit(solution)/shard_map/ppermute | solution.py:17
  38.7 4.5 %collective-permute-start.11 = (f16[512,512]{1,0:T(8,128)(2,1)S(1)}, f16[512,512]{1,0:T(8,128)(2,1)S(1)}, u32[]{:S(2)}, u32[]{:S(2)}) collective-permute-start(f16[512,512]{1,0:T(8,128)(2,1)S(1)} %get-tuple-element.19), channel_id=1, source_target_pairs={{2,0},{6,4},{10,9},{14,13},{17,18},{21,22},{25,27},{29,31}} | collective-permute-start | bytes 1572872 | tf_op jit(solution)/shard_map/ppermute | solution.py:195
  43.2 1.0 fusion.36
  45.9 3.6 %collective-permute-done.8 = f16[512,512]{1,0:T(8,128)(2,1)S(1)} collective-permute-done((f16[512,512]{1,0:T(8,128)(2,1)S(1)}, f16[512,512]{1,0:T(8,128)(2,1)S(1)}, u32[]{:S(2)}, u32[]{:S(2)}) %collective-permute-start.8) | collective-permute-done | bytes 524320 | tf_op jit(solution)/shard_map/ppermute | solution.py:190
  49.5 1.3 collective-permute-start.12
  51.0 2.1 %collective-permute-done.11 = f16[512,512]{1,0:T(8,128)(2,1)S(1)} collective-permute-done((f16[512,512]{1,0:T(8,128)(2,1)S(1)}, f16[512,512]{1,0:T(8,128)(2,1)S(1)}, u32[]{:S(2)}, u32[]{:S(2)}) %collective-permute-start.11) | collective-permute-done | bytes 524320 | tf_op jit(solution)/shard_map/ppermute | solution.py:195
  53.1 2.0 %collective-permute-start.14 = (f16[1024,256]{1,0:T(8,128)(2,1)S(1)}, f16[1024,256]{1,0:T(8,128)(2,1)S(1)}, u32[]{:S(2)}, u32[]{:S(2)}) collective-permute-start(f16[1024,256]{1,0:T(8,128)(2,1)S(1)} %get-tuple-element.37), channel_id=1, source_target_pairs={{0,1},{3,2},{4,5},{7,6},{8,9},{10,11},{12,13},{14,15},{17,16},{19,... | collective-permute-start | bytes 1572872 | tf_op jit(solution)/shard_map/ppermute | solution.py:190
  55.3 1.3 collective-permute-done.10.refs_0_
  56.6 1.0 fusion.38
  57.7 7.0 %collective-permute-start.15 = (bf16[272,1536]{1,0:T(8,128)(2,1)S(1)}, bf16[272,1536]{1,0:T(8,128)(2,1)S(1)}, u32[]{:S(2)}, u32[]{:S(2)}) collective-permute-start(bf16[272,1536]{1,0:T(8,128)(2,1)S(1)} %shard_map.25), channel_id=1, source_target_pairs={{0,16},{4,20},{8,24},{12,28},{16,0},{20,4},{24,8},{28,12},{1,17},{... | collective-permute-start | bytes 2506760 | tf_op jit(solution)/shard_map/ppermute | solution.py:17
  64.7 1.3 collective-permute-start.13
  66.0 1.0 fusion.39
  67.3 1.3 collective-permute-start.16
  68.6 6.9 %collective-permute-done.13 = f16[512,512]{1,0:T(8,128)(2,1)S(1)} collective-permute-done((f16[512,512]{1,0:T(8,128)(2,1)S(1)}, f16[512,512]{1,0:T(8,128)(2,1)S(1)}, u32[]{:S(2)}, u32[]{:S(2)}) %collective-permute-start.13) | collective-permute-done | bytes 524320 | tf_op jit(solution)/shard_map/ppermute | solution.py:195
  75.5 1.3 collective-permute-start.17
  76.9 4.0 %collective-permute-start.19 = (f16[1024,256]{1,0:T(8,128)(2,1)S(1)}, f16[1024,256]{1,0:T(8,128)(2,1)S(1)}, u32[]{:S(2)}, u32[]{:S(2)}) collective-permute-start(f16[1024,256]{1,0:T(8,128)(2,1)S(1)} %get-tuple-element.41), channel_id=1, source_target_pairs={{0,1},{3,2},{4,5},{7,6},{8,9},{10,11},{12,13},{14,15},{17,16},{19,... | collective-permute-start | bytes 1572872 | tf_op jit(solution)/shard_map/ppermute | solution.py:190
  81.2 1.0 fusion.40
  82.9 3.8 %collective-permute-done.16 = f16[1024,256]{1,0:T(8,128)(2,1)S(1)} collective-permute-done((f16[1024,256]{1,0:T(8,128)(2,1)S(1)}, f16[1024,256]{1,0:T(8,128)(2,1)S(1)}, u32[]{:S(2)}, u32[]{:S(2)}) %collective-permute-start.16) | collective-permute-done | bytes 524320 | tf_op jit(solution)/shard_map/ppermute | solution.py:195
  86.8 1.3 collective-permute-start.21
  88.2 1.0 fusion.41
  89.7 13.8 %collective-permute-start.20 = (f16[1024,256]{1,0:T(8,128)(2,1)S(1)}, f16[1024,256]{1,0:T(8,128)(2,1)S(1)}, u32[]{:S(2)}, u32[]{:S(2)}) collective-permute-start(f16[1024,256]{1,0:T(8,128)(2,1)S(1)} %get-tuple-element.11), channel_id=1, source_target_pairs={{2,1},{6,5},{10,8},{14,12},{17,19},{21,23},{25,26},{29,30}} | collective-permute-start | bytes 1572872 | tf_op jit(solution)/shard_map/ppermute | solution.py:195
  103.5 1.3 collective-permute-start.23
  106.8 6.5 %collective-permute-done.20 = f16[1024,256]{1,0:T(8,128)(2,1)S(1)} collective-permute-done((f16[1024,256]{1,0:T(8,128)(2,1)S(1)}, f16[1024,256]{1,0:T(8,128)(2,1)S(1)}, u32[]{:S(2)}, u32[]{:S(2)}) %collective-permute-start.20) | collective-permute-done | bytes 524320 | tf_op jit(solution)/shard_map/ppermute | solution.py:195
  113.4 1.2 fusion.27
  114.7 1.3 collective-permute-start.24
  116.1 1.1 collective-permute-done.23
  118.1 1.3 collective-permute-start.25
  120.2 12.4 %collective-permute-done.24 = f16[1024,256]{1,0:T(8,128)(2,1)} collective-permute-done((f16[1024,256]{1,0:T(8,128)(2,1)}, f16[1024,256]{1,0:T(8,128)(2,1)}, u32[]{:S(2)}, u32[]{:S(2)}) %collective-permute-start.24) | collective-permute-done | bytes 524320 | tf_op jit(solution)/shard_map/ppermute | solution.py:195
  132.6 1.1 convert_add_fusion.1.refs_1_
  133.8 10.0 %collective-permute-done.25 = f16[1024,256]{1,0:T(8,128)(2,1)} collective-permute-done((f16[1024,256]{1,0:T(8,128)(2,1)}, f16[1024,256]{1,0:T(8,128)(2,1)}, u32[]{:S(2)}, u32[]{:S(2)}) %collective-permute-start.25) | collective-permute-done | bytes 524320 | tf_op jit(solution)/shard_map/ppermute | solution.py:195
  143.9 1.1 convert_add_fusion
  145.7 3.0 %collective-permute-start.26 = (f32[512,512]{1,0:T(8,128)S(1)}, f32[512,512]{1,0:T(8,128)S(1)}, u32[]{:S(2)}, u32[]{:S(2)}) collective-permute-start(f32[512,512]{1,0:T(8,128)S(1)} %maximum_multiply_fusion.1), channel_id=1, source_target_pairs={{0,4},{4,0},{8,12},{12,8},{16,20},{20,16},{24,28},{28,24},{1,5},{5... | collective-permute-start | bytes 3145736 | tf_op jit(solution)/shard_map/ppermute | solution.py:17
  148.7 2.3 %collective-permute-done.26 = f32[512,512]{1,0:T(8,128)S(1)} collective-permute-done((f32[512,512]{1,0:T(8,128)S(1)}, f32[512,512]{1,0:T(8,128)S(1)}, u32[]{:S(2)}, u32[]{:S(2)}) %collective-permute-start.26) | collective-permute-done | bytes 1048608 | tf_op jit(solution)/shard_map/ppermute | solution.py:17
  151.3 1.5 maximum_multiply_fusion
  (98 shorter events, 10.1 us)
Async XLA Ops:
  3.1 2.7 %collective-permute-start = (f32[1,512]{1,0:T(1,128)}, f32[1,512]{1,0:T(1,128)S(1)}, u32[]{:S(2)}, u32[]{:S(2)}) collective-permute-start(f32[1,512]{1,0:T(1,128)} %shard_map.17.refs_1_), channel_id=1, source_target_pairs={{0,1},{1,0},{2,3},{3,2},{4,5},{5,4},{6,7},{7,6},{8,9},{9,8},{10,11... | collective-permute-start | bytes 6152 | tf_op jit(solution)/shard_map/ppermute | solution.py:17
  3.3 3.6 %collective-permute-start.1 = (f32[1,512]{1,0:T(1,128)}, f32[1,512]{1,0:T(1,128)S(1)}, u32[]{:S(2)}, u32[]{:S(2)}) collective-permute-start(f32[1,512]{1,0:T(1,128)} %shard_map.17.refs_1_), channel_id=1, source_target_pairs={{0,2},{1,3},{2,0},{3,1},{4,6},{5,7},{6,4},{7,5},{8,10},{9,11},{10,... | collective-permute-start | bytes 6152 | tf_op jit(solution)/shard_map/ppermute | solution.py:17
  5.6 2.9 %collective-permute-start.2 = (f32[1,512]{1,0:T(1,128)}, f32[1,512]{1,0:T(1,128)S(1)}, u32[]{:S(2)}, u32[]{:S(2)}) collective-permute-start(f32[1,512]{1,0:T(1,128)} %shard_map.17.refs_1_), channel_id=1, source_target_pairs={{0,3},{1,2},{2,1},{3,0},{4,7},{5,6},{6,5},{7,4},{8,11},{9,10},{10,... | collective-permute-start | bytes 6152 | tf_op jit(solution)/shard_map/ppermute | solution.py:17
  5.8 2.8 %copy-start.14 = (f32[1,512]{1,0:T(1,128)}, f32[1,512]{1,0:T(1,128)S(1)}, u32[]{:S(2)}) copy-start(f32[1,512]{1,0:T(1,128)S(1)} %collective-permute-done.refs_2_) | copy-start | bytes 6148
  6.9 1.7 %copy-start.15 = (f32[1,512]{1,0:T(1,128)}, f32[1,512]{1,0:T(1,128)S(1)}, u32[]{:S(2)}) copy-start(f32[1,512]{1,0:T(1,128)S(1)} %collective-permute-done.1.refs_3_) | copy-start | bytes 6148
  8.6 0.6 copy-start.16
  13.1 6.4 %copy-start.13 = (bf16[528,1536]{1,0:T(8,128)(2,1)S(1)}, bf16[528,1536]{1,0:T(8,128)(2,1)}, u32[]{:S(2)}) copy-start(bf16[528,1536]{1,0:T(8,128)(2,1)} %shard_map.18) | copy-start | bytes 4866052
  13.1 12.2 %collective-permute-start.3 = (bf16[528,1536]{1,0:T(8,128)(2,1)}, bf16[528,1536]{1,0:T(8,128)(2,1)S(1)}, u32[]{:S(2)}, u32[]{:S(2)}) collective-permute-start(bf16[528,1536]{1,0:T(8,128)(2,1)} %shard_map.18), channel_id=1, source_target_pairs={{0,4},{4,0},{8,12},{12,8},{16,20},{20,16},{24,28},{28,24},{1,5},{5... | collective-permute-start | bytes 4866056 | tf_op jit(solution)/shard_map/ppermute | solution.py:17
  18.1 16.6 %collective-permute-start.6 = (f16[512,512]{1,0:T(8,128)(2,1)S(1)}, f16[512,512]{1,0:T(8,128)(2,1)S(1)}, u32[]{:S(2)}, u32[]{:S(2)}) collective-permute-start(f16[512,512]{1,0:T(8,128)(2,1)S(1)} %get-tuple-element.31), channel_id=1, source_target_pairs={{1,0},{3,2},{5,4},{7,6},{8,9},{11,10},{12,13},{15,14},{16,17},{19,... | collective-permute-start | bytes 1572872 | tf_op jit(solution)/shard_map/ppermute | solution.py:190
  19.5 19.2 %collective-permute-start.5 = (bf16[256,1536]{1,0:T(8,128)(2,1)S(1)}, bf16[256,1536]{1,0:T(8,128)(2,1)S(1)}, u32[]{:S(2)}, u32[]{:S(2)}) collective-permute-start(bf16[256,1536]{1,0:T(8,128)(2,1)S(1)} %slice.114), channel_id=1, source_target_pairs={{0,8},{4,12},{8,0},{12,4},{16,24},{20,28},{24,16},{28,20},{1,9},{5... | collective-permute-start | bytes 2359304 | tf_op jit(solution)/shard_map/ppermute | solution.py:17
  20.9 23.3 %collective-permute-start.4 = (bf16[256,1536]{1,0:T(8,128)(2,1)S(1)}, bf16[256,1536]{1,0:T(8,128)(2,1)S(1)}, u32[]{:S(2)}, u32[]{:S(2)}) collective-permute-start(bf16[256,1536]{1,0:T(8,128)(2,1)S(1)} %slice.114), channel_id=1, source_target_pairs={{0,16},{4,20},{8,24},{12,28},{16,0},{20,4},{24,8},{28,12},{1,17},{... | collective-permute-start | bytes 2359304 | tf_op jit(solution)/shard_map/ppermute | solution.py:17
  23.8 32.8 %collective-permute-start.10 = (bf16[272,1536]{1,0:T(8,128)(2,1)S(1)}, bf16[272,1536]{1,0:T(8,128)(2,1)S(1)}, u32[]{:S(2)}, u32[]{:S(2)}) collective-permute-start(bf16[272,1536]{1,0:T(8,128)(2,1)S(1)} %slice.115), channel_id=1, source_target_pairs={{0,8},{4,12},{8,0},{12,4},{16,24},{20,28},{24,16},{28,20},{1,9},{5... | collective-permute-start | bytes 2506760 | tf_op jit(solution)/shard_map/ppermute | solution.py:17
  25.3 39.4 %collective-permute-start.9 = (bf16[272,1536]{1,0:T(8,128)(2,1)S(1)}, bf16[272,1536]{1,0:T(8,128)(2,1)S(1)}, u32[]{:S(2)}, u32[]{:S(2)}) collective-permute-start(bf16[272,1536]{1,0:T(8,128)(2,1)S(1)} %slice.115), channel_id=1, source_target_pairs={{0,16},{4,20},{8,24},{12,28},{16,0},{20,4},{24,8},{28,12},{1,17},{... | collective-permute-start | bytes 2506760 | tf_op jit(solution)/shard_map/ppermute | solution.py:17
  34.8 14.8 %collective-permute-start.8 = (f16[512,512]{1,0:T(8,128)(2,1)S(1)}, f16[512,512]{1,0:T(8,128)(2,1)S(1)}, u32[]{:S(2)}, u32[]{:S(2)}) collective-permute-start(f16[512,512]{1,0:T(8,128)(2,1)S(1)} %get-tuple-element.33), channel_id=1, source_target_pairs={{1,0},{3,2},{5,4},{7,6},{8,9},{11,10},{12,13},{15,14},{16,17},{19,... | collective-permute-start | bytes 1572872 | tf_op jit(solution)/shard_map/ppermute | solution.py:190
  38.7 14.4 %collective-permute-start.11 = (f16[512,512]{1,0:T(8,128)(2,1)S(1)}, f16[512,512]{1,0:T(8,128)(2,1)S(1)}, u32[]{:S(2)}, u32[]{:S(2)}) collective-permute-start(f16[512,512]{1,0:T(8,128)(2,1)S(1)} %get-tuple-element.19), channel_id=1, source_target_pairs={{2,0},{6,4},{10,9},{14,13},{17,18},{21,22},{25,27},{29,31}} | collective-permute-start | bytes 1572872 | tf_op jit(solution)/shard_map/ppermute | solution.py:195
  44.2 36.9 %collective-permute-start.7 = (bf16[256,1536]{1,0:T(8,128)(2,1)S(1)}, bf16[256,1536]{1,0:T(8,128)(2,1)S(1)}, u32[]{:S(2)}, u32[]{:S(2)}) collective-permute-start(bf16[256,1536]{1,0:T(8,128)(2,1)S(1)} %shard_map.22), channel_id=1, source_target_pairs={{0,8},{4,12},{8,0},{12,4},{16,24},{20,28},{24,16},{28,20},{1,9},{5... | collective-permute-start | bytes 2359304 | tf_op jit(solution)/shard_map/ppermute | solution.py:17
  49.5 17.5 %collective-permute-start.12 = (f16[1024,256]{1,0:T(8,128)(2,1)S(1)}, f16[1024,256]{1,0:T(8,128)(2,1)S(1)}, u32[]{:S(2)}, u32[]{:S(2)}) collective-permute-start(f16[1024,256]{1,0:T(8,128)(2,1)S(1)} %get-tuple-element.35), channel_id=1, source_target_pairs={{0,1},{3,2},{4,5},{7,6},{9,8},{11,10},{13,12},{15,14},{16,17},{18,... | collective-permute-start | bytes 1572872 | tf_op jit(solution)/shard_map/ppermute | solution.py:190
  53.1 23.8 %collective-permute-start.14 = (f16[1024,256]{1,0:T(8,128)(2,1)S(1)}, f16[1024,256]{1,0:T(8,128)(2,1)S(1)}, u32[]{:S(2)}, u32[]{:S(2)}) collective-permute-start(f16[1024,256]{1,0:T(8,128)(2,1)S(1)} %get-tuple-element.37), channel_id=1, source_target_pairs={{0,1},{3,2},{4,5},{7,6},{8,9},{10,11},{12,13},{14,15},{17,16},{19,... | collective-permute-start | bytes 1572872 | tf_op jit(solution)/shard_map/ppermute | solution.py:190
  55.3 2.4 %copy-start.6 = (f32[512,512]{1,0:T(8,128)}, f32[512,512]{1,0:T(8,128)S(1)}, u32[]{:S(2)}) copy-start(f32[512,512]{1,0:T(8,128)S(1)} %convert_add_fusion.13.refs_1_) | copy-start | bytes 3145732
  56.6 1.0 copy-start.12
  57.7 30.5 %collective-permute-start.15 = (bf16[272,1536]{1,0:T(8,128)(2,1)S(1)}, bf16[272,1536]{1,0:T(8,128)(2,1)S(1)}, u32[]{:S(2)}, u32[]{:S(2)}) collective-permute-start(bf16[272,1536]{1,0:T(8,128)(2,1)S(1)} %shard_map.25), channel_id=1, source_target_pairs={{0,16},{4,20},{8,24},{12,28},{16,0},{20,4},{24,8},{28,12},{1,17},{... | collective-permute-start | bytes 2506760 | tf_op jit(solution)/shard_map/ppermute | solution.py:17
  64.7 10.8 %collective-permute-start.13 = (f16[512,512]{1,0:T(8,128)(2,1)S(1)}, f16[512,512]{1,0:T(8,128)(2,1)S(1)}, u32[]{:S(2)}, u32[]{:S(2)}) collective-permute-start(f16[512,512]{1,0:T(8,128)(2,1)S(1)} %get-tuple-element.17), channel_id=1, source_target_pairs={{2,0},{6,4},{10,9},{14,13},{17,18},{21,22},{25,27},{29,31}} | collective-permute-start | bytes 1572872 | tf_op jit(solution)/shard_map/ppermute | solution.py:195
  66.0 1.0 copy-start.10
  67.3 19.5 %collective-permute-start.16 = (f16[1024,256]{1,0:T(8,128)(2,1)S(1)}, f16[1024,256]{1,0:T(8,128)(2,1)S(1)}, u32[]{:S(2)}, u32[]{:S(2)}) collective-permute-start(f16[1024,256]{1,0:T(8,128)(2,1)S(1)} %get-tuple-element.15), channel_id=1, source_target_pairs={{2,1},{6,5},{10,8},{14,12},{17,19},{21,23},{25,26},{29,30}} | collective-permute-start | bytes 1572872 | tf_op jit(solution)/shard_map/ppermute | solution.py:195
  75.5 14.1 %collective-permute-start.17 = (f16[1024,256]{1,0:T(8,128)(2,1)S(1)}, f16[1024,256]{1,0:T(8,128)(2,1)S(1)}, u32[]{:S(2)}, u32[]{:S(2)}) collective-permute-start(f16[1024,256]{1,0:T(8,128)(2,1)S(1)} %get-tuple-element.39), channel_id=1, source_target_pairs={{0,1},{3,2},{4,5},{7,6},{9,8},{11,10},{13,12},{15,14},{16,17},{18,... | collective-permute-start | bytes 1572872 | tf_op jit(solution)/shard_map/ppermute | solution.py:190
  76.9 29.0 %collective-permute-start.19 = (f16[1024,256]{1,0:T(8,128)(2,1)S(1)}, f16[1024,256]{1,0:T(8,128)(2,1)S(1)}, u32[]{:S(2)}, u32[]{:S(2)}) collective-permute-start(f16[1024,256]{1,0:T(8,128)(2,1)S(1)} %get-tuple-element.41), channel_id=1, source_target_pairs={{0,1},{3,2},{4,5},{7,6},{8,9},{10,11},{12,13},{14,15},{17,16},{19,... | collective-permute-start | bytes 1572872 | tf_op jit(solution)/shard_map/ppermute | solution.py:190
  82.2 22.6 %collective-permute-start.18 = (f16[1024,256]{1,0:T(8,128)(2,1)S(1)}, f16[1024,256]{1,0:T(8,128)(2,1)S(1)}, u32[]{:S(2)}, u32[]{:S(2)}) collective-permute-start(f16[1024,256]{1,0:T(8,128)(2,1)S(1)} %get-tuple-element.13), channel_id=1, source_target_pairs={{1,2},{5,6},{9,11},{13,15},{18,16},{22,20},{26,25},{30,29}} | collective-permute-start | bytes 1572872 | tf_op jit(solution)/shard_map/ppermute | solution.py:195
  86.8 26.7 %collective-permute-start.21 = (f16[1024,256]{1,0:T(8,128)(2,1)S(1)}, f16[1024,256]{1,0:T(8,128)(2,1)S(1)}, u32[]{:S(2)}, u32[]{:S(2)}) collective-permute-start(f16[1024,256]{1,0:T(8,128)(2,1)S(1)} %get-tuple-element.43), channel_id=1, source_target_pairs={{0,1},{2,3},{4,5},{6,7},{8,9},{11,10},{12,13},{15,14},{16,17},{19,... | collective-permute-start | bytes 1572872 | tf_op jit(solution)/shard_map/ppermute | solution.py:190
  88.2 1.1 copy-start.8
  88.2 1.4 copy-start.11
  89.7 23.6 %collective-permute-start.20 = (f16[1024,256]{1,0:T(8,128)(2,1)S(1)}, f16[1024,256]{1,0:T(8,128)(2,1)S(1)}, u32[]{:S(2)}, u32[]{:S(2)}) collective-permute-start(f16[1024,256]{1,0:T(8,128)(2,1)S(1)} %get-tuple-element.11), channel_id=1, source_target_pairs={{2,1},{6,5},{10,8},{14,12},{17,19},{21,23},{25,26},{29,30}} | collective-permute-start | bytes 1572872 | tf_op jit(solution)/shard_map/ppermute | solution.py:195
  103.5 13.6 %collective-permute-start.23 = (f16[1024,256]{1,0:T(8,128)(2,1)S(1)}, f16[1024,256]{1,0:T(8,128)(2,1)S(1)}, u32[]{:S(2)}, u32[]{:S(2)}) collective-permute-start(f16[1024,256]{1,0:T(8,128)(2,1)S(1)} %get-tuple-element.45), channel_id=1, source_target_pairs={{0,1},{2,3},{4,5},{6,7},{8,9},{11,10},{12,13},{15,14},{16,17},{19,... | collective-permute-start | bytes 1572872 | tf_op jit(solution)/shard_map/ppermute | solution.py:190
  105.0 1.0 copy-start
  106.1 9.8 %collective-permute-start.22 = (f16[1024,256]{1,0:T(8,128)(2,1)S(1)}, f16[1024,256]{1,0:T(8,128)(2,1)S(1)}, u32[]{:S(2)}, u32[]{:S(2)}) collective-permute-start(f16[1024,256]{1,0:T(8,128)(2,1)S(1)} %get-tuple-element.9), channel_id=1, source_target_pairs={{1,2},{5,6},{9,11},{13,15},{18,16},{22,20},{26,25},{30,29}} | collective-permute-start | bytes 1572872 | tf_op jit(solution)/shard_map/ppermute | solution.py:195
  113.4 1.2 copy-start.2
  114.7 18.0 %collective-permute-start.24 = (f16[1024,256]{1,0:T(8,128)(2,1)}, f16[1024,256]{1,0:T(8,128)(2,1)}, u32[]{:S(2)}, u32[]{:S(2)}) collective-permute-start(f16[1024,256]{1,0:T(8,128)(2,1)} %get-tuple-element.7), channel_id=1, source_target_pairs={{1,3},{5,7},{9,10},{13,14},{18,17},{22,21},{26,24},{30,28}} | collective-permute-start | bytes 1572872 | tf_op jit(solution)/shard_map/ppermute | solution.py:195
  116.1 2.0 %copy-start.4 = (f32[1024,256]{1,0:T(8,128)}, f32[1024,256]{1,0:T(8,128)S(1)}, u32[]{:S(2)}) copy-start(f32[1024,256]{1,0:T(8,128)S(1)} %convert_add_fusion.3.refs_1_) | copy-start | bytes 3145732
  118.1 25.7 %collective-permute-start.25 = (f16[1024,256]{1,0:T(8,128)(2,1)}, f16[1024,256]{1,0:T(8,128)(2,1)}, u32[]{:S(2)}, u32[]{:S(2)}) collective-permute-start(f16[1024,256]{1,0:T(8,128)(2,1)} %get-tuple-element.5), channel_id=1, source_target_pairs={{1,3},{5,7},{9,10},{13,14},{18,17},{22,21},{26,24},{30,28}} | collective-permute-start | bytes 1572872 | tf_op jit(solution)/shard_map/ppermute | solution.py:195
  133.8 11.2 %copy-start.5 = (f32[1024,256]{1,0:T(8,128)S(1)}, f32[1024,256]{1,0:T(8,128)}, u32[]{:S(2)}) copy-start(f32[1024,256]{1,0:T(8,128)} %copy-done.4) | copy-start | bytes 3145732
  133.8 11.2 %copy-start.7 = (f32[512,512]{1,0:T(8,128)S(1)}, f32[512,512]{1,0:T(8,128)}, u32[]{:S(2)}) copy-start(f32[512,512]{1,0:T(8,128)} %copy-done.6) | copy-start | bytes 3145732
  133.8 11.2 %copy-start.9 = (f32[1024,256]{1,0:T(8,128)S(1)}, f32[1024,256]{1,0:T(8,128)}, u32[]{:S(2)}) copy-start(f32[1024,256]{1,0:T(8,128)} %copy-done.8) | copy-start | bytes 3145732
  133.8 11.2 %copy-start.1 = (f32[1024,256]{1,0:T(8,128)S(1)}, f32[1024,256]{1,0:T(8,128)}, u32[]{:S(2)}) copy-start(f32[1024,256]{1,0:T(8,128)} %copy-done) | copy-start | bytes 3145732
  133.8 11.2 %copy-start.3 = (f32[1024,256]{1,0:T(8,128)S(1)}, f32[1024,256]{1,0:T(8,128)}, u32[]{:S(2)}) copy-start(f32[1024,256]{1,0:T(8,128)} %copy-done.2) | copy-start | bytes 3145732
  145.7 5.2 %collective-permute-start.26 = (f32[512,512]{1,0:T(8,128)S(1)}, f32[512,512]{1,0:T(8,128)S(1)}, u32[]{:S(2)}, u32[]{:S(2)}) collective-permute-start(f32[512,512]{1,0:T(8,128)S(1)} %maximum_multiply_fusion.1), channel_id=1, source_target_pairs={{0,4},{4,0},{8,12},{12,8},{16,20},{20,16},{24,28},{28,24},{1,5},{5... | collective-permute-start | bytes 3145736 | tf_op jit(solution)/shard_map/ppermute | solution.py:17

commit v3 on v0

v3 whole, which is shorter than its diff:
```python
import math

import jax
import jax.numpy as jnp
from jax import lax
from jax.experimental import pallas as pl
from jax.experimental.pallas import tpu as pltpu
from jax.sharding import PartitionSpec as P

EXTRA = 16
BITS = (32, 16, 8, 4, 2, 1)
CHUNKS = 2
STEPS = 2
AXES = ("proj", "row")
ROWS = {"x": "own", "y": "own"}
EVENTS = (
    ("hop", ("x", 0), 0),
    ("hop", ("own", 0), 0),
    ("hop", ("y", 0), 0),
    ("begin", ("oo", 0), 0),
    ("hop", ("x", 1), 1),
    ("hop", ("y", 1), 1),
    ("begin", ("os", 0), 1),
    ("first", ("oo", 0), 1),
    ("begin", ("x", 0), 1),
    ("begin", ("y", 0), 1),
    ("second", ("oo", 0), 1),
    ("begin", ("x", 1), 1),
    ("begin", ("y", 1), 1),
    ("first", ("os", 0), 1),
    ("begin", ("xy", 0), 1),
    ("first", ("x", 1), 1),
    ("first", ("x", 0), 1),
    ("first", ("y", 0), 1),
    ("first", ("y", 1), 1),
    ("first", ("xy", 0), 1),
    ("second", ("os", 0), 1),
    ("second", ("x", 0), 1),
    ("second", ("y", 0), 1),
    ("second", ("x", 1), 1),
    ("second", ("y", 1), 1),
    ("send", ("y", 0), 1),
    ("send", ("x", 0), 1),
    ("second", ("xy", 0), 1),
    ("wait", ("x", 0), 1),
    ("wait", ("y", 0), 1),
    ("send", ("plain", 0), 1),
    ("send", ("mirror", 0), 0),
)


def hop(x, axis, size, mask):
    return lax.ppermute(x, axis, [(i, i ^ mask) for i in range(size)])


def exponent_up(share):
    e = jnp.zeros_like(share)
    for b in BITS:
        small = share < 2.0 ** (-2 * b)
        e = jnp.where(small, e + b, e)
        share = jnp.where(small, share * 2.0 ** (2 * b), share)
    return e


def power_of_two(e, sign):
    t = jnp.ones_like(e)
    for b in BITS:
        hit = e >= b
        t = jnp.where(hit, t * 2.0 ** (sign * b), t)
        e = jnp.where(hit, e - b, e)
    return t


def column(row):
    return jnp.transpose(jnp.broadcast_to(row, (128, row.shape[1])))[:, :1]


def energy_kernel(x_ref, energy_ref):
    x = x_ref[:, 0, :]
    f = x - jnp.sum(x, axis=1, keepdims=True) * (1.0 / x.shape[1])
    total = jnp.sum(f * f, axis=1, keepdims=True)
    energy_ref[...] = jnp.transpose(jnp.broadcast_to(total, (total.shape[0], 128)))[:1, :]


def norm_kernel(entries, x_ref, *refs):
    energies, (own_ref, e_ref), piece_refs = refs[: -2 - CHUNKS], refs[-2 - CHUNKS : -CHUNKS], refs[-CHUNKS:]
    step, _, columns = x_ref.shape
    i = pl.program_id(0)
    parts = [e[...] for e in energies]
    while len(parts) > 1:
        parts = [a + b for a, b in zip(parts[::2], parts[1::2])]
    power = parts[0] / entries
    e = exponent_up(power / (power + 1e-05))
    up = column(power_of_two(e, 1))
    factor = column(lax.rsqrt(power + 1e-05))
    x = x_ref[:, 0, :]
    f = x - jnp.sum(x, axis=1, keepdims=True) * (1.0 / columns)
    normed = (f * factor * (1.0 / math.sqrt(entries)) * up).astype(jnp.bfloat16)
    own_ref[...] = normed
    e_ref[...] = e
    for q in range(CHUNKS):

        @pl.when(i == q)
        def _(q=q):
            piece_refs[q][:step, :] = normed

    last = slice(step, step + EXTRA)

    @pl.when(i == 0)
    def _():
        piece_refs[-1][last, :] = jnp.zeros((EXTRA, columns), jnp.bfloat16)

    here = pl.ds(pl.multiple_of(i * step, 128), step)
    piece_refs[-1][last, here] = jnp.broadcast_to(e, (EXTRA, step)).astype(jnp.bfloat16)


def normalize(x, nr):
    tile, _, columns = x.shape
    step = tile // CHUNKS
    rows = pl.BlockSpec((step, 1, columns), lambda i: (i, 0, 0))
    line = pl.BlockSpec((1, step), lambda i: (0, i))
    vec = jax.ShapeDtypeStruct((1, tile), jnp.float32)
    energy = pl.pallas_call(energy_kernel, grid=(CHUNKS,), in_specs=[rows], out_specs=line, out_shape=vec)(x)
    parts = [energy] + [hop(energy, "row", nr, d) for d in range(1, nr)]
    sizes = [step] * (CHUNKS - 1) + [step + EXTRA]
    return pl.pallas_call(
        lambda *refs: norm_kernel(columns * nr, *refs),
        grid=(CHUNKS,),
        in_specs=[rows] + [line] * nr,
        out_specs=[pl.BlockSpec((step, columns), lambda i: (i, 0)), line]
        + [pl.BlockSpec((n, columns), lambda i: (0, 0)) for n in sizes],
        out_shape=[jax.ShapeDtypeStruct((tile, columns), jnp.bfloat16), vec]
        + [jax.ShapeDtypeStruct((n, columns), jnp.bfloat16) for n in sizes],
    )(x, *parts)


def gate(x, *others):
    return pl.pallas_call(
        lambda *refs: None,
        in_specs=[pl.BlockSpec(memory_space=pl.ANY)] * (1 + len(others)),
        out_specs=pl.BlockSpec(memory_space=pl.ANY),
        out_shape=jax.ShapeDtypeStruct(x.shape, x.dtype),
        input_output_aliases={0: 0},
        compiler_params=pltpu.CompilerParams(vmem_limit_bytes=1 << 16),
        cost_estimate=pl.CostEstimate(flops=0, bytes_accessed=0, transcendentals=0),
    )(x, *others)


def arrived(x):
    return x[:8, :128].astype(jnp.float32)


def tree(np_, nr, group, k):
    stages = []
    size = 1
    while size < nr:
        pairs = []
        for s in range(np_):
            d = (s // group) ^ k

            def head(g):
                return min(range(g * size, (g + 1) * size), key=lambda i: abs(i - d))

            for g in range(0, nr // size, 2):
                a, b = head(g), head(g + 1)
                if abs(a - d) < abs(b - d):
                    a, b = b, a
                pairs.append((s * nr + a, s * nr + b))
        stages.append(pairs)
        size *= 2
    return stages


def assemble_kernel(place_ref, own_ref, first_e_ref, second_e_ref, first_ref, second_ref, turned_ref, out_ref):
    tile = first_ref.shape[1]
    down = column(power_of_two(own_ref[...], -1))
    first = first_ref[...] * down * power_of_two(first_e_ref[...], -1)
    second = (second_ref[...] + jnp.transpose(turned_ref[...])) * down * power_of_two(second_e_ref[...], -1)
    at = place_ref[0] == 0

    @pl.when(at)
    def _():
        out_ref[:, :tile] = first
        out_ref[:, tile:] = second

    @pl.when(jnp.logical_not(at))
    def _():
        out_ref[:, :tile] = second
        out_ref[:, tile:] = first


def assemble(place, e_own, e_first, e_second, first, second, turned):
    tile = first.shape[0]
    step = tile // STEPS
    line = pl.BlockSpec((1, tile), lambda i: (0, 0))
    rows = pl.BlockSpec((step, tile), lambda i: (i, 0))
    return pl.pallas_call(
        assemble_kernel,
        grid=(STEPS,),
        in_specs=[
            pl.BlockSpec(memory_space=pltpu.SMEM),
            pl.BlockSpec((1, step), lambda i: (0, i)),
            line,
            line,
            rows,
            rows,
            pl.BlockSpec((tile, step), lambda i: (0, i)),
        ],
        out_specs=pl.BlockSpec((step, 2 * tile), lambda i: (i, 0)),
        out_shape=jax.ShapeDtypeStruct((tile, 2 * tile), jnp.float32),
    )(place, e_own, e_first, e_second, first, second, turned)


def product(rows, columns):
    return lax.dot_general(rows, columns, (((1,), (1,)), ((), ())), preferred_element_type=jnp.float32)


def paired(projections):
    tile, _, columns = projections.shape
    np_, nr = lax.axis_size("proj"), lax.axis_size("row")
    p, z = lax.axis_index("proj"), lax.axis_index("row")
    c, h = p // 2, p % 2
    x, y = c % 2, c // 2
    k = c ^ z
    chips = range(np_ // 2)
    half, piece = tile // 2, tile // CHUNKS

    def receive(value, source):
        pairs = []
        for c in chips:
            for h in range(2):
                for z in range(nr):
                    at = source(c, h, z)
                    if at is not None:
                        pairs.append(((2 * at[0] + at[1]) * nr + at[2], (2 * c + h) * nr + z))
        return lax.ppermute(value, AXES, pairs)

    stages = {n: tree(np_, nr, 2, m) for n, m in (("oo", 0), ("os", 0), ("x", 1), ("y", 2))}
    one, two = [], []
    for s in range(np_):
        if s // 2 in (0, nr - 1):
            a, b = [(0, 1), (3, 2)], [(1, 2), (2, 1)]
        else:
            a, b = [(0, 1), (1, 0), (2, 3), (3, 2)], [(1, 3), (2, 0)]
        one += [(s * nr + i, s * nr + j) for i, j in a]
        two += [(s * nr + i, s * nr + j) for i, j in b]
    stages["xy"] = [one, two]

    carry, moving, token = {}, {}, []

    def ordered(value, wait):
        return gate(value, *token) if token and wait else value

    def send(name, stage):
        moving[name] = lax.ppermute(carry[name].astype(jnp.float16), AXES, stages[name[0]][stage])
        token[:] = [carry[name]]

    def begin(name, part):
        carry[name] = part
        send(name, 0)

    def exponents(b):
        return b[b.shape[0] - EXTRA : b.shape[0] - EXTRA + 1, :tile].astype(jnp.float32)

    own, e_own, *pieces = normalize(projections, nr)
    def from_x(c, h, z):
        return c ^ 1, h ^ (c & 1), z

    def from_y(c, h, z):
        return c ^ 2, h ^ (c & 1) ^ (c >> 1), z

    def whole(axis):
        return jnp.concatenate([got[axis, i][:piece] for i in range(CHUNKS)], axis=0)

    def wide(axis):
        return jnp.concatenate([carry[axis, i] for i in range(CHUNKS)], axis=1)

    def message(total, e):
        below = jnp.broadcast_to(ordered(e, wait), (EXTRA, tile))
        return jnp.concatenate([total.astype(jnp.float16), below.astype(jnp.float16)], axis=0)

    got, rows, arrived = {}, {"own": own}, {}
    for kind, name, wait in EVENTS:
        what, i = name
        if kind == "hop":
            if what == "own":
                sibling = hop(ordered(own, wait), "proj", np_, 1)
            else:
                got[name] = receive(ordered(pieces[i], wait), from_x if what == "x" else from_y)
        elif kind == "begin":
            if what == "oo":
                begin(name, product(own, own))
            elif what == "os":
                sibling = ordered(sibling, wait)
                rows["both"] = jnp.concatenate([own, sibling], axis=0)
                begin(name, jnp.where(h == 0, product(own[:half], sibling), product(sibling[half:], own)))
            elif what == "xy":
                begin(name, product(ordered(whole("x"), wait), whole("y")))
            else:
                got[name] = ordered(got[name], wait)
                begin(name, product(rows[ROWS[what]], got[name][:piece]))
        elif kind == "first":
            carry[name] = ordered(carry[name], wait) + moving[name].astype(jnp.float32)
            send(name, 1)
        elif kind == "second":
            carry[name] = ordered(carry[name], wait) + moving[name].astype(jnp.float32)
            token[:] = [carry[name]]
        elif kind == "wait":
            token.append(arrived[what][:8, :128].astype(jnp.float32))
        elif what == "plain":
            arrived[what] = receive(
                message(carry["xy", 0], exponents(got["y", CHUNKS - 1])),
                lambda c, h, z: (c ^ 1, h ^ (c & 1) ^ 1, z) if c ^ z == 3 else None,
            )
        elif what == "mirror":
            arrived[what] = receive(
                message(carry["xy", 0], exponents(got["x", CHUNKS - 1])),
                lambda c, h, z: (c ^ 2, h ^ (c & 1) ^ (c >> 1) ^ 1, z) if c ^ z == 3 else None,
            )
        elif what == "x":
            arrived[what] = receive(
                message(wide("x"), e_own), lambda c, h, z: (c ^ 1, h ^ (c & 1) ^ 1, c) if c ^ z == 1 else None
            )
        elif what == "y":
            arrived[what] = receive(
                message(wide("y"), e_own),
                lambda c, h, z: (c ^ 2, h ^ (c & 1) ^ (c >> 1) ^ 1, c) if c ^ z == 2 else None,
            )

    wide = {a: wide(a) for a in "xy"}
    plain, mirror = arrived["plain"], arrived["mirror"]
    e_x, e_y = exponents(got["x", CHUNKS - 1]), exponents(got["y", CHUNKS - 1])
    pad = jnp.concatenate([carry["os", 0], jnp.broadcast_to(e_own, (half, tile))], axis=0)
    if ROWS == {"x": "own", "y": "own"}:
        other = hop(pad, "proj", np_, 1)
    else:
        sent = {a: wide[a][tile:] * power_of_two(e, -1) if ROWS[a] == "both" else jnp.zeros_like(pad) for a, e in (("x", e_x), ("y", e_y))}
        other = hop(jnp.where(k == 0, pad, jnp.where(k == 1, sent["x"], sent["y"])), "proj", np_, 1)
    zero = jnp.zeros((tile, tile), jnp.float32)
    straight = jnp.where(k == 0, carry["oo", 0], jnp.where(k == 1, wide["x"][:tile], jnp.where(k == 2, wide["y"][:tile], zero)))
    straight = straight + plain[:tile].astype(jnp.float32)
    low, high = jnp.where(h == 0, carry["os", 0], other[:half]), jnp.where(h == 0, other[:half], carry["os", 0])
    cross = jnp.concatenate([low, high], axis=0)
    from_sibling = jnp.zeros_like(k == 0)
    for a, m in (("x", 1), ("y", 2)):
        if ROWS[a] == "both":
            from_sibling = from_sibling | (k == m)
    second = jnp.where(k == 0, jnp.where(h == 0, cross, zero), jnp.where(from_sibling, other, zero))
    turned = jnp.where((k == 0) & (h == 1), cross, zero) + mirror[:tile].astype(jnp.float32)
    e_first = jnp.where(k == 0, e_own, jnp.where(k == 1, e_x, jnp.where(k == 2, e_y, 0.0))) + exponents(plain)
    e_second = jnp.where(k == 0, other[half : half + 1], 0.0) + exponents(mirror)
    for a in "xy":
        if ROWS[a] == "own":
            turned = turned + arrived[a][:tile].astype(jnp.float32)
            e_second = e_second + exponents(arrived[a])
    place = jnp.where(k == 0, h, jnp.where(k == 1, h ^ x, jnp.where(k == 2, h ^ x ^ y, h ^ y)))
    return assemble(place.reshape(1), e_own, e_first, e_second, straight, second, turned)


def plain_plan(projections):
    tile, det_rows, columns = projections.shape
    entries = det_rows * lax.axis_size("row") * columns
    filtered = projections - jnp.mean(projections, axis=2, keepdims=True)
    power = lax.psum(jnp.sum(filtered * filtered, axis=(1, 2)), "row") / entries
    normed = filtered * lax.rsqrt(power + 1e-05)[:, None, None] * (1.0 / math.sqrt(entries))
    own = normed.astype(jnp.bfloat16).reshape(tile, det_rows * columns)
    part = product(own, lax.all_gather(own, "proj", axis=0, tiled=True))
    return lax.psum_scatter(part, "row", scatter_dimension=1, tiled=True)


def solution(mesh):
    fits = mesh.shape["row"] == 4 and mesh.shape["proj"] == 8
    return jax.shard_map(
        paired if fits else plain_plan,
        mesh=mesh,
        in_specs=(P("proj", "row", None),),
        out_specs=P("proj", "row"),
        check_vma=False,
    )
```

time: 261 us -> 145 us (0.56)
  waiting for transfers between devices: 219 us -> 67.2 us
  starting transfers between devices: 0.04 us -> 43 us
  between operations: 13.4 us -> 0.82 us
  Pallas kernels: 0 us -> 10.8 us
  blocking collectives: 7.26 us -> 0 us
  other arithmetic: 6.33 us -> 12.3 us
  matrix products: 12.1 us -> 7.52 us
    reduce_scatter x1 -> x0, waiting for transfers between devices: 144 us -> none  [per_device(): return lax.psum_scatter(product, 'row', scatter_dimension=1, tiled=True)]
    all_gather x1 -> x0, waiting for transfers between devices: 74.9 us -> none  [per_device(): lax.all_gather(flattened, 'proj', axis=0, tiled=True)]
    ppermute x0 -> x27, waiting for transfers between devices: none -> 67.2 us  [the longest x14 34.7 us: send(): lax.ppermute(carry[name].astype(jnp.float16), AXES, stages[name[0]][stage])]
    ppermute x0 -> x27, starting transfers between devices: none -> 43 us  [the longest x14 23.1 us: send(): lax.ppermute(carry[name].astype(jnp.float16), AXES, stages[name[0]][stage])]
    pallas_call x0 -> x26, Pallas kernels: none -> 10.8 us  [the longest x1 4.37 us: normalize(): pl.pallas_call(lambda *refs: norm_kernel(columns * nr, *refs), grid=(CHUN...]
    add x0 -> x10, other arithmetic: none -> 7.3 us  [the longest x1 2.45 us: paired(): straight = straight + plain[:tile].astype(jnp.float32)]
    psum x1 -> x0, blocking collectives: 7.26 us -> none  [per_device(): energy = lax.psum(jnp.sum(filtered * filtered, axis=(1, 2)), 'row')]
    reduce_sum x2 -> x0, other arithmetic: 4.7 us -> none  [the longest x1 4.25 us: per_device(): filtered = projections - jnp.mean(projections, axis=2, keepdims=True)]
  transfers between devices with their start and end apart: 2 -> 27, of which waited for: 2 -> 9; matrix products, arithmetic and copies ran while one was open for 0% -> 12% of each run, Pallas kernels for 0% -> 0%
where the time goes in v3:
time: 145 us; the launch traced here: 142 us
  waiting for transfers between devices  67.2 us (46%)
  starting transfers between devices  43 us (30%)
  other arithmetic  12.3 us (8%)
  Pallas kernels  10.8 us (7%)
  matrix products  7.52 us (5%)
    ppermute x14, waiting for transfers between devices, send(): lax.ppermute(carry[name].astype(jnp.float16), AXES, stages[name[0]][stage])  34.7 us
    ppermute x8, waiting for transfers between devices, receive(): return lax.ppermute(value, AXES, pairs)  29.7 us
    ppermute x14, starting transfers between devices, send(): lax.ppermute(carry[name].astype(jnp.float16), AXES, stages[name[0]][stage])  23.1 us
    ppermute x5, starting transfers between devices, hop(): return lax.ppermute(x, axis, [(i, i ^ mask) for i in range(size)])  12.3 us
    ppermute x8, starting transfers between devices, receive(): return lax.ppermute(value, AXES, pairs)  7.61 us
    dot_general x8, matrix products, product(): lax.dot_general(rows, columns, (((1,), (1,)), ((), ())), preferred_elemen...  7.52 us
    pallas_call x1, Pallas kernels, normalize(): pl.pallas_call(lambda *refs: norm_kernel(columns * nr, *refs), grid=(CHUN...  4.37 us
    pallas_call x1, Pallas kernels, assemble(): pl.pallas_call(assemble_kernel, grid=(STEPS,), in_specs=[pl.BlockSpec(mem...  3.23 us
  transfers between devices with their start and end apart: 27, of which 9 were waited for; matrix products, arithmetic and copies ran while one was open for 12% of the time, Pallas kernels for 0%

profile of v3, /device:TPU:13, one launch (start us, length us, event | category | flops | bytes accessed | tf_op | source)
XLA Modules:
  0.0 142.4 jit_solution(12384147467587565885)
XLA Ops:
  0.0 3.1 %shard_map.17.refs_1_ = f32[1,512]{1,0:T(1,128)} custom-call(f32[512,1,1536]{2,1,0:T(1,128)} %refs_0_.1), custom_call_target="tpu_custom_call" | custom-call | tf_op jit(solution)/shard_map/pallas_call | solution.py:123
  3.3 2.3 %collective-permute-start.1 = (f32[1,512]{1,0:T(1,128)}, f32[1,512]{1,0:T(1,128)S(1)}, u32[]{:S(2)}, u32[]{:S(2)}) collective-permute-start(f32[1,512]{1,0:T(1,128)} %shard_map.17.refs_1_), channel_id=1, source_target_pairs={{0,2},{1,3},{2,0},{3,1},{4,6},{5,7},{6,4},{7,5},{8,10},{9,11},{10,... | collective-permute-start | bytes 6152 | tf_op jit(solution)/shard_map/ppermute | solution.py:53
  5.8 1.1 collective-permute-done.1.refs_3_
  6.9 1.7 %collective-permute-done.2.refs_4_ = f32[1,512]{1,0:T(1,128)S(1)} collective-permute-done((f32[1,512]{1,0:T(1,128)}, f32[1,512]{1,0:T(1,128)S(1)}, u32[]{:S(2)}, u32[]{:S(2)}) %collective-permute-start.2) | collective-permute-done | bytes 2080 | tf_op jit(solution)/shard_map/ppermute | solution.py:53
  9.1 4.4 %shard_map.18 = (bf16[512,1536]{1,0:T(8,128)(2,1)}, f32[1,512]{1,0:T(1,128)}, bf16[256,1536]{1,0:T(8,128)(2,1)}, bf16[272,1536]{1,0:T(8,128)(2,1)}) custom-call(f32[512,1,1536]{2,1,0:T(1,128)} %refs_0_.1, f32[1,512]{1,0:T(1,128)} %shard_map.17.refs_1_, f32[1,512]{1,0:T(1,128)} %copy-done.11, f32[1,512]{1,0:T(1,128)} %copy-done.12, f32[1,512]{1,0:T(1,128)} %copy-done.13), custom_call_target="tpu_custom_call" | custom-call | tf_op jit(solution)/shard_map/pallas_call | solution.py:126
  13.5 2.2 %collective-permute-start.4 = (bf16[512,1536]{1,0:T(8,128)(2,1)}, bf16[512,1536]{1,0:T(8,128)(2,1)S(1)}, u32[]{:S(2)}, u32[]{:S(2)}) collective-permute-start(bf16[512,1536]{1,0:T(8,128)(2,1)} %get-tuple-element.11), channel_id=1, source_target_pairs={{0,4},{4,0},{8,12},{12,8},{16,20},{20,16},{24,28},{28,24},{1,5},{5... | collective-permute-start | bytes 4718600 | tf_op jit(solution)/shard_map/ppermute | solution.py:53
  15.6 1.2 collective-permute-start.7
  17.1 2.9 %fusion.26 = (f16[512,512]{1,0:T(8,128)(2,1)S(1)}, f32[512,512]{1,0:T(8,128)S(1)}) fusion(bf16[512,1536]{1,0:T(8,128)(2,1)} %get-tuple-element.11), kind=kOutput, calls=%fused_computation.70 | convolution fusion | flops 805568512 | bytes 3145728 | tf_op jit(solution)/shard_map/dot_general | solution.py:215
  20.0 0.6 collective-permute-start.3
  20.6 1.5 %collective-permute-start.9 = (bf16[272,1536]{1,0:T(8,128)(2,1)S(1)}, bf16[272,1536]{1,0:T(8,128)(2,1)S(1)}, u32[]{:S(2)}, u32[]{:S(2)}) collective-permute-start(bf16[272,1536]{1,0:T(8,128)(2,1)S(1)} %shard_map.19), channel_id=1, source_target_pairs={{16,0},{17,1},{18,2},{19,3},{20,4},{21,5},{22,6},{23,7},{28,8},{29... | collective-permute-start | bytes 2506760 | tf_op jit(solution)/shard_map/ppermute | solution.py:236
  22.1 1.4 collective-permute-start.5
  24.8 14.0 %collective-permute-done.5 = f16[512,512]{1,0:T(8,128)(2,1)S(1)} collective-permute-done((f16[512,512]{1,0:T(8,128)(2,1)S(1)}, f16[512,512]{1,0:T(8,128)(2,1)S(1)}, u32[]{:S(2)}, u32[]{:S(2)}) %collective-permute-start.5) | collective-permute-done | bytes 524320 | tf_op jit(solution)/shard_map/ppermute | solution.py:255
  39.0 2.0 %collective-permute-start.8 = (f16[512,512]{1,0:T(8,128)(2,1)S(1)}, f16[512,512]{1,0:T(8,128)(2,1)S(1)}, u32[]{:S(2)}, u32[]{:S(2)}) collective-permute-start(f16[512,512]{1,0:T(8,128)(2,1)S(1)} %get-tuple-element.27), channel_id=1, source_target_pairs={{2,0},{6,4},{10,9},{14,13},{17,18},{21,22},{25,27},{29,31}} | collective-permute-start | bytes 1572872 | tf_op jit(solution)/shard_map/ppermute | solution.py:255
  41.0 0.6 fusion.29
  41.6 0.6 fusion.30
  42.2 1.3 collective-permute-start.10
  43.5 1.3 collective-permute-start.12
  44.8 6.3 %collective-permute-done.8 = f16[512,512]{1,0:T(8,128)(2,1)S(1)} collective-permute-done((f16[512,512]{1,0:T(8,128)(2,1)S(1)}, f16[512,512]{1,0:T(8,128)(2,1)S(1)}, u32[]{:S(2)}, u32[]{:S(2)}) %collective-permute-start.8) | collective-permute-done | bytes 524320 | tf_op jit(solution)/shard_map/ppermute | solution.py:255
  51.2 1.3 collective-permute-start.13
  52.9 0.6 fusion.28
  53.5 1.3 collective-permute-done.9.refs_0_
  54.8 0.6 fusion.31
  55.5 1.3 collective-permute-start.11
  57.0 1.0 fusion.32
  58.1 5.0 %collective-permute-start.14 = (f16[512,256]{1,0:T(8,128)(2,1)S(1)}, f16[512,256]{1,0:T(8,128)(2,1)S(1)}, u32[]{:S(2)}, u32[]{:S(2)}) collective-permute-start(f16[512,256]{1,0:T(8,128)(2,1)S(1)} %get-tuple-element.47), channel_id=1, source_target_pairs={{0,1},{3,2},{4,5},{7,6},{8,9},{10,11},{12,13},{14,15},{17,16},{19,... | collective-permute-start | bytes 786440 | tf_op jit(solution)/shard_map/ppermute | solution.py:255
  63.1 1.9 %collective-permute-start.15 = (f16[512,512]{1,0:T(8,128)(2,1)S(1)}, f16[512,512]{1,0:T(8,128)(2,1)S(1)}, u32[]{:S(2)}, u32[]{:S(2)}) collective-permute-start(f16[512,512]{1,0:T(8,128)(2,1)S(1)} %get-tuple-element.49), channel_id=1, source_target_pairs={{0,1},{3,2},{4,5},{7,6},{8,9},{9,8},{10,11},{11,10},{12,13},{13,12... | collective-permute-start | bytes 1572872 | tf_op jit(solution)/shard_map/ppermute | solution.py:255
  65.0 1.4 collective-permute-done.11
  66.4 2.3 %collective-permute-start.16 = (f16[256,512]{1,0:T(8,128)(2,1)S(1)}, f16[256,512]{1,0:T(8,128)(2,1)S(1)}, u32[]{:S(2)}, u32[]{:S(2)}) collective-permute-start(f16[256,512]{1,0:T(8,128)(2,1)S(1)} %get-tuple-element.25), channel_id=1, source_target_pairs={{2,0},{6,4},{10,9},{14,13},{17,18},{21,22},{25,27},{29,31}} | collective-permute-start | bytes 786440 | tf_op jit(solution)/shard_map/ppermute | solution.py:255
  69.2 1.3 collective-permute-start.17
  70.5 0.7 collective-permute-start.18
  71.2 1.3 collective-permute-start.19
  72.5 13.0 %collective-permute-done.15 = f16[512,512]{1,0:T(8,128)(2,1)S(1)} collective-permute-done((f16[512,512]{1,0:T(8,128)(2,1)S(1)}, f16[512,512]{1,0:T(8,128)(2,1)S(1)}, u32[]{:S(2)}, u32[]{:S(2)}) %collective-permute-start.15) | collective-permute-done | bytes 524320 | tf_op jit(solution)/shard_map/ppermute | solution.py:255
  85.5 0.7 collective-permute-start.20
  86.8 1.3 collective-permute-start.21
  88.7 0.7 collective-permute-start.23
  89.4 0.7 collective-permute-start.22
  90.2 1.0 pad_maximum_fusion.3
  91.2 7.5 %collective-permute-start.25 = (f32[512,512]{1,0:T(8,128)}, f32[512,512]{1,0:T(8,128)}, u32[]{:S(2)}, u32[]{:S(2)}) collective-permute-start(f32[512,512]{1,0:T(8,128)} %pad_maximum_fusion.3), channel_id=1, source_target_pairs={{0,4},{4,0},{8,12},{12,8},{16,20},{20,16},{24,28},{28,24},{1,5},{5... | collective-permute-start | bytes 3145736 | tf_op jit(solution)/shard_map/ppermute | solution.py:53
  99.0 1.3 pad_maximum_fusion.8
  100.3 1.3 collective-permute-start.24
  101.7 1.4 collective-permute-start.26
  103.1 1.1 slice_select_fusion.1
  104.3 28.1 %collective-permute-done.24 = f16[528,512]{1,0:T(8,128)(2,1)} collective-permute-done((f16[528,512]{1,0:T(8,128)(2,1)}, f16[528,512]{1,0:T(8,128)(2,1)}, u32[]{:S(2)}, u32[]{:S(2)}) %collective-permute-start.24) | collective-permute-done | bytes 540704 | tf_op jit(solution)/shard_map/ppermute | solution.py:236
  132.4 1.3 fusion.9.first_e_ref
  133.7 2.5 %convert_add_fusion.1.first_ref = f32[512,512]{1,0:T(8,128)} fusion(f32[512,512]{1,0:T(8,128)S(1)} %convert_add_fusion.4.refs_1_, f32[512,256]{1,0:T(8,128)S(1)} %convert_add_fusion.6.refs_1_, f32[512,256]{1,0:T(8,128)S(1)} %convert_add_fusion.8.refs_1_, f32[512,256]{1,0:T(8,128)S(1)} %copy-done.1, f32[512,256]{1,0:T(8,128)S(1)} %convert_add_fusion.9.refs_1_, ...), kind=kLoop, calls=%fused_computation.12 | loop fusion | flops 1835008 | bytes 4718595 | tf_op jit(solution)/shard_map/add | solution.py:341
  136.2 1.3 fusion.12.second_e_ref
  137.5 1.7 %convert_add_fusion = (f32[512,512]{1,0:T(8,128)}, f32[512,512]{1,0:T(8,128)}) fusion(f32[256,512]{1,0:T(8,128)S(1)} %get-tuple-element.30, f32[256,512]{1,0:T(8,128)S(1)} %get-tuple-element.29, f16[528,512]{1,0:T(8,128)(2,1)S(1)} %copy-done.7, f16[528,512]{1,0:T(8,128)(2,1)S(1)} %copy-done.9, f16[528,512]{1,0:T(8,128)(2,1)S(1)} %collective-permute-done.26, ...), kind=kLoop, calls=%fused_computation.10 | loop fusion | flops 2621440 | bytes 4718595 | tf_op jit(solution)/shard_map/add | solution.py:354
  139.2 3.2 %shard_map.42 = f32[512,1024]{1,0:T(8,128)} custom-call(s32[1]{0:T(128)} %bitcast.place_ref, f32[1,512]{1,0:T(1,128)} %get-tuple-element.9.own_ref, f32[1,512]{1,0:T(1,128)} %fusion.9.first_e_ref, f32[1,512]{1,0:T(1,128)} %fusion.12.second_e_ref, f32[512,512]{1,0:T(8,128)} %convert_add_fusion.1.first_ref, f32[512,512]{1,0:T(8,128)} %get-tuple-element.32.second_ref, ...), custom_call_target="tpu_custom_call" | custom-call | tf_op jit(solution)/shard_map/pallas_call | solution.py:197
  (106 shorter events, 5.0 us)
Async XLA Ops:
  3.1 2.7 %collective-permute-start = (f32[1,512]{1,0:T(1,128)}, f32[1,512]{1,0:T(1,128)S(1)}, u32[]{:S(2)}, u32[]{:S(2)}) collective-permute-start(f32[1,512]{1,0:T(1,128)} %shard_map.17.refs_1_), channel_id=1, source_target_pairs={{0,1},{1,0},{2,3},{3,2},{4,5},{5,4},{6,7},{7,6},{8,9},{9,8},{10,11... | collective-permute-start | bytes 6152 | tf_op jit(solution)/shard_map/ppermute | solution.py:53
  3.3 3.6 %collective-permute-start.1 = (f32[1,512]{1,0:T(1,128)}, f32[1,512]{1,0:T(1,128)S(1)}, u32[]{:S(2)}, u32[]{:S(2)}) collective-permute-start(f32[1,512]{1,0:T(1,128)} %shard_map.17.refs_1_), channel_id=1, source_target_pairs={{0,2},{1,3},{2,0},{3,1},{4,6},{5,7},{6,4},{7,5},{8,10},{9,11},{10,... | collective-permute-start | bytes 6152 | tf_op jit(solution)/shard_map/ppermute | solution.py:53
  5.6 2.9 %collective-permute-start.2 = (f32[1,512]{1,0:T(1,128)}, f32[1,512]{1,0:T(1,128)S(1)}, u32[]{:S(2)}, u32[]{:S(2)}) collective-permute-start(f32[1,512]{1,0:T(1,128)} %shard_map.17.refs_1_), channel_id=1, source_target_pairs={{0,3},{1,2},{2,1},{3,0},{4,7},{5,6},{6,5},{7,4},{8,11},{9,10},{10,... | collective-permute-start | bytes 6152 | tf_op jit(solution)/shard_map/ppermute | solution.py:53
  5.8 2.8 %copy-start.11 = (f32[1,512]{1,0:T(1,128)}, f32[1,512]{1,0:T(1,128)S(1)}, u32[]{:S(2)}) copy-start(f32[1,512]{1,0:T(1,128)S(1)} %collective-permute-done.refs_2_) | copy-start | bytes 6148
  6.9 1.7 %copy-start.12 = (f32[1,512]{1,0:T(1,128)}, f32[1,512]{1,0:T(1,128)S(1)}, u32[]{:S(2)}) copy-start(f32[1,512]{1,0:T(1,128)S(1)} %collective-permute-done.1.refs_3_) | copy-start | bytes 6148
  8.6 0.5 copy-start.13
  13.5 8.6 %collective-permute-start.4 = (bf16[512,1536]{1,0:T(8,128)(2,1)}, bf16[512,1536]{1,0:T(8,128)(2,1)S(1)}, u32[]{:S(2)}, u32[]{:S(2)}) collective-permute-start(bf16[512,1536]{1,0:T(8,128)(2,1)} %get-tuple-element.11), channel_id=1, source_target_pairs={{0,4},{4,0},{8,12},{12,8},{16,20},{20,16},{24,28},{28,24},{1,5},{5... | collective-permute-start | bytes 4718600 | tf_op jit(solution)/shard_map/ppermute | solution.py:53
  15.6 4.3 %copy-start.4 = (bf16[272,1536]{1,0:T(8,128)(2,1)S(1)}, bf16[272,1536]{1,0:T(8,128)(2,1)}, u32[]{:S(2)}) copy-start(bf16[272,1536]{1,0:T(8,128)(2,1)} %get-tuple-element.10.refs_0_) | copy-start | bytes 2506756
  15.6 25.3 %collective-permute-start.7 = (bf16[256,1536]{1,0:T(8,128)(2,1)}, bf16[256,1536]{1,0:T(8,128)(2,1)S(1)}, u32[]{:S(2)}, u32[]{:S(2)}) collective-permute-start(bf16[256,1536]{1,0:T(8,128)(2,1)} %get-tuple-element.12), channel_id=1, source_target_pairs={{8,0},{9,1},{10,2},{11,3},{12,4},{13,5},{14,6},{15,7},{4,8},{5,9},... | collective-permute-start | bytes 2359304 | tf_op jit(solution)/shard_map/ppermute | solution.py:236
  16.8 24.8 %collective-permute-start.6 = (bf16[256,1536]{1,0:T(8,128)(2,1)}, bf16[256,1536]{1,0:T(8,128)(2,1)S(1)}, u32[]{:S(2)}, u32[]{:S(2)}) collective-permute-start(bf16[256,1536]{1,0:T(8,128)(2,1)} %get-tuple-element.12), channel_id=1, source_target_pairs={{16,0},{17,1},{18,2},{19,3},{20,4},{21,5},{22,6},{23,7},{28,8},{29... | collective-permute-start | bytes 2359304 | tf_op jit(solution)/shard_map/ppermute | solution.py:236
  19.9 2.1 %copy-start.10 = (f32[1,512]{1,0:T(1,128)S(1)}, f32[1,512]{1,0:T(1,128)}, u32[]{:S(2)}) copy-start(f32[1,512]{1,0:T(1,128)} %get-tuple-element.9.own_ref) | copy-start | bytes 6148
  20.0 32.9 %collective-permute-start.3 = (bf16[272,1536]{1,0:T(8,128)(2,1)S(1)}, bf16[272,1536]{1,0:T(8,128)(2,1)S(1)}, u32[]{:S(2)}, u32[]{:S(2)}) collective-permute-start(bf16[272,1536]{1,0:T(8,128)(2,1)S(1)} %shard_map.19), channel_id=1, source_target_pairs={{8,0},{9,1},{10,2},{11,3},{12,4},{13,5},{14,6},{15,7},{4,8},{5,9},... | collective-permute-start | bytes 2506760 | tf_op jit(solution)/shard_map/ppermute | solution.py:236
  20.6 34.2 %collective-permute-start.9 = (bf16[272,1536]{1,0:T(8,128)(2,1)S(1)}, bf16[272,1536]{1,0:T(8,128)(2,1)S(1)}, u32[]{:S(2)}, u32[]{:S(2)}) collective-permute-start(bf16[272,1536]{1,0:T(8,128)(2,1)S(1)} %shard_map.19), channel_id=1, source_target_pairs={{16,0},{17,1},{18,2},{19,3},{20,4},{21,5},{22,6},{23,7},{28,8},{29... | collective-permute-start | bytes 2506760 | tf_op jit(solution)/shard_map/ppermute | solution.py:236
  22.1 1.5 %copy-start.5 = (bf16[512,1536]{1,0:T(8,128)(2,1)S(1)}, bf16[512,1536]{1,0:T(8,128)(2,1)}, u32[]{:S(2)}) copy-start(bf16[512,1536]{1,0:T(8,128)(2,1)} %get-tuple-element.11) | copy-start | bytes 4718596
  22.1 16.6 %collective-permute-start.5 = (f16[512,512]{1,0:T(8,128)(2,1)S(1)}, f16[512,512]{1,0:T(8,128)(2,1)S(1)}, u32[]{:S(2)}, u32[]{:S(2)}) collective-permute-start(f16[512,512]{1,0:T(8,128)(2,1)S(1)} %get-tuple-element.37), channel_id=1, source_target_pairs={{1,0},{3,2},{5,4},{7,6},{8,9},{11,10},{12,13},{15,14},{16,17},{19,... | collective-permute-start | bytes 1572872 | tf_op jit(solution)/shard_map/ppermute | solution.py:255
  39.0 12.2 %collective-permute-start.8 = (f16[512,512]{1,0:T(8,128)(2,1)S(1)}, f16[512,512]{1,0:T(8,128)(2,1)S(1)}, u32[]{:S(2)}, u32[]{:S(2)}) collective-permute-start(f16[512,512]{1,0:T(8,128)(2,1)S(1)} %get-tuple-element.27), channel_id=1, source_target_pairs={{2,0},{6,4},{10,9},{14,13},{17,18},{21,22},{25,27},{29,31}} | collective-permute-start | bytes 1572872 | tf_op jit(solution)/shard_map/ppermute | solution.py:255
  42.2 14.7 %collective-permute-start.10 = (f16[256,512]{1,0:T(8,128)(2,1)S(1)}, f16[256,512]{1,0:T(8,128)(2,1)S(1)}, u32[]{:S(2)}, u32[]{:S(2)}) collective-permute-start(f16[256,512]{1,0:T(8,128)(2,1)S(1)} %get-tuple-element.39), channel_id=1, source_target_pairs={{1,0},{3,2},{5,4},{7,6},{8,9},{11,10},{12,13},{15,14},{16,17},{19,... | collective-permute-start | bytes 786440 | tf_op jit(solution)/shard_map/ppermute | solution.py:255
  43.5 25.3 %collective-permute-start.12 = (f16[512,256]{1,0:T(8,128)(2,1)S(1)}, f16[512,256]{1,0:T(8,128)(2,1)S(1)}, u32[]{:S(2)}, u32[]{:S(2)}) collective-permute-start(f16[512,256]{1,0:T(8,128)(2,1)S(1)} %get-tuple-element.43), channel_id=1, source_target_pairs={{0,1},{3,2},{4,5},{7,6},{9,8},{11,10},{13,12},{15,14},{16,17},{18,... | collective-permute-start | bytes 786440 | tf_op jit(solution)/shard_map/ppermute | solution.py:255
  51.2 17.8 %collective-permute-start.13 = (f16[512,256]{1,0:T(8,128)(2,1)S(1)}, f16[512,256]{1,0:T(8,128)(2,1)S(1)}, u32[]{:S(2)}, u32[]{:S(2)}) collective-permute-start(f16[512,256]{1,0:T(8,128)(2,1)S(1)} %get-tuple-element.45), channel_id=1, source_target_pairs={{0,1},{3,2},{4,5},{7,6},{8,9},{10,11},{12,13},{14,15},{17,16},{19,... | collective-permute-start | bytes 786440 | tf_op jit(solution)/shard_map/ppermute | solution.py:255
  52.9 36.5 %copy-start.3 = (bf16[272,1536]{1,0:T(8,128)(2,1)}, bf16[272,1536]{1,0:T(8,128)(2,1)S(1)}, u32[]{:S(2)}) copy-start(bf16[272,1536]{1,0:T(8,128)(2,1)S(1)} %shard_map.25) | copy-start | bytes 2506756
  54.8 10.2 %copy-start.2 = (bf16[272,1536]{1,0:T(8,128)(2,1)}, bf16[272,1536]{1,0:T(8,128)(2,1)S(1)}, u32[]{:S(2)}) copy-start(bf16[272,1536]{1,0:T(8,128)(2,1)S(1)} %shard_map.26) | copy-start | bytes 2506756
  55.5 10.9 %collective-permute-start.11 = (f16[512,256]{1,0:T(8,128)(2,1)S(1)}, f16[512,256]{1,0:T(8,128)(2,1)S(1)}, u32[]{:S(2)}, u32[]{:S(2)}) collective-permute-start(f16[512,256]{1,0:T(8,128)(2,1)S(1)} %get-tuple-element.41), channel_id=1, source_target_pairs={{0,1},{3,2},{4,5},{7,6},{9,8},{11,10},{13,12},{15,14},{16,17},{18,... | collective-permute-start | bytes 786440 | tf_op jit(solution)/shard_map/ppermute | solution.py:255
  58.1 11.0 %collective-permute-start.14 = (f16[512,256]{1,0:T(8,128)(2,1)S(1)}, f16[512,256]{1,0:T(8,128)(2,1)S(1)}, u32[]{:S(2)}, u32[]{:S(2)}) collective-permute-start(f16[512,256]{1,0:T(8,128)(2,1)S(1)} %get-tuple-element.47), channel_id=1, source_target_pairs={{0,1},{3,2},{4,5},{7,6},{8,9},{10,11},{12,13},{14,15},{17,16},{19,... | collective-permute-start | bytes 786440 | tf_op jit(solution)/shard_map/ppermute | solution.py:255
  63.1 22.4 %collective-permute-start.15 = (f16[512,512]{1,0:T(8,128)(2,1)S(1)}, f16[512,512]{1,0:T(8,128)(2,1)S(1)}, u32[]{:S(2)}, u32[]{:S(2)}) collective-permute-start(f16[512,512]{1,0:T(8,128)(2,1)S(1)} %get-tuple-element.49), channel_id=1, source_target_pairs={{0,1},{3,2},{4,5},{7,6},{8,9},{9,8},{10,11},{11,10},{12,13},{13,12... | collective-permute-start | bytes 1572872 | tf_op jit(solution)/shard_map/ppermute | solution.py:255
  66.4 20.0 %collective-permute-start.16 = (f16[256,512]{1,0:T(8,128)(2,1)S(1)}, f16[256,512]{1,0:T(8,128)(2,1)S(1)}, u32[]{:S(2)}, u32[]{:S(2)}) collective-permute-start(f16[256,512]{1,0:T(8,128)(2,1)S(1)} %get-tuple-element.25), channel_id=1, source_target_pairs={{2,0},{6,4},{10,9},{14,13},{17,18},{21,22},{25,27},{29,31}} | collective-permute-start | bytes 786440 | tf_op jit(solution)/shard_map/ppermute | solution.py:255
  69.2 17.3 %collective-permute-start.17 = (f16[512,256]{1,0:T(8,128)(2,1)S(1)}, f16[512,256]{1,0:T(8,128)(2,1)S(1)}, u32[]{:S(2)}, u32[]{:S(2)}) collective-permute-start(f16[512,256]{1,0:T(8,128)(2,1)S(1)} %get-tuple-element.23), channel_id=1, source_target_pairs={{2,1},{6,5},{10,8},{14,12},{17,19},{21,23},{25,26},{29,30}} | collective-permute-start | bytes 786440 | tf_op jit(solution)/shard_map/ppermute | solution.py:255
  70.5 16.1 %collective-permute-start.18 = (f16[512,256]{1,0:T(8,128)(2,1)S(1)}, f16[512,256]{1,0:T(8,128)(2,1)S(1)}, u32[]{:S(2)}, u32[]{:S(2)}) collective-permute-start(f16[512,256]{1,0:T(8,128)(2,1)S(1)} %get-tuple-element.21), channel_id=1, source_target_pairs={{1,2},{5,6},{9,11},{13,15},{18,16},{22,20},{26,25},{30,29}} | collective-permute-start | bytes 786440 | tf_op jit(solution)/shard_map/ppermute | solution.py:255
  71.2 15.5 %collective-permute-start.19 = (f16[512,256]{1,0:T(8,128)(2,1)S(1)}, f16[512,256]{1,0:T(8,128)(2,1)S(1)}, u32[]{:S(2)}, u32[]{:S(2)}) collective-permute-start(f16[512,256]{1,0:T(8,128)(2,1)S(1)} %get-tuple-element.19), channel_id=1, source_target_pairs={{2,1},{6,5},{10,8},{14,12},{17,19},{21,23},{25,26},{29,30}} | collective-permute-start | bytes 786440 | tf_op jit(solution)/shard_map/ppermute | solution.py:255
  85.5 2.7 %collective-permute-start.20 = (f16[512,256]{1,0:T(8,128)(2,1)S(1)}, f16[512,256]{1,0:T(8,128)(2,1)S(1)}, u32[]{:S(2)}, u32[]{:S(2)}) collective-permute-start(f16[512,256]{1,0:T(8,128)(2,1)S(1)} %get-tuple-element.17), channel_id=1, source_target_pairs={{1,2},{5,6},{9,11},{13,15},{18,16},{22,20},{26,25},{30,29}} | collective-permute-start | bytes 786440 | tf_op jit(solution)/shard_map/ppermute | solution.py:255
  86.8 1.4 %copy-start = (f32[512,256]{1,0:T(8,128)}, f32[512,256]{1,0:T(8,128)S(1)}, u32[]{:S(2)}) copy-start(f32[512,256]{1,0:T(8,128)S(1)} %convert_add_fusion.7.refs_1_) | copy-start | bytes 1572868
  86.8 11.9 %collective-permute-start.21 = (f16[512,512]{1,0:T(8,128)(2,1)S(1)}, f16[512,512]{1,0:T(8,128)(2,1)S(1)}, u32[]{:S(2)}, u32[]{:S(2)}) collective-permute-start(f16[512,512]{1,0:T(8,128)(2,1)S(1)} %get-tuple-element.15), channel_id=1, source_target_pairs={{1,2},{2,1},{5,6},{6,5},{9,11},{10,8},{13,15},{14,12},{17,19},{18,... | collective-permute-start | bytes 1572872 | tf_op jit(solution)/shard_map/ppermute | solution.py:255
  88.7 10.3 %collective-permute-start.23 = (f16[528,512]{1,0:T(8,128)(2,1)S(1)}, f16[528,512]{1,0:T(8,128)(2,1)S(1)}, u32[]{:S(2)}, u32[]{:S(2)}) collective-permute-start(f16[528,512]{1,0:T(8,128)(2,1)S(1)} %get-tuple-element.35), channel_id=1, source_target_pairs={{20,2},{16,6},{25,11},{29,15},{2,16},{6,20},{15,25},{11,29}} | collective-permute-start | bytes 1622024 | tf_op jit(solution)/shard_map/ppermute | solution.py:236
  89.4 9.5 %collective-permute-start.22 = (f16[528,512]{1,0:T(8,128)(2,1)S(1)}, f16[528,512]{1,0:T(8,128)(2,1)S(1)}, u32[]{:S(2)}, u32[]{:S(2)}) collective-permute-start(f16[528,512]{1,0:T(8,128)(2,1)S(1)} %get-tuple-element.36), channel_id=1, source_target_pairs={{12,1},{8,5},{1,8},{5,12},{30,19},{26,23},{19,26},{23,30}} | collective-permute-start | bytes 1622024 | tf_op jit(solution)/shard_map/ppermute | solution.py:236
  91.2 11.9 %collective-permute-start.25 = (f32[512,512]{1,0:T(8,128)}, f32[512,512]{1,0:T(8,128)}, u32[]{:S(2)}, u32[]{:S(2)}) collective-permute-start(f32[512,512]{1,0:T(8,128)} %pad_maximum_fusion.3), channel_id=1, source_target_pairs={{0,4},{4,0},{8,12},{12,8},{16,20},{20,16},{24,28},{28,24},{1,5},{5... | collective-permute-start | bytes 3145736 | tf_op jit(solution)/shard_map/ppermute | solution.py:53
  98.9 1.4 copy-start.6
  99.0 1.3 copy-start.8
  100.3 32.1 %collective-permute-start.24 = (f16[528,512]{1,0:T(8,128)(2,1)}, f16[528,512]{1,0:T(8,128)(2,1)}, u32[]{:S(2)}, u32[]{:S(2)}) collective-permute-start(f16[528,512]{1,0:T(8,128)(2,1)} %get-tuple-element.34), channel_id=1, source_target_pairs={{15,3},{11,7},{2,10},{6,14},{29,17},{25,21},{16,24},{20,28}} | collective-permute-start | bytes 1622024 | tf_op jit(solution)/shard_map/ppermute | solution.py:236
  101.7 32.1 %copy-start.1 = (f32[512,256]{1,0:T(8,128)S(1)}, f32[512,256]{1,0:T(8,128)}, u32[]{:S(2)}) copy-start(f32[512,256]{1,0:T(8,128)} %copy-done) | copy-start | bytes 1572868
  101.7 34.5 %collective-permute-start.26 = (f16[528,512]{1,0:T(8,128)(2,1)}, f16[528,512]{1,0:T(8,128)(2,1)S(1)}, u32[]{:S(2)}, u32[]{:S(2)}) collective-permute-start(f16[528,512]{1,0:T(8,128)(2,1)} %get-tuple-element.33), channel_id=1, source_target_pairs={{23,3},{19,7},{26,10},{30,14},{1,17},{5,21},{12,24},{8,28}} | collective-permute-start | bytes 1622024 | tf_op jit(solution)/shard_map/ppermute | solution.py:236
  133.7 2.5 %copy-start.7 = (f16[528,512]{1,0:T(8,128)(2,1)S(1)}, f16[528,512]{1,0:T(8,128)(2,1)}, u32[]{:S(2)}) copy-start(f16[528,512]{1,0:T(8,128)(2,1)} %copy-done.6) | copy-start | bytes 1622020
  133.7 2.5 %copy-start.9 = (f16[528,512]{1,0:T(8,128)(2,1)S(1)}, f16[528,512]{1,0:T(8,128)(2,1)}, u32[]{:S(2)}) copy-start(f16[528,512]{1,0:T(8,128)(2,1)} %copy-done.8) | copy-start | bytes 1622020

commit v4 on v3

--- a/solution.py
+++ b/solution.py
@@ -12,40 +12,37 @@
 CHUNKS = 2
 STEPS = 2
 AXES = ("proj", "row")
-ROWS = {"x": "own", "y": "own"}
 EVENTS = (
     ("hop", ("x", 0), 0),
     ("hop", ("own", 0), 0),
     ("hop", ("y", 0), 0),
     ("begin", ("oo", 0), 0),
-    ("hop", ("x", 1), 1),
-    ("hop", ("y", 1), 1),
     ("begin", ("os", 0), 1),
     ("first", ("oo", 0), 1),
     ("begin", ("x", 0), 1),
+    ("hop", ("x", 1), 1),
     ("begin", ("y", 0), 1),
+    ("hop", ("y", 1), 1),
+    ("first", ("os", 0), 1),
     ("second", ("oo", 0), 1),
+    ("first", ("x", 0), 1),
+    ("first", ("y", 0), 1),
+    ("second", ("os", 0), 1),
     ("begin", ("x", 1), 1),
     ("begin", ("y", 1), 1),
-    ("first", ("os", 0), 1),
     ("begin", ("xy", 0), 1),
+    ("second", ("x", 0), 1),
+    ("second", ("y", 0), 1),
     ("first", ("x", 1), 1),
-    ("first", ("x", 0), 1),
-    ("first", ("y", 0), 1),
     ("first", ("y", 1), 1),
     ("first", ("xy", 0), 1),
-    ("second", ("os", 0), 1),
-    ("second", ("x", 0), 1),
-    ("second", ("y", 0), 1),
     ("second", ("x", 1), 1),
     ("second", ("y", 1), 1),
+    ("send", ("x", 0), 1),
     ("send", ("y", 0), 1),
-    ("send", ("x", 0), 1),
     ("second", ("xy", 0), 1),
-    ("wait", ("x", 0), 1),
-    ("wait", ("y", 0), 1),
     ("send", ("plain", 0), 1),
-    ("send", ("mirror", 0), 0),
+    ("send", ("mirror", 0), 1),
 )
 
 
@@ -171,11 +168,14 @@
     return stages
 
 
-def assemble_kernel(place_ref, own_ref, first_e_ref, second_e_ref, first_ref, second_ref, turned_ref, out_ref):
+def assemble_kernel(place_ref, own_ref, first_e_ref, second_e_ref, plain_e_ref, mirror_e_ref, *refs):
+    first_ref, second_ref, turned_ref, plain_ref, mirror_ref, out_ref = refs
     tile = first_ref.shape[1]
     down = column(power_of_two(own_ref[...], -1))
-    first = first_ref[...] * down * power_of_two(first_e_ref[...], -1)
-    second = (second_ref[...] + jnp.transpose(turned_ref[...])) * down * power_of_two(second_e_ref[...], -1)
+    e_first, e_second = first_e_ref[...] + plain_e_ref[:1, :], second_e_ref[...] + mirror_e_ref[:1, :]
+    first = (first_ref[...] + plain_ref[...]) * down * power_of_two(e_first, -1)
+    turned = jnp.transpose(turned_ref[...] + mirror_ref[:tile, :])
+    second = (second_ref[...] + turned) * down * power_of_two(e_second, -1)
     at = place_ref[0] == 0
 
     @pl.when(at)
@@ -189,10 +189,11 @@
         out_ref[:, tile:] = first
 
 
-def assemble(place, e_own, e_first, e_second, first, second, turned):
+def assemble(place, e_own, e_first, e_second, first, second, turned, plain, mirror):
     tile = first.shape[0]
     step = tile // STEPS
     line = pl.BlockSpec((1, tile), lambda i: (0, 0))
+    below = pl.BlockSpec((8, tile), lambda i: (tile // 8, 0))
     rows = pl.BlockSpec((step, tile), lambda i: (i, 0))
     return pl.pallas_call(
         assemble_kernel,
@@ -202,13 +203,17 @@
             pl.BlockSpec((1, step), lambda i: (0, i)),
             line,
             line,
+            below,
+            below,
             rows,
             rows,
             pl.BlockSpec((tile, step), lambda i: (0, i)),
+            rows,
+            pl.BlockSpec((tile + EXTRA, step), lambda i: (0, i)),
         ],
         out_specs=pl.BlockSpec((step, 2 * tile), lambda i: (i, 0)),
         out_shape=jax.ShapeDtypeStruct((tile, 2 * tile), jnp.float32),
-    )(place, e_own, e_first, e_second, first, second, turned)
+    )(place, e_own, e_first, e_second, plain, mirror, first, second, turned, plain, mirror)
 
 
 def product(rows, columns):
@@ -235,16 +240,23 @@
                         pairs.append(((2 * at[0] + at[1]) * nr + at[2], (2 * c + h) * nr + z))
         return lax.ppermute(value, AXES, pairs)
 
-    stages = {n: tree(np_, nr, 2, m) for n, m in (("oo", 0), ("os", 0), ("x", 1), ("y", 2))}
-    one, two = [], []
-    for s in range(np_):
-        if s // 2 in (0, nr - 1):
-            a, b = [(0, 1), (3, 2)], [(1, 2), (2, 1)]
-        else:
-            a, b = [(0, 1), (1, 0), (2, 3), (3, 2)], [(1, 3), (2, 0)]
-        one += [(s * nr + i, s * nr + j) for i, j in a]
-        two += [(s * nr + i, s * nr + j) for i, j in b]
-    stages["xy"] = [one, two]
+    def pairs_of(line):
+        found = []
+        for s in range(np_):
+            found += [(s * nr + i, s * nr + j) for i, j in line(s // 2)]
+        return found
+
+    def y_line(c):
+        return [[(1, 0), (3, 2)], [(0, 2), (2, 0)]] if c % 2 == 0 else [[(0, 1), (2, 3)], [(1, 3), (3, 1)]]
+
+    def xy_line(c):
+        if c in (0, 3):
+            return [[(0, 1), (3, 2)], [(1, 2), (2, 1)]]
+        return [[(0, 1), (1, 0), (2, 3), (3, 2)], [(1, 3), (2, 0)]]
+
+    stages = {n: tree(np_, nr, 2, m) for n, m in (("oo", 0), ("os", 0), ("x", 1))}
+    for n, line in (("y", y_line), ("xy", xy_line)):
+        stages[n] = [pairs_of(lambda c: line(c)[i]) for i in range(2)]
 
     carry, moving, token = {}, {}, []
 
@@ -279,7 +291,7 @@
         below = jnp.broadcast_to(ordered(e, wait), (EXTRA, tile))
         return jnp.concatenate([total.astype(jnp.float16), below.astype(jnp.float16)], axis=0)
 
-    got, rows, arrived = {}, {"own": own}, {}
+    got, arrived = {}, {}
     for kind, name, wait in EVENTS:
         what, i = name
         if kind == "hop":
@@ -292,13 +304,12 @@
                 begin(name, product(own, own))
             elif what == "os":
                 sibling = ordered(sibling, wait)
-                rows["both"] = jnp.concatenate([own, sibling], axis=0)
                 begin(name, jnp.where(h == 0, product(own[:half], sibling), product(sibling[half:], own)))
             elif what == "xy":
                 begin(name, product(ordered(whole("x"), wait), whole("y")))
             else:
                 got[name] = ordered(got[name], wait)
-                begin(name, product(rows[ROWS[what]], got[name][:piece]))
+                begin(name, product(own, got[name][:piece]))
         elif kind == "first":
             carry[name] = ordered(carry[name], wait) + moving[name].astype(jnp.float32)
             send(name, 1)
@@ -324,37 +335,27 @@
         elif what == "y":
             arrived[what] = receive(
                 message(wide("y"), e_own),
-                lambda c, h, z: (c ^ 2, h ^ (c & 1) ^ (c >> 1) ^ 1, c) if c ^ z == 2 else None,
+                lambda c, h, z: (c ^ 2, h ^ (c & 1) ^ (c >> 1) ^ 1, z) if c ^ z == 2 else None,
             )
 
-    wide = {a: wide(a) for a in "xy"}
-    plain, mirror = arrived["plain"], arrived["mirror"]
+    def is_k(m, value):
+        return jnp.where(k == m, value, jnp.zeros_like(value))
+
     e_x, e_y = exponents(got["x", CHUNKS - 1]), exponents(got["y", CHUNKS - 1])
-    pad = jnp.concatenate([carry["os", 0], jnp.broadcast_to(e_own, (half, tile))], axis=0)
-    if ROWS == {"x": "own", "y": "own"}:
-        other = hop(pad, "proj", np_, 1)
-    else:
-        sent = {a: wide[a][tile:] * power_of_two(e, -1) if ROWS[a] == "both" else jnp.zeros_like(pad) for a, e in (("x", e_x), ("y", e_y))}
-        other = hop(jnp.where(k == 0, pad, jnp.where(k == 1, sent["x"], sent["y"])), "proj", np_, 1)
-    zero = jnp.zeros((tile, tile), jnp.float32)
-    straight = jnp.where(k == 0, carry["oo", 0], jnp.where(k == 1, wide["x"][:tile], jnp.where(k == 2, wide["y"][:tile], zero)))
-    straight = straight + plain[:tile].astype(jnp.float32)
-    low, high = jnp.where(h == 0, carry["os", 0], other[:half]), jnp.where(h == 0, other[:half], carry["os", 0])
-    cross = jnp.concatenate([low, high], axis=0)
-    from_sibling = jnp.zeros_like(k == 0)
-    for a, m in (("x", 1), ("y", 2)):
-        if ROWS[a] == "both":
-            from_sibling = from_sibling | (k == m)
-    second = jnp.where(k == 0, jnp.where(h == 0, cross, zero), jnp.where(from_sibling, other, zero))
-    turned = jnp.where((k == 0) & (h == 1), cross, zero) + mirror[:tile].astype(jnp.float32)
-    e_first = jnp.where(k == 0, e_own, jnp.where(k == 1, e_x, jnp.where(k == 2, e_y, 0.0))) + exponents(plain)
-    e_second = jnp.where(k == 0, other[half : half + 1], 0.0) + exponents(mirror)
-    for a in "xy":
-        if ROWS[a] == "own":
-            turned = turned + arrived[a][:tile].astype(jnp.float32)
-            e_second = e_second + exponents(arrived[a])
+    diagonal, cross = carry["oo", 0], carry["os", 0]
+    e_below = jnp.broadcast_to(e_own, (8, tile))
+    other = hop(jnp.concatenate([cross, e_below], axis=0), "proj", np_, 1)
+    cross = jnp.where(h == 0, jnp.concatenate([cross, other[:half]], axis=0), jnp.concatenate([other[:half], cross], axis=0))
+    cross = is_k(0, cross)
+    wide_x, wide_y = arrived["x"].astype(jnp.float32), arrived["y"].astype(jnp.float32)
+    first = is_k(0, diagonal) + is_k(1, wide("x")) + is_k(2, wide("y"))
+    second = jnp.where(h == 0, cross, jnp.zeros_like(cross))
+    turned = jnp.where(h == 1, cross, jnp.zeros_like(cross)) + wide_x[:tile] + wide_y[:tile]
+    e_first = is_k(0, e_own) + is_k(1, e_x) + is_k(2, e_y)
+    e_second = is_k(0, other[half : half + 1]) + exponents(wide_x) + exponents(wide_y)
+    plain, mirror = arrived["plain"].astype(jnp.float32), arrived["mirror"].astype(jnp.float32)
     place = jnp.where(k == 0, h, jnp.where(k == 1, h ^ x, jnp.where(k == 2, h ^ x ^ y, h ^ y)))
-    return assemble(place.reshape(1), e_own, e_first, e_second, straight, second, turned)
+    return assemble(place.reshape(1), e_own, e_first, e_second, first, second, turned, plain, mirror)
 
 
 def plain_plan(projections):

time: 145 us -> 138 us (0.952)
  waiting for transfers between devices: 67.2 us -> 52.7 us
  starting transfers between devices: 43 us -> 51.3 us
  other arithmetic: 12.3 us -> 9.05 us
    ppermute x8, waiting for transfers between devices: 29.7 us -> 15.2 us  [receive(): return lax.ppermute(value, AXES, pairs)]
    ppermute x14, starting transfers between devices: 23.1 us -> 28.2 us  [send(): lax.ppermute(carry[name].astype(jnp.float16), AXES, stages[name[0]][stage])]
    ppermute x5, starting transfers between devices: 12.3 us -> 16.5 us  [hop(): return lax.ppermute(x, axis, [(i, i ^ mask) for i in range(size)])]
    convert_element_type x2 -> x4, other arithmetic: 0.01 us -> 2.59 us  [the longest x1 1.17 us: paired(): arrived['plain'].astype(jnp.float32)]
    add x4, other arithmetic: 6.76 us -> 4.28 us  [the longest x1 1.73 us: paired(): jnp.where(h == 1, cross, jnp.zeros_like(cross)) + wide_x[:tile]]
  transfers between devices with their start and end apart: 27 -> 27, of which waited for: 9 -> 11; matrix products, arithmetic and copies ran while one was open for 12% -> 12% of each run, Pallas kernels for 0% -> 0%
where the time goes in v4:
time: 138 us; the launch traced here: 135 us
  waiting for transfers between devices  52.7 us (38%)
  starting transfers between devices  51.3 us (37%)
  Pallas kernels  11.5 us (8%)
  other arithmetic  9.05 us (7%)
  matrix products  7.54 us (5%)
  local copies, waits for them, and re-layouts  2.21 us (2%)
    ppermute x14, waiting for transfers between devices, send(): lax.ppermute(carry[name].astype(jnp.float16), AXES, stages[name[0]][stage])  34.7 us
    ppermute x14, starting transfers between devices, send(): lax.ppermute(carry[name].astype(jnp.float16), AXES, stages[name[0]][stage])  28.2 us
    ppermute x5, starting transfers between devices, hop(): return lax.ppermute(x, axis, [(i, i ^ mask) for i in range(size)])  16.5 us
    ppermute x8, waiting for transfers between devices, receive(): return lax.ppermute(value, AXES, pairs)  15.2 us
    dot_general x8, matrix products, product(): lax.dot_general(rows, columns, (((1,), (1,)), ((), ())), preferred_elemen...  7.54 us
    ppermute x8, starting transfers between devices, receive(): return lax.ppermute(value, AXES, pairs)  6.62 us
    pallas_call x1, Pallas kernels, normalize(): pl.pallas_call(lambda *refs: norm_kernel(columns * nr, *refs), grid=(CHUN...  4.37 us
    pallas_call x1, Pallas kernels, assemble(): pl.pallas_call(assemble_kernel, grid=(STEPS,), in_specs=[pl.BlockSpec(mem...  3.91 us
  transfers between devices with their start and end apart: 27, of which 11 were waited for; matrix products, arithmetic and copies ran while one was open for 12% of the time, Pallas kernels for 0%

profile of v4, /device:TPU:13, one launch (start us, length us, event | category | flops | bytes accessed | tf_op | source)
XLA Modules:
  0.0 134.9 jit_solution(11468095322405131229)
XLA Ops:
  0.0 3.2 %shard_map.17.refs_1_ = f32[1,512]{1,0:T(1,128)} custom-call(f32[512,1,1536]{2,1,0:T(1,128)} %refs_0_.1), custom_call_target="tpu_custom_call" | custom-call | tf_op jit(solution)/shard_map/pallas_call | solution.py:120
  3.3 2.3 %collective-permute-start.1 = (f32[1,512]{1,0:T(1,128)}, f32[1,512]{1,0:T(1,128)S(1)}, u32[]{:S(2)}, u32[]{:S(2)}) collective-permute-start(f32[1,512]{1,0:T(1,128)} %shard_map.17.refs_1_), channel_id=1, source_target_pairs={{0,2},{1,3},{2,0},{3,1},{4,6},{5,7},{6,4},{7,5},{8,10},{9,11},{10,... | collective-permute-start | bytes 6152 | tf_op jit(solution)/shard_map/ppermute | solution.py:50
  5.8 1.1 collective-permute-done.1.refs_3_
  6.9 1.7 %collective-permute-done.2.refs_4_ = f32[1,512]{1,0:T(1,128)S(1)} collective-permute-done((f32[1,512]{1,0:T(1,128)}, f32[1,512]{1,0:T(1,128)S(1)}, u32[]{:S(2)}, u32[]{:S(2)}) %collective-permute-start.2) | collective-permute-done | bytes 2080 | tf_op jit(solution)/shard_map/ppermute | solution.py:50
  9.2 4.4 %shard_map.18 = (bf16[512,1536]{1,0:T(8,128)(2,1)}, f32[1,512]{1,0:T(1,128)}, bf16[256,1536]{1,0:T(8,128)(2,1)}, bf16[272,1536]{1,0:T(8,128)(2,1)}) custom-call(f32[512,1,1536]{2,1,0:T(1,128)} %refs_0_.1, f32[1,512]{1,0:T(1,128)} %shard_map.17.refs_1_, f32[1,512]{1,0:T(1,128)} %copy-done.3, f32[1,512]{1,0:T(1,128)} %copy-done.4, f32[1,512]{1,0:T(1,128)} %copy-done.5), custom_call_target="tpu_custom_call" | custom-call | tf_op jit(solution)/shard_map/pallas_call | solution.py:123
  13.5 2.2 %collective-permute-start.4 = (bf16[512,1536]{1,0:T(8,128)(2,1)}, bf16[512,1536]{1,0:T(8,128)(2,1)S(1)}, u32[]{:S(2)}, u32[]{:S(2)}) collective-permute-start(bf16[512,1536]{1,0:T(8,128)(2,1)} %get-tuple-element.11), channel_id=1, source_target_pairs={{0,4},{4,0},{8,12},{12,8},{16,20},{20,16},{24,28},{28,24},{1,5},{5... | collective-permute-start | bytes 4718600 | tf_op jit(solution)/shard_map/ppermute | solution.py:50
  15.7 1.3 collective-permute-start.3
  17.2 2.9 %fusion.28 = (f16[512,512]{1,0:T(8,128)(2,1)S(1)}, f32[512,512]{1,0:T(8,128)S(1)}) fusion(bf16[512,1536]{1,0:T(8,128)(2,1)} %get-tuple-element.11), kind=kOutput, calls=%fused_computation.64 | convolution fusion | flops 805568512 | bytes 3145728 | tf_op jit(solution)/shard_map/dot_general | solution.py:220
  20.1 1.3 collective-permute-start.5
  21.5 1.4 %copy-done.1 = bf16[512,1536]{1,0:T(8,128)(2,1)S(1)} copy-done((bf16[512,1536]{1,0:T(8,128)(2,1)S(1)}, bf16[512,1536]{1,0:T(8,128)(2,1)}, u32[]{:S(2)}) %copy-start.1) | copy-done | bytes 1572888
  24.1 1.3 collective-permute-start.8
  25.4 10.7 %collective-permute-done.5 = f16[512,512]{1,0:T(8,128)(2,1)S(1)} collective-permute-done((f16[512,512]{1,0:T(8,128)(2,1)S(1)}, f16[512,512]{1,0:T(8,128)(2,1)S(1)}, u32[]{:S(2)}, u32[]{:S(2)}) %collective-permute-start.5) | collective-permute-done | bytes 524320 | tf_op jit(solution)/shard_map/ppermute | solution.py:267
  36.4 1.9 %collective-permute-start.9 = (f16[512,512]{1,0:T(8,128)(2,1)S(1)}, f16[512,512]{1,0:T(8,128)(2,1)S(1)}, u32[]{:S(2)}, u32[]{:S(2)}) collective-permute-start(f16[512,512]{1,0:T(8,128)(2,1)S(1)} %get-tuple-element.27), channel_id=1, source_target_pairs={{2,0},{6,4},{10,9},{14,13},{17,18},{21,22},{25,27},{29,31}} | collective-permute-start | bytes 1572872 | tf_op jit(solution)/shard_map/ppermute | solution.py:267
  38.3 0.6 fusion.30
  39.0 0.6 fusion.31
  39.6 1.3 collective-permute-start.10
  40.9 4.0 %collective-permute-start.11 = (f16[512,256]{1,0:T(8,128)(2,1)S(1)}, f16[512,256]{1,0:T(8,128)(2,1)S(1)}, u32[]{:S(2)}, u32[]{:S(2)}) collective-permute-start(f16[512,256]{1,0:T(8,128)(2,1)S(1)} %get-tuple-element.44), channel_id=1, source_target_pairs={{1,0},{3,2},{5,4},{7,6},{8,9},{10,11},{12,13},{14,15},{17,16},{19,... | collective-permute-start | bytes 786440 | tf_op jit(solution)/shard_map/ppermute | solution.py:267
  45.3 0.8 collective-permute-start.13
  46.2 0.7 collective-permute-done.9
  46.9 5.9 %collective-permute-start.12 = (f16[256,512]{1,0:T(8,128)(2,1)S(1)}, f16[256,512]{1,0:T(8,128)(2,1)S(1)}, u32[]{:S(2)}, u32[]{:S(2)}) collective-permute-start(f16[256,512]{1,0:T(8,128)(2,1)S(1)} %get-tuple-element.25), channel_id=1, source_target_pairs={{2,0},{6,4},{10,9},{14,13},{17,18},{21,22},{25,27},{29,31}} | collective-permute-start | bytes 786440 | tf_op jit(solution)/shard_map/ppermute | solution.py:267
  53.2 1.3 collective-permute-start.15
  54.5 0.7 collective-permute-start.16
  55.2 0.9 collective-permute-done.12
  56.2 11.7 %collective-permute-start.14 = (f32[264,512]{1,0:T(8,128)S(1)}, f32[264,512]{1,0:T(8,128)S(1)}, u32[]{:S(2)}, u32[]{:S(2)}) collective-permute-start(f32[264,512]{1,0:T(8,128)S(1)} %pad_maximum_fusion.5), channel_id=1, source_target_pairs={{0,4},{4,0},{8,12},{12,8},{16,20},{20,16},{24,28},{28,24},{1,5},{5... | collective-permute-start | bytes 1622024 | tf_op jit(solution)/shard_map/ppermute | solution.py:50
  67.9 0.6 fusion.32
  68.7 0.6 fusion.33
  69.5 1.0 fusion.34
  70.6 1.3 collective-permute-start.17
  72.0 4.0 %collective-permute-start.18 = (f16[512,256]{1,0:T(8,128)(2,1)S(1)}, f16[512,256]{1,0:T(8,128)(2,1)S(1)}, u32[]{:S(2)}, u32[]{:S(2)}) collective-permute-start(f16[512,256]{1,0:T(8,128)(2,1)S(1)} %get-tuple-element.48), channel_id=1, source_target_pairs={{1,0},{3,2},{5,4},{7,6},{8,9},{10,11},{12,13},{14,15},{17,16},{19,... | collective-permute-start | bytes 786440 | tf_op jit(solution)/shard_map/ppermute | solution.py:267
  76.0 1.9 %collective-permute-start.19 = (f16[512,512]{1,0:T(8,128)(2,1)S(1)}, f16[512,512]{1,0:T(8,128)(2,1)S(1)}, u32[]{:S(2)}, u32[]{:S(2)}) collective-permute-start(f16[512,512]{1,0:T(8,128)(2,1)S(1)} %get-tuple-element.50), channel_id=1, source_target_pairs={{0,1},{3,2},{4,5},{7,6},{8,9},{9,8},{10,11},{11,10},{12,13},{13,12... | collective-permute-start | bytes 1572872 | tf_op jit(solution)/shard_map/ppermute | solution.py:267
  78.6 1.9 %collective-permute-done.17 = f16[512,256]{1,0:T(8,128)(2,1)S(1)} collective-permute-done((f16[512,256]{1,0:T(8,128)(2,1)S(1)}, f16[512,256]{1,0:T(8,128)(2,1)S(1)}, u32[]{:S(2)}, u32[]{:S(2)}) %collective-permute-start.17) | collective-permute-done | bytes 262176 | tf_op jit(solution)/shard_map/ppermute | solution.py:267
  80.6 0.9 collective-permute-done.18
  81.6 1.3 collective-permute-start.20
  82.9 0.7 collective-permute-start.21
  83.6 14.8 %collective-permute-done.19 = f16[512,512]{1,0:T(8,128)(2,1)S(1)} collective-permute-done((f16[512,512]{1,0:T(8,128)(2,1)S(1)}, f16[512,512]{1,0:T(8,128)(2,1)S(1)}, u32[]{:S(2)}, u32[]{:S(2)}) %collective-permute-start.19) | collective-permute-done | bytes 524320 | tf_op jit(solution)/shard_map/ppermute | solution.py:267
  98.8 1.3 collective-permute-start.24
  100.2 1.3 select_add_fusion
  101.8 0.7 collective-permute-start.22
  102.5 0.7 collective-permute-start.23
  103.2 4.9 %collective-permute-done.24 = f16[512,512]{1,0:T(8,128)(2,1)S(1)} collective-permute-done((f16[512,512]{1,0:T(8,128)(2,1)S(1)}, f16[512,512]{1,0:T(8,128)(2,1)S(1)}, u32[]{:S(2)}, u32[]{:S(2)}) %collective-permute-start.24) | collective-permute-done | bytes 524320 | tf_op jit(solution)/shard_map/ppermute | solution.py:267
  108.4 1.3 collective-permute-start.25
  109.7 1.3 collective-permute-start.26
  111.3 0.6 fusion.14.second_e_ref
  111.9 1.7 %slice_add_fusion = (f32[512,512]{1,0:T(8,128)}, f32[512,512]{1,0:T(8,128)}) fusion(f32[528,512]{1,0:T(8,128)S(1)} %convert_element_type.169, f32[528,512]{1,0:T(8,128)S(1)} %convert_element_type.167, f32[256,512]{1,0:T(8,128)S(1)} %convert_add_fusion.10.refs_1_, f32[256,512]{1,0:T(8,128)S(1)} %slice.61, pred[]{:T(512)S(6)} %eq.32, pred[]{:T(512)S(6)} %eq.16, ...), kind=kLoop, calls=%fused_computation.6 | loop fusion | flops 2097152 | bytes 5242883 | tf_op jit(solution)/shard_map/add | solution.py:353
  113.7 15.0 %collective-permute-done.25 = f16[528,512]{1,0:T(8,128)(2,1)S(1)} collective-permute-done((f16[528,512]{1,0:T(8,128)(2,1)S(1)}, f16[528,512]{1,0:T(8,128)(2,1)S(1)}, u32[]{:S(2)}, u32[]{:S(2)}) %collective-permute-start.25) | collective-permute-done | bytes 540704 | tf_op jit(solution)/shard_map/ppermute | solution.py:241
  128.7 1.2 convert_element_type.175.plain_e_ref.refs_3_
  129.9 1.2 convert_element_type.178.mirror_e_ref.refs_4_
  131.0 3.9 %shard_map.44 = f32[512,1024]{1,0:T(8,128)} custom-call(s32[1]{0:T(128)} %bitcast.place_ref, f32[1,512]{1,0:T(1,128)} %get-tuple-element.9.own_ref, f32[1,512]{1,0:T(1,128)} %fusion.12.first_e_ref, f32[1,512]{1,0:T(1,128)} %fusion.14.second_e_ref, f32[528,512]{1,0:T(8,128)} %convert_element_type.175.plain_e_ref.refs_3_, ...), custom_call_target="tpu_custom_call" | custom-call | tf_op jit(solution)/shard_map/pallas_call | solution.py:198
  (94 shorter events, 6.2 us)
Async XLA Ops:
  3.2 2.7 %collective-permute-start = (f32[1,512]{1,0:T(1,128)}, f32[1,512]{1,0:T(1,128)S(1)}, u32[]{:S(2)}, u32[]{:S(2)}) collective-permute-start(f32[1,512]{1,0:T(1,128)} %shard_map.17.refs_1_), channel_id=1, source_target_pairs={{0,1},{1,0},{2,3},{3,2},{4,5},{5,4},{6,7},{7,6},{8,9},{9,8},{10,11... | collective-permute-start | bytes 6152 | tf_op jit(solution)/shard_map/ppermute | solution.py:50
  3.3 3.6 %collective-permute-start.1 = (f32[1,512]{1,0:T(1,128)}, f32[1,512]{1,0:T(1,128)S(1)}, u32[]{:S(2)}, u32[]{:S(2)}) collective-permute-start(f32[1,512]{1,0:T(1,128)} %shard_map.17.refs_1_), channel_id=1, source_target_pairs={{0,2},{1,3},{2,0},{3,1},{4,6},{5,7},{6,4},{7,5},{8,10},{9,11},{10,... | collective-permute-start | bytes 6152 | tf_op jit(solution)/shard_map/ppermute | solution.py:50
  5.6 2.9 %collective-permute-start.2 = (f32[1,512]{1,0:T(1,128)}, f32[1,512]{1,0:T(1,128)S(1)}, u32[]{:S(2)}, u32[]{:S(2)}) collective-permute-start(f32[1,512]{1,0:T(1,128)} %shard_map.17.refs_1_), channel_id=1, source_target_pairs={{0,3},{1,2},{2,1},{3,0},{4,7},{5,6},{6,5},{7,4},{8,11},{9,10},{10,... | collective-permute-start | bytes 6152 | tf_op jit(solution)/shard_map/ppermute | solution.py:50
  5.8 2.8 %copy-start.3 = (f32[1,512]{1,0:T(1,128)}, f32[1,512]{1,0:T(1,128)S(1)}, u32[]{:S(2)}) copy-start(f32[1,512]{1,0:T(1,128)S(1)} %collective-permute-done.refs_2_) | copy-start | bytes 6148
  6.9 1.7 %copy-start.4 = (f32[1,512]{1,0:T(1,128)}, f32[1,512]{1,0:T(1,128)S(1)}, u32[]{:S(2)}) copy-start(f32[1,512]{1,0:T(1,128)S(1)} %collective-permute-done.1.refs_3_) | copy-start | bytes 6148
  8.6 0.6 copy-start.5
  13.5 7.9 %collective-permute-start.4 = (bf16[512,1536]{1,0:T(8,128)(2,1)}, bf16[512,1536]{1,0:T(8,128)(2,1)S(1)}, u32[]{:S(2)}, u32[]{:S(2)}) collective-permute-start(bf16[512,1536]{1,0:T(8,128)(2,1)} %get-tuple-element.11), channel_id=1, source_target_pairs={{0,4},{4,0},{8,12},{12,8},{16,20},{20,16},{24,28},{28,24},{1,5},{5... | collective-permute-start | bytes 4718600 | tf_op jit(solution)/shard_map/ppermute | solution.py:50
  15.7 5.7 %copy-start = (bf16[272,1536]{1,0:T(8,128)(2,1)S(1)}, bf16[272,1536]{1,0:T(8,128)(2,1)}, u32[]{:S(2)}) copy-start(bf16[272,1536]{1,0:T(8,128)(2,1)} %get-tuple-element.10.refs_0_) | copy-start | bytes 2506756
  15.7 22.6 %collective-permute-start.3 = (bf16[256,1536]{1,0:T(8,128)(2,1)}, bf16[256,1536]{1,0:T(8,128)(2,1)S(1)}, u32[]{:S(2)}, u32[]{:S(2)}) collective-permute-start(bf16[256,1536]{1,0:T(8,128)(2,1)} %get-tuple-element.12), channel_id=1, source_target_pairs={{8,0},{9,1},{10,2},{11,3},{12,4},{13,5},{14,6},{15,7},{4,8},{5,9},... | collective-permute-start | bytes 2359304 | tf_op jit(solution)/shard_map/ppermute | solution.py:241
  16.9 22.0 %collective-permute-start.7 = (bf16[256,1536]{1,0:T(8,128)(2,1)}, bf16[256,1536]{1,0:T(8,128)(2,1)S(1)}, u32[]{:S(2)}, u32[]{:S(2)}) collective-permute-start(bf16[256,1536]{1,0:T(8,128)(2,1)} %get-tuple-element.12), channel_id=1, source_target_pairs={{16,0},{17,1},{18,2},{19,3},{20,4},{21,5},{22,6},{23,7},{28,8},{29... | collective-permute-start | bytes 2359304 | tf_op jit(solution)/shard_map/ppermute | solution.py:241
  20.1 1.4 %copy-start.2 = (f32[1,512]{1,0:T(1,128)S(1)}, f32[1,512]{1,0:T(1,128)}, u32[]{:S(2)}) copy-start(f32[1,512]{1,0:T(1,128)} %get-tuple-element.9.own_ref) | copy-start | bytes 6148
  20.1 16.1 %collective-permute-start.5 = (f16[512,512]{1,0:T(8,128)(2,1)S(1)}, f16[512,512]{1,0:T(8,128)(2,1)S(1)}, u32[]{:S(2)}, u32[]{:S(2)}) collective-permute-start(f16[512,512]{1,0:T(8,128)(2,1)S(1)} %get-tuple-element.38), channel_id=1, source_target_pairs={{1,0},{3,2},{5,4},{7,6},{8,9},{11,10},{12,13},{15,14},{16,17},{19,... | collective-permute-start | bytes 1572872 | tf_op jit(solution)/shard_map/ppermute | solution.py:267
  21.5 1.4 %copy-start.1 = (bf16[512,1536]{1,0:T(8,128)(2,1)S(1)}, bf16[512,1536]{1,0:T(8,128)(2,1)}, u32[]{:S(2)}) copy-start(bf16[512,1536]{1,0:T(8,128)(2,1)} %get-tuple-element.11) | copy-start | bytes 4718596
  24.1 21.2 %collective-permute-start.8 = (f16[256,512]{1,0:T(8,128)(2,1)S(1)}, f16[256,512]{1,0:T(8,128)(2,1)S(1)}, u32[]{:S(2)}, u32[]{:S(2)}) collective-permute-start(f16[256,512]{1,0:T(8,128)(2,1)S(1)} %get-tuple-element.40), channel_id=1, source_target_pairs={{1,0},{3,2},{5,4},{7,6},{8,9},{11,10},{12,13},{15,14},{16,17},{19,... | collective-permute-start | bytes 786440 | tf_op jit(solution)/shard_map/ppermute | solution.py:267
  36.4 10.5 %collective-permute-start.9 = (f16[512,512]{1,0:T(8,128)(2,1)S(1)}, f16[512,512]{1,0:T(8,128)(2,1)S(1)}, u32[]{:S(2)}, u32[]{:S(2)}) collective-permute-start(f16[512,512]{1,0:T(8,128)(2,1)S(1)} %get-tuple-element.27), channel_id=1, source_target_pairs={{2,0},{6,4},{10,9},{14,13},{17,18},{21,22},{25,27},{29,31}} | collective-permute-start | bytes 1572872 | tf_op jit(solution)/shard_map/ppermute | solution.py:267
  39.6 13.3 %collective-permute-start.10 = (f16[512,256]{1,0:T(8,128)(2,1)S(1)}, f16[512,256]{1,0:T(8,128)(2,1)S(1)}, u32[]{:S(2)}, u32[]{:S(2)}) collective-permute-start(f16[512,256]{1,0:T(8,128)(2,1)S(1)} %get-tuple-element.42), channel_id=1, source_target_pairs={{0,1},{3,2},{4,5},{7,6},{9,8},{11,10},{13,12},{15,14},{16,17},{18,... | collective-permute-start | bytes 786440 | tf_op jit(solution)/shard_map/ppermute | solution.py:267
  40.9 12.2 %collective-permute-start.11 = (f16[512,256]{1,0:T(8,128)(2,1)S(1)}, f16[512,256]{1,0:T(8,128)(2,1)S(1)}, u32[]{:S(2)}, u32[]{:S(2)}) collective-permute-start(f16[512,256]{1,0:T(8,128)(2,1)S(1)} %get-tuple-element.44), channel_id=1, source_target_pairs={{1,0},{3,2},{5,4},{7,6},{8,9},{10,11},{12,13},{14,15},{17,16},{19,... | collective-permute-start | bytes 786440 | tf_op jit(solution)/shard_map/ppermute | solution.py:267
  44.9 22.9 %collective-permute-start.6 = (bf16[272,1536]{1,0:T(8,128)(2,1)S(1)}, bf16[272,1536]{1,0:T(8,128)(2,1)S(1)}, u32[]{:S(2)}, u32[]{:S(2)}) collective-permute-start(bf16[272,1536]{1,0:T(8,128)(2,1)S(1)} %shard_map.22), channel_id=1, source_target_pairs={{8,0},{9,1},{10,2},{11,3},{12,4},{13,5},{14,6},{15,7},{4,8},{5,9},... | collective-permute-start | bytes 2506760 | tf_op jit(solution)/shard_map/ppermute | solution.py:241
  45.3 23.4 %collective-permute-start.13 = (bf16[272,1536]{1,0:T(8,128)(2,1)S(1)}, bf16[272,1536]{1,0:T(8,128)(2,1)S(1)}, u32[]{:S(2)}, u32[]{:S(2)}) collective-permute-start(bf16[272,1536]{1,0:T(8,128)(2,1)S(1)} %shard_map.30), channel_id=1, source_target_pairs={{16,0},{17,1},{18,2},{19,3},{20,4},{21,5},{22,6},{23,7},{28,8},{29... | collective-permute-start | bytes 2506760 | tf_op jit(solution)/shard_map/ppermute | solution.py:241
  46.9 9.2 %collective-permute-start.12 = (f16[256,512]{1,0:T(8,128)(2,1)S(1)}, f16[256,512]{1,0:T(8,128)(2,1)S(1)}, u32[]{:S(2)}, u32[]{:S(2)}) collective-permute-start(f16[256,512]{1,0:T(8,128)(2,1)S(1)} %get-tuple-element.25), channel_id=1, source_target_pairs={{2,0},{6,4},{10,9},{14,13},{17,18},{21,22},{25,27},{29,31}} | collective-permute-start | bytes 786440 | tf_op jit(solution)/shard_map/ppermute | solution.py:267
  53.2 17.4 %collective-permute-start.15 = (f16[512,256]{1,0:T(8,128)(2,1)S(1)}, f16[512,256]{1,0:T(8,128)(2,1)S(1)}, u32[]{:S(2)}, u32[]{:S(2)}) collective-permute-start(f16[512,256]{1,0:T(8,128)(2,1)S(1)} %get-tuple-element.23), channel_id=1, source_target_pairs={{2,1},{6,5},{10,8},{14,12},{17,19},{21,23},{25,26},{29,30}} | collective-permute-start | bytes 786440 | tf_op jit(solution)/shard_map/ppermute | solution.py:267
  54.5 17.4 %collective-permute-start.16 = (f16[512,256]{1,0:T(8,128)(2,1)S(1)}, f16[512,256]{1,0:T(8,128)(2,1)S(1)}, u32[]{:S(2)}, u32[]{:S(2)}) collective-permute-start(f16[512,256]{1,0:T(8,128)(2,1)S(1)} %get-tuple-element.21), channel_id=1, source_target_pairs={{0,2},{2,0},{4,6},{6,4},{9,11},{11,9},{13,15},{15,13},{16,18},{18,... | collective-permute-start | bytes 786440 | tf_op jit(solution)/shard_map/ppermute | solution.py:267
  56.2 22.4 %collective-permute-start.14 = (f32[264,512]{1,0:T(8,128)S(1)}, f32[264,512]{1,0:T(8,128)S(1)}, u32[]{:S(2)}, u32[]{:S(2)}) collective-permute-start(f32[264,512]{1,0:T(8,128)S(1)} %pad_maximum_fusion.5), channel_id=1, source_target_pairs={{0,4},{4,0},{8,12},{12,8},{16,20},{20,16},{24,28},{28,24},{1,5},{5... | collective-permute-start | bytes 1622024 | tf_op jit(solution)/shard_map/ppermute | solution.py:50
  70.6 9.9 %collective-permute-start.17 = (f16[512,256]{1,0:T(8,128)(2,1)S(1)}, f16[512,256]{1,0:T(8,128)(2,1)S(1)}, u32[]{:S(2)}, u32[]{:S(2)}) collective-permute-start(f16[512,256]{1,0:T(8,128)(2,1)S(1)} %get-tuple-element.46), channel_id=1, source_target_pairs={{0,1},{3,2},{4,5},{7,6},{9,8},{11,10},{13,12},{15,14},{16,17},{18,... | collective-permute-start | bytes 786440 | tf_op jit(solution)/shard_map/ppermute | solution.py:267
  72.0 9.5 %collective-permute-start.18 = (f16[512,256]{1,0:T(8,128)(2,1)S(1)}, f16[512,256]{1,0:T(8,128)(2,1)S(1)}, u32[]{:S(2)}, u32[]{:S(2)}) collective-permute-start(f16[512,256]{1,0:T(8,128)(2,1)S(1)} %get-tuple-element.48), channel_id=1, source_target_pairs={{1,0},{3,2},{5,4},{7,6},{8,9},{10,11},{12,13},{14,15},{17,16},{19,... | collective-permute-start | bytes 786440 | tf_op jit(solution)/shard_map/ppermute | solution.py:267
  76.0 22.3 %collective-permute-start.19 = (f16[512,512]{1,0:T(8,128)(2,1)S(1)}, f16[512,512]{1,0:T(8,128)(2,1)S(1)}, u32[]{:S(2)}, u32[]{:S(2)}) collective-permute-start(f16[512,512]{1,0:T(8,128)(2,1)S(1)} %get-tuple-element.50), channel_id=1, source_target_pairs={{0,1},{3,2},{4,5},{7,6},{8,9},{9,8},{10,11},{11,10},{12,13},{13,12... | collective-permute-start | bytes 1572872 | tf_op jit(solution)/shard_map/ppermute | solution.py:267
  81.6 17.0 %collective-permute-start.20 = (f16[512,256]{1,0:T(8,128)(2,1)S(1)}, f16[512,256]{1,0:T(8,128)(2,1)S(1)}, u32[]{:S(2)}, u32[]{:S(2)}) collective-permute-start(f16[512,256]{1,0:T(8,128)(2,1)S(1)} %get-tuple-element.19), channel_id=1, source_target_pairs={{2,1},{6,5},{10,8},{14,12},{17,19},{21,23},{25,26},{29,30}} | collective-permute-start | bytes 786440 | tf_op jit(solution)/shard_map/ppermute | solution.py:267
  82.9 15.8 %collective-permute-start.21 = (f16[512,256]{1,0:T(8,128)(2,1)S(1)}, f16[512,256]{1,0:T(8,128)(2,1)S(1)}, u32[]{:S(2)}, u32[]{:S(2)}) collective-permute-start(f16[512,256]{1,0:T(8,128)(2,1)S(1)} %get-tuple-element.17), channel_id=1, source_target_pairs={{0,2},{2,0},{4,6},{6,4},{9,11},{11,9},{13,15},{15,13},{16,18},{18,... | collective-permute-start | bytes 786440 | tf_op jit(solution)/shard_map/ppermute | solution.py:267
  98.8 9.2 %collective-permute-start.24 = (f16[512,512]{1,0:T(8,128)(2,1)S(1)}, f16[512,512]{1,0:T(8,128)(2,1)S(1)}, u32[]{:S(2)}, u32[]{:S(2)}) collective-permute-start(f16[512,512]{1,0:T(8,128)(2,1)S(1)} %get-tuple-element.15), channel_id=1, source_target_pairs={{1,2},{2,1},{5,6},{6,5},{9,11},{10,8},{13,15},{14,12},{17,19},{18,... | collective-permute-start | bytes 1572872 | tf_op jit(solution)/shard_map/ppermute | solution.py:267
  101.8 9.3 %collective-permute-start.22 = (f16[528,512]{1,0:T(8,128)(2,1)S(1)}, f16[528,512]{1,0:T(8,128)(2,1)S(1)}, u32[]{:S(2)}, u32[]{:S(2)}) collective-permute-start(f16[528,512]{1,0:T(8,128)(2,1)S(1)} %get-tuple-element.36), channel_id=1, source_target_pairs={{12,1},{8,5},{1,8},{5,12},{30,19},{26,23},{19,26},{23,30}} | collective-permute-start | bytes 1622024 | tf_op jit(solution)/shard_map/ppermute | solution.py:241
  102.5 8.7 %collective-permute-start.23 = (f16[528,512]{1,0:T(8,128)(2,1)S(1)}, f16[528,512]{1,0:T(8,128)(2,1)S(1)}, u32[]{:S(2)}, u32[]{:S(2)}) collective-permute-start(f16[528,512]{1,0:T(8,128)(2,1)S(1)} %get-tuple-element.37), channel_id=1, source_target_pairs={{22,2},{18,6},{27,11},{31,15},{0,16},{4,20},{13,25},{9,29}} | collective-permute-start | bytes 1622024 | tf_op jit(solution)/shard_map/ppermute | solution.py:241
  108.4 20.3 %collective-permute-start.25 = (f16[528,512]{1,0:T(8,128)(2,1)S(1)}, f16[528,512]{1,0:T(8,128)(2,1)S(1)}, u32[]{:S(2)}, u32[]{:S(2)}) collective-permute-start(f16[528,512]{1,0:T(8,128)(2,1)S(1)} %get-tuple-element.35), channel_id=1, source_target_pairs={{15,3},{11,7},{2,10},{6,14},{29,17},{25,21},{16,24},{20,28}} | collective-permute-start | bytes 1622024 | tf_op jit(solution)/shard_map/ppermute | solution.py:241
  109.7 20.2 %collective-permute-start.26 = (f16[528,512]{1,0:T(8,128)(2,1)S(1)}, f16[528,512]{1,0:T(8,128)(2,1)S(1)}, u32[]{:S(2)}, u32[]{:S(2)}) collective-permute-start(f16[528,512]{1,0:T(8,128)(2,1)S(1)} %get-tuple-element.34), channel_id=1, source_target_pairs={{23,3},{19,7},{26,10},{30,14},{1,17},{5,21},{12,24},{8,28}} | collective-permute-start | bytes 1622024 | tf_op jit(solution)/shard_map/ppermute | solution.py:241

commit v5 on v4

--- a/solution.py
+++ b/solution.py
@@ -19,21 +19,21 @@
     ("begin", ("oo", 0), 0),
     ("begin", ("os", 0), 1),
     ("first", ("oo", 0), 1),
+    ("begin", ("y", 0), 1),
+    ("hop", ("y", 1), 2),
+    ("first", ("os", 0), 1),
     ("begin", ("x", 0), 1),
-    ("hop", ("x", 1), 1),
-    ("begin", ("y", 0), 1),
-    ("hop", ("y", 1), 1),
-    ("first", ("os", 0), 1),
+    ("hop", ("x", 1), 2),
     ("second", ("oo", 0), 1),
     ("first", ("x", 0), 1),
     ("first", ("y", 0), 1),
+    ("begin", ("x", 1), 1),
     ("second", ("os", 0), 1),
-    ("begin", ("x", 1), 1),
     ("begin", ("y", 1), 1),
     ("begin", ("xy", 0), 1),
+    ("first", ("x", 1), 1),
     ("second", ("x", 0), 1),
     ("second", ("y", 0), 1),
-    ("first", ("x", 1), 1),
     ("first", ("y", 1), 1),
     ("first", ("xy", 0), 1),
     ("second", ("x", 1), 1),
@@ -298,7 +298,8 @@
             if what == "own":
                 sibling = hop(ordered(own, wait), "proj", np_, 1)
             else:
-                got[name] = receive(ordered(pieces[i], wait), from_x if what == "x" else from_y)
+                value = gate(pieces[i], got[what, i - 1]) if wait == 2 else ordered(pieces[i], wait)
+                got[name] = receive(value, from_x if what == "x" else from_y)
         elif kind == "begin":
             if what == "oo":
                 begin(name, product(own, own))
@@ -369,12 +370,15 @@
     return lax.psum_scatter(part, "row", scatter_dimension=1, tiled=True)
 
 
+def per_device(projections):
+    tile, det_rows, columns = projections.shape
+    fits = lax.axis_size("proj") == 8 and lax.axis_size("row") == 4 and det_rows == 1
+    if fits and tile % (128 * CHUNKS) == 0 and columns >= tile:
+        return paired(projections)
+    return plain_plan(projections)
+
+
 def solution(mesh):
-    fits = mesh.shape["row"] == 4 and mesh.shape["proj"] == 8
     return jax.shard_map(
-        paired if fits else plain_plan,
-        mesh=mesh,
-        in_specs=(P("proj", "row", None),),
-        out_specs=P("proj", "row"),
-        check_vma=False,
+        per_device, mesh=mesh, in_specs=(P("proj", "row", None),), out_specs=P("proj", "row"), check_vma=False
     )

time: 138 us -> 133 us (0.964)
  waiting for transfers between devices: 52.7 us -> 47.4 us
    ppermute x5, starting transfers between devices: 16.5 us -> 9.54 us  [hop(): return lax.ppermute(x, axis, [(i, i ^ mask) for i in range(size)])]
    ppermute x14, starting transfers between devices: 28.2 us -> 34.8 us  [send(): lax.ppermute(carry[name].astype(jnp.float16), AXES, stages[name[0]][stage])]
    ppermute x14, waiting for transfers between devices: 34.7 us -> 30.5 us  [send(): lax.ppermute(carry[name].astype(jnp.float16), AXES, stages[name[0]][stage])]
    ppermute x8, starting transfers between devices: 6.62 us -> 8.06 us  [receive(): return lax.ppermute(value, AXES, pairs)]
  transfers between devices with their start and end apart: 27 -> 27, of which waited for: 11 -> 8; matrix products, arithmetic and copies ran while one was open for 12% -> 12% of each run, Pallas kernels for 0% -> 0%
where the time goes in v5:
time: 133 us; the launch traced here: 131 us
  starting transfers between devices  52.4 us (39%)
  waiting for transfers between devices  47.4 us (36%)
  Pallas kernels  11.5 us (9%)
  other arithmetic  8.97 us (7%)
  matrix products  7.52 us (6%)
  local copies, waits for them, and re-layouts  2.21 us (2%)
    ppermute x14, starting transfers between devices, send(): lax.ppermute(carry[name].astype(jnp.float16), AXES, stages[name[0]][stage])  34.8 us
    ppermute x14, waiting for transfers between devices, send(): lax.ppermute(carry[name].astype(jnp.float16), AXES, stages[name[0]][stage])  30.5 us
    ppermute x8, waiting for transfers between devices, receive(): return lax.ppermute(value, AXES, pairs)  14.2 us
    ppermute x5, starting transfers between devices, hop(): return lax.ppermute(x, axis, [(i, i ^ mask) for i in range(size)])  9.54 us
    ppermute x8, starting transfers between devices, receive(): return lax.ppermute(value, AXES, pairs)  8.06 us
    dot_general x8, matrix products, product(): lax.dot_general(rows, columns, (((1,), (1,)), ((), ())), preferred_elemen...  7.52 us
    pallas_call x1, Pallas kernels, normalize(): pl.pallas_call(lambda *refs: norm_kernel(columns * nr, *refs), grid=(CHUN...  4.37 us
    pallas_call x1, Pallas kernels, assemble(): pl.pallas_call(assemble_kernel, grid=(STEPS,), in_specs=[pl.BlockSpec(mem...  3.91 us
  transfers between devices with their start and end apart: 27, of which 8 were waited for; matrix products, arithmetic and copies ran while one was open for 12% of the time, Pallas kernels for 0%

profile of v5, /device:TPU:13, one launch (start us, length us, event | category | flops | bytes accessed | tf_op | source)
XLA Modules:
  0.0 130.7 jit_solution(3103532457539425967)
XLA Ops:
  0.0 3.2 %shard_map.17.refs_1_ = f32[1,512]{1,0:T(1,128)} custom-call(f32[512,1,1536]{2,1,0:T(1,128)} %refs_0_.1), custom_call_target="tpu_custom_call" | custom-call | tf_op jit(solution)/shard_map/pallas_call | solution.py:120
  3.3 2.3 %collective-permute-start.1 = (f32[1,512]{1,0:T(1,128)}, f32[1,512]{1,0:T(1,128)S(1)}, u32[]{:S(2)}, u32[]{:S(2)}) collective-permute-start(f32[1,512]{1,0:T(1,128)} %shard_map.17.refs_1_), channel_id=1, source_target_pairs={{0,2},{1,3},{2,0},{3,1},{4,6},{5,7},{6,4},{7,5},{8,10},{9,11},{10,... | collective-permute-start | bytes 6152 | tf_op jit(solution)/shard_map/ppermute | solution.py:50
  5.8 1.1 collective-permute-done.1.refs_3_
  6.9 1.7 %collective-permute-done.2.refs_4_ = f32[1,512]{1,0:T(1,128)S(1)} collective-permute-done((f32[1,512]{1,0:T(1,128)}, f32[1,512]{1,0:T(1,128)S(1)}, u32[]{:S(2)}, u32[]{:S(2)}) %collective-permute-start.2) | collective-permute-done | bytes 2080 | tf_op jit(solution)/shard_map/ppermute | solution.py:50
  9.2 4.4 %shard_map.18 = (bf16[512,1536]{1,0:T(8,128)(2,1)}, f32[1,512]{1,0:T(1,128)}, bf16[256,1536]{1,0:T(8,128)(2,1)}, bf16[272,1536]{1,0:T(8,128)(2,1)}) custom-call(f32[512,1,1536]{2,1,0:T(1,128)} %refs_0_.1, f32[1,512]{1,0:T(1,128)} %shard_map.17.refs_1_, f32[1,512]{1,0:T(1,128)} %copy-done.3, f32[1,512]{1,0:T(1,128)} %copy-done.4, f32[1,512]{1,0:T(1,128)} %copy-done.5), custom_call_target="tpu_custom_call" | custom-call | tf_op jit(solution)/shard_map/pallas_call | solution.py:123
  13.5 2.2 %collective-permute-start.4 = (bf16[512,1536]{1,0:T(8,128)(2,1)}, bf16[512,1536]{1,0:T(8,128)(2,1)S(1)}, u32[]{:S(2)}, u32[]{:S(2)}) collective-permute-start(bf16[512,1536]{1,0:T(8,128)(2,1)} %get-tuple-element.12), channel_id=1, source_target_pairs={{0,4},{4,0},{8,12},{12,8},{16,20},{20,16},{24,28},{28,24},{1,5},{5... | collective-permute-start | bytes 4718600 | tf_op jit(solution)/shard_map/ppermute | solution.py:50
  15.9 1.5 %collective-permute-start.3 = (bf16[256,1536]{1,0:T(8,128)(2,1)}, bf16[256,1536]{1,0:T(8,128)(2,1)S(1)}, u32[]{:S(2)}, u32[]{:S(2)}) collective-permute-start(bf16[256,1536]{1,0:T(8,128)(2,1)} %get-tuple-element.11), channel_id=1, source_target_pairs={{8,0},{9,1},{10,2},{11,3},{12,4},{13,5},{14,6},{15,7},{4,8},{5,9},... | collective-permute-start | bytes 2359304 | tf_op jit(solution)/shard_map/ppermute | solution.py:241
  17.4 2.9 %fusion.28 = (f16[512,512]{1,0:T(8,128)(2,1)S(1)}, f32[512,512]{1,0:T(8,128)S(1)}) fusion(bf16[512,1536]{1,0:T(8,128)(2,1)} %get-tuple-element.12), kind=kOutput, calls=%fused_computation.64 | convolution fusion | flops 805568512 | bytes 3145728 | tf_op jit(solution)/shard_map/dot_general | solution.py:220
  20.3 1.3 collective-permute-start.6
  21.7 1.4 %copy-done.1 = bf16[512,1536]{1,0:T(8,128)(2,1)S(1)} copy-done((bf16[512,1536]{1,0:T(8,128)(2,1)S(1)}, bf16[512,1536]{1,0:T(8,128)(2,1)}, u32[]{:S(2)}) %copy-start.1) | copy-done | bytes 1572888
  23.7 0.6 fusion.29
  24.4 1.3 collective-permute-start.7
  25.7 11.2 %collective-permute-done.6 = f16[512,512]{1,0:T(8,128)(2,1)S(1)} collective-permute-done((f16[512,512]{1,0:T(8,128)(2,1)S(1)}, f16[512,512]{1,0:T(8,128)(2,1)S(1)}, u32[]{:S(2)}, u32[]{:S(2)}) %collective-permute-start.6) | collective-permute-done | bytes 524320 | tf_op jit(solution)/shard_map/ppermute | solution.py:267
  37.0 0.6 fusion.31
  37.7 2.0 %collective-permute-start.9 = (f16[512,512]{1,0:T(8,128)(2,1)S(1)}, f16[512,512]{1,0:T(8,128)(2,1)S(1)}, u32[]{:S(2)}, u32[]{:S(2)}) collective-permute-start(f16[512,512]{1,0:T(8,128)(2,1)S(1)} %get-tuple-element.27), channel_id=1, source_target_pairs={{2,0},{6,4},{10,9},{14,13},{17,18},{21,22},{25,27},{29,31}} | collective-permute-start | bytes 1572872 | tf_op jit(solution)/shard_map/ppermute | solution.py:267
  39.7 2.2 %collective-permute-start.11 = (f16[512,256]{1,0:T(8,128)(2,1)S(1)}, f16[512,256]{1,0:T(8,128)(2,1)S(1)}, u32[]{:S(2)}, u32[]{:S(2)}) collective-permute-start(f16[512,256]{1,0:T(8,128)(2,1)S(1)} %get-tuple-element.44), channel_id=1, source_target_pairs={{1,0},{3,2},{5,4},{7,6},{8,9},{10,11},{12,13},{14,15},{17,16},{19,... | collective-permute-start | bytes 786440 | tf_op jit(solution)/shard_map/ppermute | solution.py:267
  41.9 2.3 %collective-permute-start.12 = (bf16[272,1536]{1,0:T(8,128)(2,1)S(1)}, bf16[272,1536]{1,0:T(8,128)(2,1)S(1)}, u32[]{:S(2)}, u32[]{:S(2)}) collective-permute-start(bf16[272,1536]{1,0:T(8,128)(2,1)S(1)} %shard_map.29), channel_id=1, source_target_pairs={{16,0},{17,1},{18,2},{19,3},{20,4},{21,5},{22,6},{23,7},{28,8},{29... | collective-permute-start | bytes 2506760 | tf_op jit(solution)/shard_map/ppermute | solution.py:241
  44.4 0.6 fusion.30
  45.0 1.3 collective-permute-start.10
  46.3 3.0 %collective-permute-done.9 = f16[512,512]{1,0:T(8,128)(2,1)S(1)} collective-permute-done((f16[512,512]{1,0:T(8,128)(2,1)S(1)}, f16[512,512]{1,0:T(8,128)(2,1)S(1)}, u32[]{:S(2)}, u32[]{:S(2)}) %collective-permute-start.9) | collective-permute-done | bytes 524320 | tf_op jit(solution)/shard_map/ppermute | solution.py:267
  49.3 4.1 %collective-permute-start.13 = (f16[256,512]{1,0:T(8,128)(2,1)S(1)}, f16[256,512]{1,0:T(8,128)(2,1)S(1)}, u32[]{:S(2)}, u32[]{:S(2)}) collective-permute-start(f16[256,512]{1,0:T(8,128)(2,1)S(1)} %get-tuple-element.25), channel_id=1, source_target_pairs={{2,0},{6,4},{10,9},{14,13},{17,18},{21,22},{25,27},{29,31}} | collective-permute-start | bytes 786440 | tf_op jit(solution)/shard_map/ppermute | solution.py:267
  53.7 3.8 %collective-permute-start.16 = (f16[512,256]{1,0:T(8,128)(2,1)S(1)}, f16[512,256]{1,0:T(8,128)(2,1)S(1)}, u32[]{:S(2)}, u32[]{:S(2)}) collective-permute-start(f16[512,256]{1,0:T(8,128)(2,1)S(1)} %get-tuple-element.23), channel_id=1, source_target_pairs={{2,1},{6,5},{10,8},{14,12},{17,19},{21,23},{25,26},{29,30}} | collective-permute-start | bytes 786440 | tf_op jit(solution)/shard_map/ppermute | solution.py:267
  57.6 0.7 collective-permute-start.17
  58.3 4.2 %collective-permute-done.8.refs_0_ = bf16[272,1536]{1,0:T(8,128)(2,1)S(1)} collective-permute-done((bf16[272,1536]{1,0:T(8,128)(2,1)S(1)}, bf16[272,1536]{1,0:T(8,128)(2,1)S(1)}, u32[]{:S(2)}, u32[]{:S(2)}) %collective-permute-start.8) | collective-permute-done | bytes 835616 | tf_op jit(solution)/shard_map/ppermute | solution.py:241
  62.6 0.6 fusion.32
  63.4 0.6 fusion.33
  64.2 1.3 collective-permute-start.15
  65.5 4.0 %collective-permute-start.18 = (f16[512,256]{1,0:T(8,128)(2,1)S(1)}, f16[512,256]{1,0:T(8,128)(2,1)S(1)}, u32[]{:S(2)}, u32[]{:S(2)}) collective-permute-start(f16[512,256]{1,0:T(8,128)(2,1)S(1)} %get-tuple-element.48), channel_id=1, source_target_pairs={{1,0},{3,2},{5,4},{7,6},{8,9},{10,11},{12,13},{14,15},{17,16},{19,... | collective-permute-start | bytes 786440 | tf_op jit(solution)/shard_map/ppermute | solution.py:267
  69.5 1.0 fusion.34
  70.5 1.9 %collective-permute-start.19 = (f16[512,512]{1,0:T(8,128)(2,1)S(1)}, f16[512,512]{1,0:T(8,128)(2,1)S(1)}, u32[]{:S(2)}, u32[]{:S(2)}) collective-permute-start(f16[512,512]{1,0:T(8,128)(2,1)S(1)} %get-tuple-element.50), channel_id=1, source_target_pairs={{0,1},{3,2},{4,5},{7,6},{8,9},{9,8},{10,11},{11,10},{12,13},{13,12... | collective-permute-start | bytes 1572872 | tf_op jit(solution)/shard_map/ppermute | solution.py:267
  72.5 0.6 fusion.12.first_e_ref
  73.1 4.7 %collective-permute-start.14 = (f32[264,512]{1,0:T(8,128)S(1)}, f32[264,512]{1,0:T(8,128)S(1)}, u32[]{:S(2)}, u32[]{:S(2)}) collective-permute-start(f32[264,512]{1,0:T(8,128)S(1)} %pad_maximum_fusion.5), channel_id=1, source_target_pairs={{0,4},{4,0},{8,12},{12,8},{16,20},{20,16},{24,28},{28,24},{1,5},{5... | collective-permute-start | bytes 1622024 | tf_op jit(solution)/shard_map/ppermute | solution.py:50
  78.3 5.2 %collective-permute-start.20 = (f16[512,256]{1,0:T(8,128)(2,1)S(1)}, f16[512,256]{1,0:T(8,128)(2,1)S(1)}, u32[]{:S(2)}, u32[]{:S(2)}) collective-permute-start(f16[512,256]{1,0:T(8,128)(2,1)S(1)} %get-tuple-element.19), channel_id=1, source_target_pairs={{2,1},{6,5},{10,8},{14,12},{17,19},{21,23},{25,26},{29,30}} | collective-permute-start | bytes 786440 | tf_op jit(solution)/shard_map/ppermute | solution.py:267
  83.4 0.7 collective-permute-start.21
  84.3 9.7 %collective-permute-done.20 = f16[512,256]{1,0:T(8,128)(2,1)S(1)} collective-permute-done((f16[512,256]{1,0:T(8,128)(2,1)S(1)}, f16[512,256]{1,0:T(8,128)(2,1)S(1)}, u32[]{:S(2)}, u32[]{:S(2)}) %collective-permute-start.20) | collective-permute-done | bytes 262176 | tf_op jit(solution)/shard_map/ppermute | solution.py:267
  94.2 5.0 %collective-permute-start.24 = (f16[512,512]{1,0:T(8,128)(2,1)S(1)}, f16[512,512]{1,0:T(8,128)(2,1)S(1)}, u32[]{:S(2)}, u32[]{:S(2)}) collective-permute-start(f16[512,512]{1,0:T(8,128)(2,1)S(1)} %get-tuple-element.15), channel_id=1, source_target_pairs={{1,2},{2,1},{5,6},{6,5},{9,11},{10,8},{13,15},{14,12},{17,19},{18,... | collective-permute-start | bytes 1572872 | tf_op jit(solution)/shard_map/ppermute | solution.py:267
  99.3 1.3 select_add_fusion
  100.8 0.7 collective-permute-start.22
  101.5 0.7 collective-permute-start.23
  102.3 6.6 %collective-permute-done.24 = f16[512,512]{1,0:T(8,128)(2,1)S(1)} collective-permute-done((f16[512,512]{1,0:T(8,128)(2,1)S(1)}, f16[512,512]{1,0:T(8,128)(2,1)S(1)}, u32[]{:S(2)}, u32[]{:S(2)}) %collective-permute-start.24) | collective-permute-done | bytes 524320 | tf_op jit(solution)/shard_map/ppermute | solution.py:267
  109.3 1.3 collective-permute-start.25
  110.6 1.3 collective-permute-start.26
  112.2 0.6 fusion.14.second_e_ref
  112.9 1.7 %slice_add_fusion = (f32[512,512]{1,0:T(8,128)}, f32[512,512]{1,0:T(8,128)}) fusion(f32[528,512]{1,0:T(8,128)S(1)} %convert_element_type.169, f32[528,512]{1,0:T(8,128)S(1)} %convert_element_type.167, f32[256,512]{1,0:T(8,128)S(1)} %convert_add_fusion.10.refs_1_, f32[256,512]{1,0:T(8,128)S(1)} %slice.61, pred[]{:T(512)S(6)} %eq.32, pred[]{:T(512)S(6)} %eq.16, ...), kind=kLoop, calls=%fused_computation.6 | loop fusion | flops 2097152 | bytes 5242883 | tf_op jit(solution)/shard_map/add | solution.py:354
  114.6 9.9 %collective-permute-done.25 = f16[528,512]{1,0:T(8,128)(2,1)S(1)} collective-permute-done((f16[528,512]{1,0:T(8,128)(2,1)S(1)}, f16[528,512]{1,0:T(8,128)(2,1)S(1)}, u32[]{:S(2)}, u32[]{:S(2)}) %collective-permute-start.25) | collective-permute-done | bytes 540704 | tf_op jit(solution)/shard_map/ppermute | solution.py:241
  124.5 1.2 convert_element_type.175.plain_e_ref.refs_3_
  125.6 1.2 convert_element_type.178.mirror_e_ref.refs_4_
  126.8 3.9 %shard_map.44 = f32[512,1024]{1,0:T(8,128)} custom-call(s32[1]{0:T(128)} %bitcast.place_ref, f32[1,512]{1,0:T(1,128)} %get-tuple-element.9.own_ref, f32[1,512]{1,0:T(1,128)} %fusion.12.first_e_ref, f32[1,512]{1,0:T(1,128)} %fusion.14.second_e_ref, f32[528,512]{1,0:T(8,128)} %convert_element_type.175.plain_e_ref.refs_3_, ...), custom_call_target="tpu_custom_call" | custom-call | tf_op jit(solution)/shard_map/pallas_call | solution.py:198
  (94 shorter events, 4.6 us)
Async XLA Ops:
  3.2 2.7 %collective-permute-start = (f32[1,512]{1,0:T(1,128)}, f32[1,512]{1,0:T(1,128)S(1)}, u32[]{:S(2)}, u32[]{:S(2)}) collective-permute-start(f32[1,512]{1,0:T(1,128)} %shard_map.17.refs_1_), channel_id=1, source_target_pairs={{0,1},{1,0},{2,3},{3,2},{4,5},{5,4},{6,7},{7,6},{8,9},{9,8},{10,11... | collective-permute-start | bytes 6152 | tf_op jit(solution)/shard_map/ppermute | solution.py:50
  3.3 3.6 %collective-permute-start.1 = (f32[1,512]{1,0:T(1,128)}, f32[1,512]{1,0:T(1,128)S(1)}, u32[]{:S(2)}, u32[]{:S(2)}) collective-permute-start(f32[1,512]{1,0:T(1,128)} %shard_map.17.refs_1_), channel_id=1, source_target_pairs={{0,2},{1,3},{2,0},{3,1},{4,6},{5,7},{6,4},{7,5},{8,10},{9,11},{10,... | collective-permute-start | bytes 6152 | tf_op jit(solution)/shard_map/ppermute | solution.py:50
  5.6 2.9 %collective-permute-start.2 = (f32[1,512]{1,0:T(1,128)}, f32[1,512]{1,0:T(1,128)S(1)}, u32[]{:S(2)}, u32[]{:S(2)}) collective-permute-start(f32[1,512]{1,0:T(1,128)} %shard_map.17.refs_1_), channel_id=1, source_target_pairs={{0,3},{1,2},{2,1},{3,0},{4,7},{5,6},{6,5},{7,4},{8,11},{9,10},{10,... | collective-permute-start | bytes 6152 | tf_op jit(solution)/shard_map/ppermute | solution.py:50
  5.8 2.8 %copy-start.3 = (f32[1,512]{1,0:T(1,128)}, f32[1,512]{1,0:T(1,128)S(1)}, u32[]{:S(2)}) copy-start(f32[1,512]{1,0:T(1,128)S(1)} %collective-permute-done.refs_2_) | copy-start | bytes 6148
  6.9 1.7 %copy-start.4 = (f32[1,512]{1,0:T(1,128)}, f32[1,512]{1,0:T(1,128)S(1)}, u32[]{:S(2)}) copy-start(f32[1,512]{1,0:T(1,128)S(1)} %collective-permute-done.1.refs_3_) | copy-start | bytes 6148
  8.6 0.6 copy-start.5
  13.5 8.2 %collective-permute-start.4 = (bf16[512,1536]{1,0:T(8,128)(2,1)}, bf16[512,1536]{1,0:T(8,128)(2,1)S(1)}, u32[]{:S(2)}, u32[]{:S(2)}) collective-permute-start(bf16[512,1536]{1,0:T(8,128)(2,1)} %get-tuple-element.12), channel_id=1, source_target_pairs={{0,4},{4,0},{8,12},{12,8},{16,20},{20,16},{24,28},{28,24},{1,5},{5... | collective-permute-start | bytes 4718600 | tf_op jit(solution)/shard_map/ppermute | solution.py:50
  15.7 5.9 %copy-start = (bf16[272,1536]{1,0:T(8,128)(2,1)S(1)}, bf16[272,1536]{1,0:T(8,128)(2,1)}, u32[]{:S(2)}) copy-start(bf16[272,1536]{1,0:T(8,128)(2,1)} %get-tuple-element.10.refs_0_) | copy-start | bytes 2506756
  15.7 21.3 %collective-permute-start.5 = (bf16[256,1536]{1,0:T(8,128)(2,1)}, bf16[256,1536]{1,0:T(8,128)(2,1)S(1)}, u32[]{:S(2)}, u32[]{:S(2)}) collective-permute-start(bf16[256,1536]{1,0:T(8,128)(2,1)} %get-tuple-element.11), channel_id=1, source_target_pairs={{16,0},{17,1},{18,2},{19,3},{20,4},{21,5},{22,6},{23,7},{28,8},{29... | collective-permute-start | bytes 2359304 | tf_op jit(solution)/shard_map/ppermute | solution.py:241
  15.9 28.4 %collective-permute-start.3 = (bf16[256,1536]{1,0:T(8,128)(2,1)}, bf16[256,1536]{1,0:T(8,128)(2,1)S(1)}, u32[]{:S(2)}, u32[]{:S(2)}) collective-permute-start(bf16[256,1536]{1,0:T(8,128)(2,1)} %get-tuple-element.11), channel_id=1, source_target_pairs={{8,0},{9,1},{10,2},{11,3},{12,4},{13,5},{14,6},{15,7},{4,8},{5,9},... | collective-permute-start | bytes 2359304 | tf_op jit(solution)/shard_map/ppermute | solution.py:241
  20.3 1.4 %copy-start.2 = (f32[1,512]{1,0:T(1,128)S(1)}, f32[1,512]{1,0:T(1,128)}, u32[]{:S(2)}) copy-start(f32[1,512]{1,0:T(1,128)} %get-tuple-element.9.own_ref) | copy-start | bytes 6148
  20.3 16.5 %collective-permute-start.6 = (f16[512,512]{1,0:T(8,128)(2,1)S(1)}, f16[512,512]{1,0:T(8,128)(2,1)S(1)}, u32[]{:S(2)}, u32[]{:S(2)}) collective-permute-start(f16[512,512]{1,0:T(8,128)(2,1)S(1)} %get-tuple-element.38), channel_id=1, source_target_pairs={{1,0},{3,2},{5,4},{7,6},{8,9},{11,10},{12,13},{15,14},{16,17},{19,... | collective-permute-start | bytes 1572872 | tf_op jit(solution)/shard_map/ppermute | solution.py:267
  21.7 1.4 %copy-start.1 = (bf16[512,1536]{1,0:T(8,128)(2,1)S(1)}, bf16[512,1536]{1,0:T(8,128)(2,1)}, u32[]{:S(2)}) copy-start(bf16[512,1536]{1,0:T(8,128)(2,1)} %get-tuple-element.12) | copy-start | bytes 4718596
  24.4 19.8 %collective-permute-start.7 = (f16[256,512]{1,0:T(8,128)(2,1)S(1)}, f16[256,512]{1,0:T(8,128)(2,1)S(1)}, u32[]{:S(2)}, u32[]{:S(2)}) collective-permute-start(f16[256,512]{1,0:T(8,128)(2,1)S(1)} %get-tuple-element.40), channel_id=1, source_target_pairs={{1,0},{3,2},{5,4},{7,6},{8,9},{11,10},{12,13},{15,14},{16,17},{19,... | collective-permute-start | bytes 786440 | tf_op jit(solution)/shard_map/ppermute | solution.py:267
  37.7 11.6 %collective-permute-start.9 = (f16[512,512]{1,0:T(8,128)(2,1)S(1)}, f16[512,512]{1,0:T(8,128)(2,1)S(1)}, u32[]{:S(2)}, u32[]{:S(2)}) collective-permute-start(f16[512,512]{1,0:T(8,128)(2,1)S(1)} %get-tuple-element.27), channel_id=1, source_target_pairs={{2,0},{6,4},{10,9},{14,13},{17,18},{21,22},{25,27},{29,31}} | collective-permute-start | bytes 1572872 | tf_op jit(solution)/shard_map/ppermute | solution.py:267
  39.7 17.9 %collective-permute-start.11 = (f16[512,256]{1,0:T(8,128)(2,1)S(1)}, f16[512,256]{1,0:T(8,128)(2,1)S(1)}, u32[]{:S(2)}, u32[]{:S(2)}) collective-permute-start(f16[512,256]{1,0:T(8,128)(2,1)S(1)} %get-tuple-element.44), channel_id=1, source_target_pairs={{1,0},{3,2},{5,4},{7,6},{8,9},{10,11},{12,13},{14,15},{17,16},{19,... | collective-permute-start | bytes 786440 | tf_op jit(solution)/shard_map/ppermute | solution.py:267
  41.9 21.5 %collective-permute-start.12 = (bf16[272,1536]{1,0:T(8,128)(2,1)S(1)}, bf16[272,1536]{1,0:T(8,128)(2,1)S(1)}, u32[]{:S(2)}, u32[]{:S(2)}) collective-permute-start(bf16[272,1536]{1,0:T(8,128)(2,1)S(1)} %shard_map.29), channel_id=1, source_target_pairs={{16,0},{17,1},{18,2},{19,3},{20,4},{21,5},{22,6},{23,7},{28,8},{29... | collective-permute-start | bytes 2506760 | tf_op jit(solution)/shard_map/ppermute | solution.py:241
  44.3 18.3 %collective-permute-start.8 = (bf16[272,1536]{1,0:T(8,128)(2,1)S(1)}, bf16[272,1536]{1,0:T(8,128)(2,1)S(1)}, u32[]{:S(2)}, u32[]{:S(2)}) collective-permute-start(bf16[272,1536]{1,0:T(8,128)(2,1)S(1)} %shard_map.24), channel_id=1, source_target_pairs={{8,0},{9,1},{10,2},{11,3},{12,4},{13,5},{14,6},{15,7},{4,8},{5,9},... | collective-permute-start | bytes 2506760 | tf_op jit(solution)/shard_map/ppermute | solution.py:241
  45.0 8.6 %collective-permute-start.10 = (f16[512,256]{1,0:T(8,128)(2,1)S(1)}, f16[512,256]{1,0:T(8,128)(2,1)S(1)}, u32[]{:S(2)}, u32[]{:S(2)}) collective-permute-start(f16[512,256]{1,0:T(8,128)(2,1)S(1)} %get-tuple-element.42), channel_id=1, source_target_pairs={{0,1},{3,2},{4,5},{7,6},{9,8},{11,10},{13,12},{15,14},{16,17},{18,... | collective-permute-start | bytes 786440 | tf_op jit(solution)/shard_map/ppermute | solution.py:267
  49.3 14.0 %collective-permute-start.13 = (f16[256,512]{1,0:T(8,128)(2,1)S(1)}, f16[256,512]{1,0:T(8,128)(2,1)S(1)}, u32[]{:S(2)}, u32[]{:S(2)}) collective-permute-start(f16[256,512]{1,0:T(8,128)(2,1)S(1)} %get-tuple-element.25), channel_id=1, source_target_pairs={{2,0},{6,4},{10,9},{14,13},{17,18},{21,22},{25,27},{29,31}} | collective-permute-start | bytes 786440 | tf_op jit(solution)/shard_map/ppermute | solution.py:267
  53.7 24.3 %collective-permute-start.16 = (f16[512,256]{1,0:T(8,128)(2,1)S(1)}, f16[512,256]{1,0:T(8,128)(2,1)S(1)}, u32[]{:S(2)}, u32[]{:S(2)}) collective-permute-start(f16[512,256]{1,0:T(8,128)(2,1)S(1)} %get-tuple-element.23), channel_id=1, source_target_pairs={{2,1},{6,5},{10,8},{14,12},{17,19},{21,23},{25,26},{29,30}} | collective-permute-start | bytes 786440 | tf_op jit(solution)/shard_map/ppermute | solution.py:267
  57.6 20.4 %collective-permute-start.17 = (f16[512,256]{1,0:T(8,128)(2,1)S(1)}, f16[512,256]{1,0:T(8,128)(2,1)S(1)}, u32[]{:S(2)}, u32[]{:S(2)}) collective-permute-start(f16[512,256]{1,0:T(8,128)(2,1)S(1)} %get-tuple-element.21), channel_id=1, source_target_pairs={{0,2},{2,0},{4,6},{6,4},{9,11},{11,9},{13,15},{15,13},{16,18},{18,... | collective-permute-start | bytes 786440 | tf_op jit(solution)/shard_map/ppermute | solution.py:267
  64.2 8.9 %collective-permute-start.15 = (f16[512,256]{1,0:T(8,128)(2,1)S(1)}, f16[512,256]{1,0:T(8,128)(2,1)S(1)}, u32[]{:S(2)}, u32[]{:S(2)}) collective-permute-start(f16[512,256]{1,0:T(8,128)(2,1)S(1)} %get-tuple-element.46), channel_id=1, source_target_pairs={{0,1},{3,2},{4,5},{7,6},{9,8},{11,10},{13,12},{15,14},{16,17},{18,... | collective-permute-start | bytes 786440 | tf_op jit(solution)/shard_map/ppermute | solution.py:267
  65.5 12.7 %collective-permute-start.18 = (f16[512,256]{1,0:T(8,128)(2,1)S(1)}, f16[512,256]{1,0:T(8,128)(2,1)S(1)}, u32[]{:S(2)}, u32[]{:S(2)}) collective-permute-start(f16[512,256]{1,0:T(8,128)(2,1)S(1)} %get-tuple-element.48), channel_id=1, source_target_pairs={{1,0},{3,2},{5,4},{7,6},{8,9},{10,11},{12,13},{14,15},{17,16},{19,... | collective-permute-start | bytes 786440 | tf_op jit(solution)/shard_map/ppermute | solution.py:267
  70.5 13.6 %collective-permute-start.19 = (f16[512,512]{1,0:T(8,128)(2,1)S(1)}, f16[512,512]{1,0:T(8,128)(2,1)S(1)}, u32[]{:S(2)}, u32[]{:S(2)}) collective-permute-start(f16[512,512]{1,0:T(8,128)(2,1)S(1)} %get-tuple-element.50), channel_id=1, source_target_pairs={{0,1},{3,2},{4,5},{7,6},{8,9},{9,8},{10,11},{11,10},{12,13},{13,12... | collective-permute-start | bytes 1572872 | tf_op jit(solution)/shard_map/ppermute | solution.py:267
  73.1 29.1 %collective-permute-start.14 = (f32[264,512]{1,0:T(8,128)S(1)}, f32[264,512]{1,0:T(8,128)S(1)}, u32[]{:S(2)}, u32[]{:S(2)}) collective-permute-start(f32[264,512]{1,0:T(8,128)S(1)} %pad_maximum_fusion.5), channel_id=1, source_target_pairs={{0,4},{4,0},{8,12},{12,8},{16,20},{20,16},{24,28},{28,24},{1,5},{5... | collective-permute-start | bytes 1622024 | tf_op jit(solution)/shard_map/ppermute | solution.py:50
  78.3 15.8 %collective-permute-start.20 = (f16[512,256]{1,0:T(8,128)(2,1)S(1)}, f16[512,256]{1,0:T(8,128)(2,1)S(1)}, u32[]{:S(2)}, u32[]{:S(2)}) collective-permute-start(f16[512,256]{1,0:T(8,128)(2,1)S(1)} %get-tuple-element.19), channel_id=1, source_target_pairs={{2,1},{6,5},{10,8},{14,12},{17,19},{21,23},{25,26},{29,30}} | collective-permute-start | bytes 786440 | tf_op jit(solution)/shard_map/ppermute | solution.py:267
  83.4 10.7 %collective-permute-start.21 = (f16[512,256]{1,0:T(8,128)(2,1)S(1)}, f16[512,256]{1,0:T(8,128)(2,1)S(1)}, u32[]{:S(2)}, u32[]{:S(2)}) collective-permute-start(f16[512,256]{1,0:T(8,128)(2,1)S(1)} %get-tuple-element.17), channel_id=1, source_target_pairs={{0,2},{2,0},{4,6},{6,4},{9,11},{11,9},{13,15},{15,13},{16,18},{18,... | collective-permute-start | bytes 786440 | tf_op jit(solution)/shard_map/ppermute | solution.py:267
  94.2 14.7 %collective-permute-start.24 = (f16[512,512]{1,0:T(8,128)(2,1)S(1)}, f16[512,512]{1,0:T(8,128)(2,1)S(1)}, u32[]{:S(2)}, u32[]{:S(2)}) collective-permute-start(f16[512,512]{1,0:T(8,128)(2,1)S(1)} %get-tuple-element.15), channel_id=1, source_target_pairs={{1,2},{2,1},{5,6},{6,5},{9,11},{10,8},{13,15},{14,12},{17,19},{18,... | collective-permute-start | bytes 1572872 | tf_op jit(solution)/shard_map/ppermute | solution.py:267
  100.8 11.1 %collective-permute-start.22 = (f16[528,512]{1,0:T(8,128)(2,1)S(1)}, f16[528,512]{1,0:T(8,128)(2,1)S(1)}, u32[]{:S(2)}, u32[]{:S(2)}) collective-permute-start(f16[528,512]{1,0:T(8,128)(2,1)S(1)} %get-tuple-element.36), channel_id=1, source_target_pairs={{12,1},{8,5},{1,8},{5,12},{30,19},{26,23},{19,26},{23,30}} | collective-permute-start | bytes 1622024 | tf_op jit(solution)/shard_map/ppermute | solution.py:241
  101.5 10.5 %collective-permute-start.23 = (f16[528,512]{1,0:T(8,128)(2,1)S(1)}, f16[528,512]{1,0:T(8,128)(2,1)S(1)}, u32[]{:S(2)}, u32[]{:S(2)}) collective-permute-start(f16[528,512]{1,0:T(8,128)(2,1)S(1)} %get-tuple-element.37), channel_id=1, source_target_pairs={{22,2},{18,6},{27,11},{31,15},{0,16},{4,20},{13,25},{9,29}} | collective-permute-start | bytes 1622024 | tf_op jit(solution)/shard_map/ppermute | solution.py:241
  109.3 15.1 %collective-permute-start.25 = (f16[528,512]{1,0:T(8,128)(2,1)S(1)}, f16[528,512]{1,0:T(8,128)(2,1)S(1)}, u32[]{:S(2)}, u32[]{:S(2)}) collective-permute-start(f16[528,512]{1,0:T(8,128)(2,1)S(1)} %get-tuple-element.35), channel_id=1, source_target_pairs={{15,3},{11,7},{2,10},{6,14},{29,17},{25,21},{16,24},{20,28}} | collective-permute-start | bytes 1622024 | tf_op jit(solution)/shard_map/ppermute | solution.py:241
  110.6 15.0 %collective-permute-start.26 = (f16[528,512]{1,0:T(8,128)(2,1)S(1)}, f16[528,512]{1,0:T(8,128)(2,1)S(1)}, u32[]{:S(2)}, u32[]{:S(2)}) collective-permute-start(f16[528,512]{1,0:T(8,128)(2,1)S(1)} %get-tuple-element.34), channel_id=1, source_target_pairs={{23,3},{19,7},{26,10},{30,14},{1,17},{5,21},{12,24},{8,28}} | collective-permute-start | bytes 1622024 | tf_op jit(solution)/shard_map/ppermute | solution.py:241

commit v6 on v5

--- a/solution.py
+++ b/solution.py
@@ -41,8 +41,8 @@
     ("send", ("x", 0), 1),
     ("send", ("y", 0), 1),
     ("second", ("xy", 0), 1),
-    ("send", ("plain", 0), 1),
-    ("send", ("mirror", 0), 1),
+    ("send", ("plain", 0), 0),
+    ("send", ("mirror", 0), 0),
 )
 
 

time: 133 us -> 132 us (level)
  no operation moved by 1% of the time
where the time goes in v6:
time: 132 us; the launch traced here: 130 us
  starting transfers between devices  52.4 us (40%)
  waiting for transfers between devices  47.1 us (36%)
  Pallas kernels  11.5 us (9%)
  other arithmetic  8.91 us (7%)
  matrix products  7.52 us (6%)
  local copies, waits for them, and re-layouts  2.23 us (2%)
    ppermute x14, starting transfers between devices, send(): lax.ppermute(carry[name].astype(jnp.float16), AXES, stages[name[0]][stage])  34.8 us
    ppermute x14, waiting for transfers between devices, send(): lax.ppermute(carry[name].astype(jnp.float16), AXES, stages[name[0]][stage])  30.3 us
    ppermute x8, waiting for transfers between devices, receive(): return lax.ppermute(value, AXES, pairs)  14 us
    ppermute x5, starting transfers between devices, hop(): return lax.ppermute(x, axis, [(i, i ^ mask) for i in range(size)])  9.53 us
    ppermute x8, starting transfers between devices, receive(): return lax.ppermute(value, AXES, pairs)  8.09 us
    dot_general x8, matrix products, product(): lax.dot_general(rows, columns, (((1,), (1,)), ((), ())), preferred_elemen...  7.52 us
    pallas_call x1, Pallas kernels, normalize(): pl.pallas_call(lambda *refs: norm_kernel(columns * nr, *refs), grid=(CHUN...  4.36 us
    pallas_call x1, Pallas kernels, assemble(): pl.pallas_call(assemble_kernel, grid=(STEPS,), in_specs=[pl.BlockSpec(mem...  3.91 us
  transfers between devices with their start and end apart: 27, of which 8 were waited for; matrix products, arithmetic and copies ran while one was open for 12% of the time, Pallas kernels for 0%

profile of v6, /device:TPU:13, one launch (start us, length us, event | category | flops | bytes accessed | tf_op | source)
XLA Modules:
  0.0 130.3 jit_solution(15905824919408501401)
XLA Ops:
  0.0 3.1 %shard_map.17.refs_1_ = f32[1,512]{1,0:T(1,128)} custom-call(f32[512,1,1536]{2,1,0:T(1,128)} %refs_0_.1), custom_call_target="tpu_custom_call" | custom-call | tf_op jit(solution)/shard_map/pallas_call | solution.py:120
  3.3 2.3 %collective-permute-start.1 = (f32[1,512]{1,0:T(1,128)}, f32[1,512]{1,0:T(1,128)S(1)}, u32[]{:S(2)}, u32[]{:S(2)}) collective-permute-start(f32[1,512]{1,0:T(1,128)} %shard_map.17.refs_1_), channel_id=1, source_target_pairs={{0,2},{1,3},{2,0},{3,1},{4,6},{5,7},{6,4},{7,5},{8,10},{9,11},{10,... | collective-permute-start | bytes 6152 | tf_op jit(solution)/shard_map/ppermute | solution.py:50
  5.8 1.1 collective-permute-done.1.refs_3_
  6.9 1.7 %collective-permute-done.2.refs_4_ = f32[1,512]{1,0:T(1,128)S(1)} collective-permute-done((f32[1,512]{1,0:T(1,128)}, f32[1,512]{1,0:T(1,128)S(1)}, u32[]{:S(2)}, u32[]{:S(2)}) %collective-permute-start.2) | collective-permute-done | bytes 2080 | tf_op jit(solution)/shard_map/ppermute | solution.py:50
  9.2 4.4 %shard_map.18 = (bf16[512,1536]{1,0:T(8,128)(2,1)}, f32[1,512]{1,0:T(1,128)}, bf16[256,1536]{1,0:T(8,128)(2,1)}, bf16[272,1536]{1,0:T(8,128)(2,1)}) custom-call(f32[512,1,1536]{2,1,0:T(1,128)} %refs_0_.1, f32[1,512]{1,0:T(1,128)} %shard_map.17.refs_1_, f32[1,512]{1,0:T(1,128)} %copy-done.3, f32[1,512]{1,0:T(1,128)} %copy-done.4, f32[1,512]{1,0:T(1,128)} %copy-done.5), custom_call_target="tpu_custom_call" | custom-call | tf_op jit(solution)/shard_map/pallas_call | solution.py:123
  13.5 2.2 %collective-permute-start.4 = (bf16[512,1536]{1,0:T(8,128)(2,1)}, bf16[512,1536]{1,0:T(8,128)(2,1)S(1)}, u32[]{:S(2)}, u32[]{:S(2)}) collective-permute-start(bf16[512,1536]{1,0:T(8,128)(2,1)} %get-tuple-element.12), channel_id=1, source_target_pairs={{0,4},{4,0},{8,12},{12,8},{16,20},{20,16},{24,28},{28,24},{1,5},{5... | collective-permute-start | bytes 4718600 | tf_op jit(solution)/shard_map/ppermute | solution.py:50
  15.9 1.5 %collective-permute-start.3 = (bf16[256,1536]{1,0:T(8,128)(2,1)}, bf16[256,1536]{1,0:T(8,128)(2,1)S(1)}, u32[]{:S(2)}, u32[]{:S(2)}) collective-permute-start(bf16[256,1536]{1,0:T(8,128)(2,1)} %get-tuple-element.11), channel_id=1, source_target_pairs={{8,0},{9,1},{10,2},{11,3},{12,4},{13,5},{14,6},{15,7},{4,8},{5,9},... | collective-permute-start | bytes 2359304 | tf_op jit(solution)/shard_map/ppermute | solution.py:241
  17.4 2.9 %fusion.27 = (f16[512,512]{1,0:T(8,128)(2,1)S(1)}, f32[512,512]{1,0:T(8,128)S(1)}) fusion(bf16[512,1536]{1,0:T(8,128)(2,1)} %get-tuple-element.12), kind=kOutput, calls=%fused_computation.63 | convolution fusion | flops 805568512 | bytes 3145728 | tf_op jit(solution)/shard_map/dot_general | solution.py:220
  20.3 1.3 collective-permute-start.6
  21.7 1.4 %copy-done.1 = bf16[512,1536]{1,0:T(8,128)(2,1)S(1)} copy-done((bf16[512,1536]{1,0:T(8,128)(2,1)S(1)}, bf16[512,1536]{1,0:T(8,128)(2,1)}, u32[]{:S(2)}) %copy-start.1) | copy-done | bytes 1572888
  23.1 0.6 fusion.7
  23.7 0.6 fusion.28
  24.4 1.3 collective-permute-start.7
  25.7 11.2 %collective-permute-done.6 = f16[512,512]{1,0:T(8,128)(2,1)S(1)} collective-permute-done((f16[512,512]{1,0:T(8,128)(2,1)S(1)}, f16[512,512]{1,0:T(8,128)(2,1)S(1)}, u32[]{:S(2)}, u32[]{:S(2)}) %collective-permute-start.6) | collective-permute-done | bytes 524320 | tf_op jit(solution)/shard_map/ppermute | solution.py:267
  37.0 0.6 fusion.30
  37.7 2.0 %collective-permute-start.9 = (f16[512,512]{1,0:T(8,128)(2,1)S(1)}, f16[512,512]{1,0:T(8,128)(2,1)S(1)}, u32[]{:S(2)}, u32[]{:S(2)}) collective-permute-start(f16[512,512]{1,0:T(8,128)(2,1)S(1)} %get-tuple-element.25), channel_id=1, source_target_pairs={{2,0},{6,4},{10,9},{14,13},{17,18},{21,22},{25,27},{29,31}} | collective-permute-start | bytes 1572872 | tf_op jit(solution)/shard_map/ppermute | solution.py:267
  39.7 2.2 %collective-permute-start.11 = (f16[512,256]{1,0:T(8,128)(2,1)S(1)}, f16[512,256]{1,0:T(8,128)(2,1)S(1)}, u32[]{:S(2)}, u32[]{:S(2)}) collective-permute-start(f16[512,256]{1,0:T(8,128)(2,1)S(1)} %get-tuple-element.42), channel_id=1, source_target_pairs={{1,0},{3,2},{5,4},{7,6},{8,9},{10,11},{12,13},{14,15},{17,16},{19,... | collective-permute-start | bytes 786440 | tf_op jit(solution)/shard_map/ppermute | solution.py:267
  41.9 2.3 %collective-permute-start.12 = (bf16[272,1536]{1,0:T(8,128)(2,1)S(1)}, bf16[272,1536]{1,0:T(8,128)(2,1)S(1)}, u32[]{:S(2)}, u32[]{:S(2)}) collective-permute-start(bf16[272,1536]{1,0:T(8,128)(2,1)S(1)} %shard_map.29), channel_id=1, source_target_pairs={{16,0},{17,1},{18,2},{19,3},{20,4},{21,5},{22,6},{23,7},{28,8},{29... | collective-permute-start | bytes 2506760 | tf_op jit(solution)/shard_map/ppermute | solution.py:241
  44.4 0.6 fusion.29
  45.0 1.3 collective-permute-start.10
  46.3 3.0 %collective-permute-done.9 = f16[512,512]{1,0:T(8,128)(2,1)S(1)} collective-permute-done((f16[512,512]{1,0:T(8,128)(2,1)S(1)}, f16[512,512]{1,0:T(8,128)(2,1)S(1)}, u32[]{:S(2)}, u32[]{:S(2)}) %collective-permute-start.9) | collective-permute-done | bytes 524320 | tf_op jit(solution)/shard_map/ppermute | solution.py:267
  49.3 4.1 %collective-permute-start.13 = (f16[256,512]{1,0:T(8,128)(2,1)S(1)}, f16[256,512]{1,0:T(8,128)(2,1)S(1)}, u32[]{:S(2)}, u32[]{:S(2)}) collective-permute-start(f16[256,512]{1,0:T(8,128)(2,1)S(1)} %get-tuple-element.23), channel_id=1, source_target_pairs={{2,0},{6,4},{10,9},{14,13},{17,18},{21,22},{25,27},{29,31}} | collective-permute-start | bytes 786440 | tf_op jit(solution)/shard_map/ppermute | solution.py:267
  53.7 3.8 %collective-permute-start.16 = (f16[512,256]{1,0:T(8,128)(2,1)S(1)}, f16[512,256]{1,0:T(8,128)(2,1)S(1)}, u32[]{:S(2)}, u32[]{:S(2)}) collective-permute-start(f16[512,256]{1,0:T(8,128)(2,1)S(1)} %get-tuple-element.21), channel_id=1, source_target_pairs={{2,1},{6,5},{10,8},{14,12},{17,19},{21,23},{25,26},{29,30}} | collective-permute-start | bytes 786440 | tf_op jit(solution)/shard_map/ppermute | solution.py:267
  57.7 0.7 collective-permute-start.17
  58.3 4.3 %collective-permute-done.8.refs_0_ = bf16[272,1536]{1,0:T(8,128)(2,1)S(1)} collective-permute-done((bf16[272,1536]{1,0:T(8,128)(2,1)S(1)}, bf16[272,1536]{1,0:T(8,128)(2,1)S(1)}, u32[]{:S(2)}, u32[]{:S(2)}) %collective-permute-start.8) | collective-permute-done | bytes 835616 | tf_op jit(solution)/shard_map/ppermute | solution.py:241
  62.6 0.6 fusion.31
  63.4 0.6 fusion.32
  64.2 1.3 collective-permute-start.15
  65.5 4.0 %collective-permute-start.18 = (f16[512,256]{1,0:T(8,128)(2,1)S(1)}, f16[512,256]{1,0:T(8,128)(2,1)S(1)}, u32[]{:S(2)}, u32[]{:S(2)}) collective-permute-start(f16[512,256]{1,0:T(8,128)(2,1)S(1)} %get-tuple-element.46), channel_id=1, source_target_pairs={{1,0},{3,2},{5,4},{7,6},{8,9},{10,11},{12,13},{14,15},{17,16},{19,... | collective-permute-start | bytes 786440 | tf_op jit(solution)/shard_map/ppermute | solution.py:267
  69.5 1.0 fusion.33
  70.5 1.9 %collective-permute-start.19 = (f16[512,512]{1,0:T(8,128)(2,1)S(1)}, f16[512,512]{1,0:T(8,128)(2,1)S(1)}, u32[]{:S(2)}, u32[]{:S(2)}) collective-permute-start(f16[512,512]{1,0:T(8,128)(2,1)S(1)} %get-tuple-element.48), channel_id=1, source_target_pairs={{0,1},{3,2},{4,5},{7,6},{8,9},{9,8},{10,11},{11,10},{12,13},{13,12... | collective-permute-start | bytes 1572872 | tf_op jit(solution)/shard_map/ppermute | solution.py:267
  73.1 4.7 %collective-permute-start.14 = (f32[264,512]{1,0:T(8,128)S(1)}, f32[264,512]{1,0:T(8,128)S(1)}, u32[]{:S(2)}, u32[]{:S(2)}) collective-permute-start(f32[264,512]{1,0:T(8,128)S(1)} %pad_maximum_fusion.5), channel_id=1, source_target_pairs={{0,4},{4,0},{8,12},{12,8},{16,20},{20,16},{24,28},{28,24},{1,5},{5... | collective-permute-start | bytes 1622024 | tf_op jit(solution)/shard_map/ppermute | solution.py:50
  78.2 5.2 %collective-permute-start.20 = (f16[512,256]{1,0:T(8,128)(2,1)S(1)}, f16[512,256]{1,0:T(8,128)(2,1)S(1)}, u32[]{:S(2)}, u32[]{:S(2)}) collective-permute-start(f16[512,256]{1,0:T(8,128)(2,1)S(1)} %get-tuple-element.17), channel_id=1, source_target_pairs={{2,1},{6,5},{10,8},{14,12},{17,19},{21,23},{25,26},{29,30}} | collective-permute-start | bytes 786440 | tf_op jit(solution)/shard_map/ppermute | solution.py:267
  83.5 0.7 collective-permute-start.21
  84.4 9.7 %collective-permute-done.20 = f16[512,256]{1,0:T(8,128)(2,1)S(1)} collective-permute-done((f16[512,256]{1,0:T(8,128)(2,1)S(1)}, f16[512,256]{1,0:T(8,128)(2,1)S(1)}, u32[]{:S(2)}, u32[]{:S(2)}) %collective-permute-start.20) | collective-permute-done | bytes 262176 | tf_op jit(solution)/shard_map/ppermute | solution.py:267
  94.1 5.0 %collective-permute-start.24 = (f16[512,512]{1,0:T(8,128)(2,1)S(1)}, f16[512,512]{1,0:T(8,128)(2,1)S(1)}, u32[]{:S(2)}, u32[]{:S(2)}) collective-permute-start(f16[512,512]{1,0:T(8,128)(2,1)S(1)} %get-tuple-element.13), channel_id=1, source_target_pairs={{1,2},{2,1},{5,6},{6,5},{9,11},{10,8},{13,15},{14,12},{17,19},{18,... | collective-permute-start | bytes 1572872 | tf_op jit(solution)/shard_map/ppermute | solution.py:267
  99.3 1.3 select_add_fusion
  100.8 0.7 collective-permute-start.22
  101.5 0.7 collective-permute-start.23
  102.3 6.5 %collective-permute-done.24 = f16[512,512]{1,0:T(8,128)(2,1)S(1)} collective-permute-done((f16[512,512]{1,0:T(8,128)(2,1)S(1)}, f16[512,512]{1,0:T(8,128)(2,1)S(1)}, u32[]{:S(2)}, u32[]{:S(2)}) %collective-permute-start.24) | collective-permute-done | bytes 524320 | tf_op jit(solution)/shard_map/ppermute | solution.py:267
  109.2 1.3 collective-permute-start.25
  110.5 1.3 collective-permute-start.26
  112.1 0.6 fusion.14.second_e_ref
  112.7 1.7 %slice_add_fusion = (f32[512,512]{1,0:T(8,128)}, f32[512,512]{1,0:T(8,128)}) fusion(f32[528,512]{1,0:T(8,128)S(1)} %convert_element_type.169, f32[528,512]{1,0:T(8,128)S(1)} %convert_element_type.167, f32[256,512]{1,0:T(8,128)S(1)} %convert_add_fusion.9.refs_1_, f32[256,512]{1,0:T(8,128)S(1)} %slice.61, pred[]{:T(512)S(6)} %eq.32, pred[]{:T(512)S(6)} %eq.16, ...), kind=kLoop, calls=%fused_computation.6 | loop fusion | flops 2097152 | bytes 5242883 | tf_op jit(solution)/shard_map/add | solution.py:354
  114.4 9.7 %collective-permute-done.25 = f16[528,512]{1,0:T(8,128)(2,1)S(1)} collective-permute-done((f16[528,512]{1,0:T(8,128)(2,1)S(1)}, f16[528,512]{1,0:T(8,128)(2,1)S(1)}, u32[]{:S(2)}, u32[]{:S(2)}) %collective-permute-start.25) | collective-permute-done | bytes 540704 | tf_op jit(solution)/shard_map/ppermute | solution.py:241
  124.1 1.2 convert_element_type.175.plain_e_ref.refs_3_
  125.3 1.1 convert_element_type.178.mirror_e_ref.refs_4_
  126.4 3.9 %shard_map.42 = f32[512,1024]{1,0:T(8,128)} custom-call(s32[1]{0:T(128)} %bitcast.place_ref, f32[1,512]{1,0:T(1,128)} %get-tuple-element.9.own_ref, f32[1,512]{1,0:T(1,128)} %fusion.12.first_e_ref, f32[1,512]{1,0:T(1,128)} %fusion.14.second_e_ref, f32[528,512]{1,0:T(8,128)} %convert_element_type.175.plain_e_ref.refs_3_, ...), custom_call_target="tpu_custom_call" | custom-call | tf_op jit(solution)/shard_map/pallas_call | solution.py:198
  (90 shorter events, 4.5 us)
Async XLA Ops:
  3.1 2.7 %collective-permute-start = (f32[1,512]{1,0:T(1,128)}, f32[1,512]{1,0:T(1,128)S(1)}, u32[]{:S(2)}, u32[]{:S(2)}) collective-permute-start(f32[1,512]{1,0:T(1,128)} %shard_map.17.refs_1_), channel_id=1, source_target_pairs={{0,1},{1,0},{2,3},{3,2},{4,5},{5,4},{6,7},{7,6},{8,9},{9,8},{10,11... | collective-permute-start | bytes 6152 | tf_op jit(solution)/shard_map/ppermute | solution.py:50
  3.3 3.6 %collective-permute-start.1 = (f32[1,512]{1,0:T(1,128)}, f32[1,512]{1,0:T(1,128)S(1)}, u32[]{:S(2)}, u32[]{:S(2)}) collective-permute-start(f32[1,512]{1,0:T(1,128)} %shard_map.17.refs_1_), channel_id=1, source_target_pairs={{0,2},{1,3},{2,0},{3,1},{4,6},{5,7},{6,4},{7,5},{8,10},{9,11},{10,... | collective-permute-start | bytes 6152 | tf_op jit(solution)/shard_map/ppermute | solution.py:50
  5.6 2.9 %collective-permute-start.2 = (f32[1,512]{1,0:T(1,128)}, f32[1,512]{1,0:T(1,128)S(1)}, u32[]{:S(2)}, u32[]{:S(2)}) collective-permute-start(f32[1,512]{1,0:T(1,128)} %shard_map.17.refs_1_), channel_id=1, source_target_pairs={{0,3},{1,2},{2,1},{3,0},{4,7},{5,6},{6,5},{7,4},{8,11},{9,10},{10,... | collective-permute-start | bytes 6152 | tf_op jit(solution)/shard_map/ppermute | solution.py:50
  5.8 2.8 %copy-start.3 = (f32[1,512]{1,0:T(1,128)}, f32[1,512]{1,0:T(1,128)S(1)}, u32[]{:S(2)}) copy-start(f32[1,512]{1,0:T(1,128)S(1)} %collective-permute-done.refs_2_) | copy-start | bytes 6148
  6.9 1.7 %copy-start.4 = (f32[1,512]{1,0:T(1,128)}, f32[1,512]{1,0:T(1,128)S(1)}, u32[]{:S(2)}) copy-start(f32[1,512]{1,0:T(1,128)S(1)} %collective-permute-done.1.refs_3_) | copy-start | bytes 6148
  8.6 0.6 copy-start.5
  13.5 8.2 %collective-permute-start.4 = (bf16[512,1536]{1,0:T(8,128)(2,1)}, bf16[512,1536]{1,0:T(8,128)(2,1)S(1)}, u32[]{:S(2)}, u32[]{:S(2)}) collective-permute-start(bf16[512,1536]{1,0:T(8,128)(2,1)} %get-tuple-element.12), channel_id=1, source_target_pairs={{0,4},{4,0},{8,12},{12,8},{16,20},{20,16},{24,28},{28,24},{1,5},{5... | collective-permute-start | bytes 4718600 | tf_op jit(solution)/shard_map/ppermute | solution.py:50
  15.7 5.9 %copy-start = (bf16[272,1536]{1,0:T(8,128)(2,1)S(1)}, bf16[272,1536]{1,0:T(8,128)(2,1)}, u32[]{:S(2)}) copy-start(bf16[272,1536]{1,0:T(8,128)(2,1)} %get-tuple-element.10.refs_0_) | copy-start | bytes 2506756
  15.7 21.3 %collective-permute-start.5 = (bf16[256,1536]{1,0:T(8,128)(2,1)}, bf16[256,1536]{1,0:T(8,128)(2,1)S(1)}, u32[]{:S(2)}, u32[]{:S(2)}) collective-permute-start(bf16[256,1536]{1,0:T(8,128)(2,1)} %get-tuple-element.11), channel_id=1, source_target_pairs={{16,0},{17,1},{18,2},{19,3},{20,4},{21,5},{22,6},{23,7},{28,8},{29... | collective-permute-start | bytes 2359304 | tf_op jit(solution)/shard_map/ppermute | solution.py:241
  15.9 28.4 %collective-permute-start.3 = (bf16[256,1536]{1,0:T(8,128)(2,1)}, bf16[256,1536]{1,0:T(8,128)(2,1)S(1)}, u32[]{:S(2)}, u32[]{:S(2)}) collective-permute-start(bf16[256,1536]{1,0:T(8,128)(2,1)} %get-tuple-element.11), channel_id=1, source_target_pairs={{8,0},{9,1},{10,2},{11,3},{12,4},{13,5},{14,6},{15,7},{4,8},{5,9},... | collective-permute-start | bytes 2359304 | tf_op jit(solution)/shard_map/ppermute | solution.py:241
  20.3 1.4 %copy-start.2 = (f32[1,512]{1,0:T(1,128)S(1)}, f32[1,512]{1,0:T(1,128)}, u32[]{:S(2)}) copy-start(f32[1,512]{1,0:T(1,128)} %get-tuple-element.9.own_ref) | copy-start | bytes 6148
  20.3 16.5 %collective-permute-start.6 = (f16[512,512]{1,0:T(8,128)(2,1)S(1)}, f16[512,512]{1,0:T(8,128)(2,1)S(1)}, u32[]{:S(2)}, u32[]{:S(2)}) collective-permute-start(f16[512,512]{1,0:T(8,128)(2,1)S(1)} %get-tuple-element.36), channel_id=1, source_target_pairs={{1,0},{3,2},{5,4},{7,6},{8,9},{11,10},{12,13},{15,14},{16,17},{19,... | collective-permute-start | bytes 1572872 | tf_op jit(solution)/shard_map/ppermute | solution.py:267
  21.7 1.4 %copy-start.1 = (bf16[512,1536]{1,0:T(8,128)(2,1)S(1)}, bf16[512,1536]{1,0:T(8,128)(2,1)}, u32[]{:S(2)}) copy-start(bf16[512,1536]{1,0:T(8,128)(2,1)} %get-tuple-element.12) | copy-start | bytes 4718596
  24.4 19.9 %collective-permute-start.7 = (f16[256,512]{1,0:T(8,128)(2,1)S(1)}, f16[256,512]{1,0:T(8,128)(2,1)S(1)}, u32[]{:S(2)}, u32[]{:S(2)}) collective-permute-start(f16[256,512]{1,0:T(8,128)(2,1)S(1)} %get-tuple-element.38), channel_id=1, source_target_pairs={{1,0},{3,2},{5,4},{7,6},{8,9},{11,10},{12,13},{15,14},{16,17},{19,... | collective-permute-start | bytes 786440 | tf_op jit(solution)/shard_map/ppermute | solution.py:267
  37.7 11.6 %collective-permute-start.9 = (f16[512,512]{1,0:T(8,128)(2,1)S(1)}, f16[512,512]{1,0:T(8,128)(2,1)S(1)}, u32[]{:S(2)}, u32[]{:S(2)}) collective-permute-start(f16[512,512]{1,0:T(8,128)(2,1)S(1)} %get-tuple-element.25), channel_id=1, source_target_pairs={{2,0},{6,4},{10,9},{14,13},{17,18},{21,22},{25,27},{29,31}} | collective-permute-start | bytes 1572872 | tf_op jit(solution)/shard_map/ppermute | solution.py:267
  39.7 17.9 %collective-permute-start.11 = (f16[512,256]{1,0:T(8,128)(2,1)S(1)}, f16[512,256]{1,0:T(8,128)(2,1)S(1)}, u32[]{:S(2)}, u32[]{:S(2)}) collective-permute-start(f16[512,256]{1,0:T(8,128)(2,1)S(1)} %get-tuple-element.42), channel_id=1, source_target_pairs={{1,0},{3,2},{5,4},{7,6},{8,9},{10,11},{12,13},{14,15},{17,16},{19,... | collective-permute-start | bytes 786440 | tf_op jit(solution)/shard_map/ppermute | solution.py:267
  41.9 21.5 %collective-permute-start.12 = (bf16[272,1536]{1,0:T(8,128)(2,1)S(1)}, bf16[272,1536]{1,0:T(8,128)(2,1)S(1)}, u32[]{:S(2)}, u32[]{:S(2)}) collective-permute-start(bf16[272,1536]{1,0:T(8,128)(2,1)S(1)} %shard_map.29), channel_id=1, source_target_pairs={{16,0},{17,1},{18,2},{19,3},{20,4},{21,5},{22,6},{23,7},{28,8},{29... | collective-permute-start | bytes 2506760 | tf_op jit(solution)/shard_map/ppermute | solution.py:241
  44.3 18.3 %collective-permute-start.8 = (bf16[272,1536]{1,0:T(8,128)(2,1)S(1)}, bf16[272,1536]{1,0:T(8,128)(2,1)S(1)}, u32[]{:S(2)}, u32[]{:S(2)}) collective-permute-start(bf16[272,1536]{1,0:T(8,128)(2,1)S(1)} %shard_map.24), channel_id=1, source_target_pairs={{8,0},{9,1},{10,2},{11,3},{12,4},{13,5},{14,6},{15,7},{4,8},{5,9},... | collective-permute-start | bytes 2506760 | tf_op jit(solution)/shard_map/ppermute | solution.py:241
  45.0 8.6 %collective-permute-start.10 = (f16[512,256]{1,0:T(8,128)(2,1)S(1)}, f16[512,256]{1,0:T(8,128)(2,1)S(1)}, u32[]{:S(2)}, u32[]{:S(2)}) collective-permute-start(f16[512,256]{1,0:T(8,128)(2,1)S(1)} %get-tuple-element.40), channel_id=1, source_target_pairs={{0,1},{3,2},{4,5},{7,6},{9,8},{11,10},{13,12},{15,14},{16,17},{18,... | collective-permute-start | bytes 786440 | tf_op jit(solution)/shard_map/ppermute | solution.py:267
  49.3 14.0 %collective-permute-start.13 = (f16[256,512]{1,0:T(8,128)(2,1)S(1)}, f16[256,512]{1,0:T(8,128)(2,1)S(1)}, u32[]{:S(2)}, u32[]{:S(2)}) collective-permute-start(f16[256,512]{1,0:T(8,128)(2,1)S(1)} %get-tuple-element.23), channel_id=1, source_target_pairs={{2,0},{6,4},{10,9},{14,13},{17,18},{21,22},{25,27},{29,31}} | collective-permute-start | bytes 786440 | tf_op jit(solution)/shard_map/ppermute | solution.py:267
  53.7 24.2 %collective-permute-start.16 = (f16[512,256]{1,0:T(8,128)(2,1)S(1)}, f16[512,256]{1,0:T(8,128)(2,1)S(1)}, u32[]{:S(2)}, u32[]{:S(2)}) collective-permute-start(f16[512,256]{1,0:T(8,128)(2,1)S(1)} %get-tuple-element.21), channel_id=1, source_target_pairs={{2,1},{6,5},{10,8},{14,12},{17,19},{21,23},{25,26},{29,30}} | collective-permute-start | bytes 786440 | tf_op jit(solution)/shard_map/ppermute | solution.py:267
  57.7 20.4 %collective-permute-start.17 = (f16[512,256]{1,0:T(8,128)(2,1)S(1)}, f16[512,256]{1,0:T(8,128)(2,1)S(1)}, u32[]{:S(2)}, u32[]{:S(2)}) collective-permute-start(f16[512,256]{1,0:T(8,128)(2,1)S(1)} %get-tuple-element.19), channel_id=1, source_target_pairs={{0,2},{2,0},{4,6},{6,4},{9,11},{11,9},{13,15},{15,13},{16,18},{18,... | collective-permute-start | bytes 786440 | tf_op jit(solution)/shard_map/ppermute | solution.py:267
  64.2 8.9 %collective-permute-start.15 = (f16[512,256]{1,0:T(8,128)(2,1)S(1)}, f16[512,256]{1,0:T(8,128)(2,1)S(1)}, u32[]{:S(2)}, u32[]{:S(2)}) collective-permute-start(f16[512,256]{1,0:T(8,128)(2,1)S(1)} %get-tuple-element.44), channel_id=1, source_target_pairs={{0,1},{3,2},{4,5},{7,6},{9,8},{11,10},{13,12},{15,14},{16,17},{18,... | collective-permute-start | bytes 786440 | tf_op jit(solution)/shard_map/ppermute | solution.py:267
  65.5 12.6 %collective-permute-start.18 = (f16[512,256]{1,0:T(8,128)(2,1)S(1)}, f16[512,256]{1,0:T(8,128)(2,1)S(1)}, u32[]{:S(2)}, u32[]{:S(2)}) collective-permute-start(f16[512,256]{1,0:T(8,128)(2,1)S(1)} %get-tuple-element.46), channel_id=1, source_target_pairs={{1,0},{3,2},{5,4},{7,6},{8,9},{10,11},{12,13},{14,15},{17,16},{19,... | collective-permute-start | bytes 786440 | tf_op jit(solution)/shard_map/ppermute | solution.py:267
  70.5 13.6 %collective-permute-start.19 = (f16[512,512]{1,0:T(8,128)(2,1)S(1)}, f16[512,512]{1,0:T(8,128)(2,1)S(1)}, u32[]{:S(2)}, u32[]{:S(2)}) collective-permute-start(f16[512,512]{1,0:T(8,128)(2,1)S(1)} %get-tuple-element.48), channel_id=1, source_target_pairs={{0,1},{3,2},{4,5},{7,6},{8,9},{9,8},{10,11},{11,10},{12,13},{13,12... | collective-permute-start | bytes 1572872 | tf_op jit(solution)/shard_map/ppermute | solution.py:267
  73.1 29.2 %collective-permute-start.14 = (f32[264,512]{1,0:T(8,128)S(1)}, f32[264,512]{1,0:T(8,128)S(1)}, u32[]{:S(2)}, u32[]{:S(2)}) collective-permute-start(f32[264,512]{1,0:T(8,128)S(1)} %pad_maximum_fusion.5), channel_id=1, source_target_pairs={{0,4},{4,0},{8,12},{12,8},{16,20},{20,16},{24,28},{28,24},{1,5},{5... | collective-permute-start | bytes 1622024 | tf_op jit(solution)/shard_map/ppermute | solution.py:50
  78.2 15.8 %collective-permute-start.20 = (f16[512,256]{1,0:T(8,128)(2,1)S(1)}, f16[512,256]{1,0:T(8,128)(2,1)S(1)}, u32[]{:S(2)}, u32[]{:S(2)}) collective-permute-start(f16[512,256]{1,0:T(8,128)(2,1)S(1)} %get-tuple-element.17), channel_id=1, source_target_pairs={{2,1},{6,5},{10,8},{14,12},{17,19},{21,23},{25,26},{29,30}} | collective-permute-start | bytes 786440 | tf_op jit(solution)/shard_map/ppermute | solution.py:267
  83.5 15.7 %collective-permute-start.21 = (f16[512,256]{1,0:T(8,128)(2,1)S(1)}, f16[512,256]{1,0:T(8,128)(2,1)S(1)}, u32[]{:S(2)}, u32[]{:S(2)}) collective-permute-start(f16[512,256]{1,0:T(8,128)(2,1)S(1)} %get-tuple-element.15), channel_id=1, source_target_pairs={{0,2},{2,0},{4,6},{6,4},{9,11},{11,9},{13,15},{15,13},{16,18},{18,... | collective-permute-start | bytes 786440 | tf_op jit(solution)/shard_map/ppermute | solution.py:267
  94.1 14.7 %collective-permute-start.24 = (f16[512,512]{1,0:T(8,128)(2,1)S(1)}, f16[512,512]{1,0:T(8,128)(2,1)S(1)}, u32[]{:S(2)}, u32[]{:S(2)}) collective-permute-start(f16[512,512]{1,0:T(8,128)(2,1)S(1)} %get-tuple-element.13), channel_id=1, source_target_pairs={{1,2},{2,1},{5,6},{6,5},{9,11},{10,8},{13,15},{14,12},{17,19},{18,... | collective-permute-start | bytes 1572872 | tf_op jit(solution)/shard_map/ppermute | solution.py:267
  100.8 10.9 %collective-permute-start.22 = (f16[528,512]{1,0:T(8,128)(2,1)S(1)}, f16[528,512]{1,0:T(8,128)(2,1)S(1)}, u32[]{:S(2)}, u32[]{:S(2)}) collective-permute-start(f16[528,512]{1,0:T(8,128)(2,1)S(1)} %get-tuple-element.34), channel_id=1, source_target_pairs={{12,1},{8,5},{1,8},{5,12},{30,19},{26,23},{19,26},{23,30}} | collective-permute-start | bytes 1622024 | tf_op jit(solution)/shard_map/ppermute | solution.py:241
  101.5 10.4 %collective-permute-start.23 = (f16[528,512]{1,0:T(8,128)(2,1)S(1)}, f16[528,512]{1,0:T(8,128)(2,1)S(1)}, u32[]{:S(2)}, u32[]{:S(2)}) collective-permute-start(f16[528,512]{1,0:T(8,128)(2,1)S(1)} %get-tuple-element.35), channel_id=1, source_target_pairs={{22,2},{18,6},{27,11},{31,15},{0,16},{4,20},{13,25},{9,29}} | collective-permute-start | bytes 1622024 | tf_op jit(solution)/shard_map/ppermute | solution.py:241
  109.2 15.0 %collective-permute-start.25 = (f16[528,512]{1,0:T(8,128)(2,1)S(1)}, f16[528,512]{1,0:T(8,128)(2,1)S(1)}, u32[]{:S(2)}, u32[]{:S(2)}) collective-permute-start(f16[528,512]{1,0:T(8,128)(2,1)S(1)} %get-tuple-element.33), channel_id=1, source_target_pairs={{15,3},{11,7},{2,10},{6,14},{29,17},{25,21},{16,24},{20,28}} | collective-permute-start | bytes 1622024 | tf_op jit(solution)/shard_map/ppermute | solution.py:241
  110.5 14.8 %collective-permute-start.26 = (f16[528,512]{1,0:T(8,128)(2,1)S(1)}, f16[528,512]{1,0:T(8,128)(2,1)S(1)}, u32[]{:S(2)}, u32[]{:S(2)}) collective-permute-start(f16[528,512]{1,0:T(8,128)(2,1)S(1)} %get-tuple-element.32), channel_id=1, source_target_pairs={{23,3},{19,7},{26,10},{30,14},{1,17},{5,21},{12,24},{8,28}} | collective-permute-start | bytes 1622024 | tf_op jit(solution)/shard_map/ppermute | solution.py:241
